TPU v7x, 32 devices: a whole 2x2x4 slice. The times are simulated.
32 devices in a mesh: dp: 8 (over z, y), mp: 4 (over x, core).
Axes of the slice: x: 2, y: 2, z: 4, core: 2. Of those that a mesh axis runs over, the one named last changes fastest.
Arguments:
- text_tokens: bfloat16 [2048, 768], P('dp'), may hold values from -6 to 6
- segment_ids: int32 [2048], P('dp'), may hold values from 0 to 191, as said below
- labels: int32 [192], P('dp'), may hold values from 0 to 191, each once
- image_tokens: bfloat16 [9600, 768], P('dp'), may hold values from -6 to 6
- image_gain_one: float32 [768], replicated, may hold values from 0.5 to 1.5
- image_bias_one: float32 [768], replicated, may hold values from -4 to 4
- image_qkv: bfloat16 [768, 3, 768], P(None, None, 'mp'), may hold values from -0.21875 to 0.21875
- image_out: bfloat16 [768, 768], P('mp'), may hold values from -0.875 to 0.875
- image_gain_two: float32 [768], replicated, may hold values from 0.5 to 1.5
- image_bias_two: float32 [768], replicated, may hold values from -4 to 4
- image_up: bfloat16 [768, 3072], P(None, 'mp'), may hold values from -0.21875 to 0.21875
- image_up_bias: float32 [3072], P('mp'), may hold values from -6 to 6
- image_down: bfloat16 [3072, 768], P('mp'), may hold values from -0.109375 to 0.109375
- text_gain_one: float32 [768], replicated, may hold values from 0.5 to 1.5
- text_bias_one: float32 [768], replicated, may hold values from -4 to 4
- text_qkv: bfloat16 [768, 3, 768], P(None, None, 'mp'), may hold values from -0.21875 to 0.21875
- text_out: bfloat16 [768, 768], P('mp'), may hold values from -0.625 to 0.625
- text_gain_two: float32 [768], replicated, may hold values from 0.5 to 1.5
- text_bias_two: float32 [768], replicated, may hold values from -4 to 4
- text_up: bfloat16 [768, 3072], P(None, 'mp'), may hold values from -0.21875 to 0.21875
- text_up_bias: float32 [3072], P('mp'), may hold values from -6 to 6
- text_down: bfloat16 [3072, 768], P('mp'), may hold values from -0.109375 to 0.109375
Outputs:
- pair_loss: float32 [192], P('dp')
- text_grad: float32 [2048, 768], P('dp')
- grad_gain_one: float32 [768], replicated
- grad_bias_one: float32 [768], replicated
- grad_qkv: float32 [768, 3, 768], P(None, None, 'mp')
- grad_out: float32 [768, 768], P('mp')
- grad_gain_two: float32 [768], replicated
- grad_bias_two: float32 [768], replicated
- grad_up: float32 [768, 3072], P(None, 'mp')
- grad_up_bias: float32 [3072], P('mp')
- grad_down: float32 [3072, 768], P('mp')
Inputs may be any that keep to these rules, and one draw needn't show every extreme that they name: `segment_ids`: each packed row of 64 tokens holds exactly 6 whole captions one after another; captions are numbered row after row, so the rows of one index of dp hold captions of that index only. `labels`: each image number appears once.
All inputs are finite; a program needn't handle non-finite values.
Results may differ from a plain program's by a relative error of at most 0.033.
Values may be sent and summed in bfloat16 or wider, within the bound.
A program may use at most 128 MiB of HBM per device.

v0:
```python
import jax
import jax.numpy as jnp
from jax import lax
from jax.sharding import PartitionSpec as P

HEAD = 64
IMG_LEN = 50
ROW_LEN = 64


def from_behind(value, axis, by):
    peers = lax.axis_size(axis)
    return lax.ppermute(value, axis, [(i, (i + by) % peers) for i in range(peers)])


def layer_norm(values, gain, shift_bias):
    center = values - jnp.mean(values, axis=-1, keepdims=True)
    factor = lax.rsqrt(jnp.mean(center * center, axis=-1, keepdims=True) + 1e-05)
    return center * factor * gain + shift_bias


def unit(rows):
    return rows * lax.rsqrt(jnp.sum(rows * rows, axis=-1, keepdims=True) + 1e-06)


def exact_gelu(values):
    return jax.nn.gelu(values, approximate=False)


def masked_scores(queries, keys, allowed):
    scale = queries.shape[-1] ** (-0.5)
    scores = (
        jnp.einsum("sqhe,skhe->shqk", queries, keys, preferred_element_type=jnp.float32) * scale
    )
    if allowed is not None:
        scores = jnp.where(allowed[:, None], scores, -1e30)
    return scores


def block_forward(stream, params, seq_len, allowed):
    gain_one, bias_one, w_qkv, w_out, gain_two, bias_two, w_up, b_up, w_down = params
    count = stream.shape[0]
    width = w_qkv.shape[2]
    normed = layer_norm(stream, gain_one, bias_one).astype(jnp.bfloat16)
    mixed = jnp.einsum("td,dke->tke", normed, w_qkv, preferred_element_type=jnp.float32).astype(
        jnp.bfloat16
    )
    mixed = mixed.reshape(count // seq_len, seq_len, 3, width // HEAD, HEAD)
    scores = masked_scores(mixed[:, :, 0], mixed[:, :, 1], allowed)
    top = jnp.max(scores, axis=-1, keepdims=True)
    expo = jnp.exp(scores - top)
    denom = jnp.sum(expo, axis=-1, keepdims=True)
    probs = expo / denom
    lse = top + jnp.log(denom)
    context = (
        jnp.einsum(
            "shqk,skhe->sqhe",
            probs.astype(jnp.bfloat16),
            mixed[:, :, 2],
            preferred_element_type=jnp.float32,
        )
        .astype(jnp.bfloat16)
        .reshape(count, width)
    )
    attended = jnp.dot(context, w_out, preferred_element_type=jnp.float32)
    attended = lax.psum(attended.astype(jnp.bfloat16), "mp").astype(jnp.float32)
    middle = stream + attended
    normed_two = layer_norm(middle, gain_two, bias_two).astype(jnp.bfloat16)
    hidden = jnp.dot(normed_two, w_up, preferred_element_type=jnp.float32) + b_up
    active = exact_gelu(hidden).astype(jnp.bfloat16)
    branch = jnp.dot(active, w_down, preferred_element_type=jnp.float32)
    branch = lax.psum(branch.astype(jnp.bfloat16), "mp").astype(jnp.float32)
    return (middle + branch, (mixed, lse, context, middle, normed_two, hidden, active))


def block_backward(stream, params, saved, grad_final, allowed):
    gain_one, bias_one, w_qkv, w_out, gain_two, bias_two, w_up, b_up, w_down = params
    mixed, lse, context, middle, normed_two, hidden, active = saved
    count = stream.shape[0]
    width = w_qkv.shape[2]
    grad_low = grad_final.astype(jnp.bfloat16)
    down_grad = jnp.einsum("tf,td->fd", active, grad_low, preferred_element_type=jnp.float32)
    grad_active = jnp.einsum("td,fd->tf", grad_low, w_down, preferred_element_type=jnp.float32)
    ignored, gelu_back = jax.vjp(exact_gelu, hidden)
    grad_hidden = gelu_back(grad_active)[0].astype(jnp.bfloat16)
    up_bias_grad = jnp.sum(grad_hidden.astype(jnp.float32), axis=0)
    up_grad = jnp.einsum("td,tf->df", normed_two, grad_hidden, preferred_element_type=jnp.float32)
    grad_normed_two = lax.psum(
        jnp.einsum("tf,df->td", grad_hidden, w_up, preferred_element_type=jnp.float32).astype(
            jnp.bfloat16
        ),
        "mp",
    ).astype(jnp.float32)
    ignored, norm_back_two = jax.vjp(layer_norm, middle, gain_two, bias_two)
    grad_middle, gain_two_grad, bias_two_grad = norm_back_two(grad_normed_two)
    grad_middle = grad_middle + grad_final
    grad_attended = grad_middle.astype(jnp.bfloat16)
    out_grad = jnp.einsum("tc,td->cd", context, grad_attended, preferred_element_type=jnp.float32)
    grad_context = jnp.einsum("td,cd->tc", grad_attended, w_out, preferred_element_type=jnp.float32)
    grad_context = grad_context.astype(jnp.bfloat16).reshape(
        mixed.shape[0], mixed.shape[1], width // HEAD, HEAD
    )
    queries = mixed[:, :, 0]
    keys = mixed[:, :, 1]
    values = mixed[:, :, 2]
    scale = queries.shape[-1] ** (-0.5)
    probs = jnp.exp(masked_scores(queries, keys, allowed) - lse)
    grad_probs = jnp.einsum(
        "sqhe,skhe->shqk", grad_context, values, preferred_element_type=jnp.float32
    )
    grad_values = jnp.einsum(
        "shqk,sqhe->skhe",
        probs.astype(jnp.bfloat16),
        grad_context,
        preferred_element_type=jnp.float32,
    ).astype(jnp.bfloat16)
    grad_scores = probs * (grad_probs - jnp.sum(grad_probs * probs, axis=-1, keepdims=True))
    grad_scores = grad_scores.astype(jnp.bfloat16)
    grad_queries = (
        jnp.einsum("shqk,skhe->sqhe", grad_scores, keys, preferred_element_type=jnp.float32) * scale
    ).astype(jnp.bfloat16)
    grad_keys = (
        jnp.einsum("shqk,sqhe->skhe", grad_scores, queries, preferred_element_type=jnp.float32)
        * scale
    ).astype(jnp.bfloat16)
    grad_mixed = jnp.stack([grad_queries, grad_keys, grad_values], axis=2).reshape(count, 3, width)
    normed, norm_back_one = jax.vjp(layer_norm, stream, gain_one, bias_one)
    qkv_grad = jnp.einsum(
        "td,tke->dke", normed.astype(jnp.bfloat16), grad_mixed, preferred_element_type=jnp.float32
    )
    grad_normed = lax.psum(
        jnp.einsum("tke,dke->td", grad_mixed, w_qkv, preferred_element_type=jnp.float32).astype(
            jnp.bfloat16
        ),
        "mp",
    ).astype(jnp.float32)
    grad_stream, gain_one_grad, bias_one_grad = norm_back_one(grad_normed)
    grads = (
        gain_one_grad,
        bias_one_grad,
        qkv_grad,
        out_grad,
        gain_two_grad,
        bias_two_grad,
        up_grad,
        up_bias_grad,
        down_grad,
    )
    return (grad_stream + grad_middle, grads)


def pass_on(image_block, col_top, col_sum):
    return from_behind((image_block, col_top, col_sum), "dp", 1)


def per_device(
    text_tokens,
    segment_ids,
    labels,
    image_tokens,
    image_gain_one,
    image_bias_one,
    image_qkv,
    image_out,
    image_gain_two,
    image_bias_two,
    image_up,
    image_up_bias,
    image_down,
    text_gain_one,
    text_bias_one,
    text_qkv,
    text_out,
    text_gain_two,
    text_bias_two,
    text_up,
    text_up_bias,
    text_down,
):
    f32 = jnp.float32
    bf16 = jnp.bfloat16
    text_params = (
        text_gain_one,
        text_bias_one,
        text_qkv,
        text_out,
        text_gain_two,
        text_bias_two,
        text_up,
        text_up_bias,
        text_down,
    )
    devices = lax.axis_size("dp")
    rank = lax.axis_index("dp")
    pairs_dev = labels.shape[0]
    image_params = (
        image_gain_one,
        image_bias_one,
        image_qkv,
        image_out,
        image_gain_two,
        image_bias_two,
        image_up,
        image_up_bias,
        image_down,
    )
    image_final, ignored = block_forward(image_tokens.astype(f32), image_params, IMG_LEN, None)
    firsts = image_final.reshape(pairs_dev, IMG_LEN, image_final.shape[1])[:, 0]
    image_low = unit(firsts).astype(bf16)
    stream = text_tokens.astype(f32)
    tokens_dev = stream.shape[0]
    grouped = segment_ids.reshape(tokens_dev // ROW_LEN, ROW_LEN)
    places = jnp.arange(ROW_LEN)
    allowed = (grouped[:, :, None] == grouped[:, None, :]) & (
        places[None, None, :] <= places[None, :, None]
    )
    final, saved = block_forward(stream, text_params, ROW_LEN, allowed)
    following = jnp.concatenate([segment_ids[1:], jnp.full((1,), -1, jnp.int32)])
    ends = segment_ids != following
    local_ids = segment_ids - rank * pairs_dev
    selector = ((local_ids[None, :] == jnp.arange(pairs_dev)[:, None]) & ends[None, :]).astype(f32)
    pooled = jnp.dot(selector, final, precision=lax.Precision.HIGHEST)
    text_unit, unit_back = jax.vjp(unit, pooled)
    text_low = text_unit.astype(bf16)
    column_base = jnp.arange(pairs_dev)

    def block_logits(image_block):
        return 64.0 * jnp.einsum(
            "pd,jd->pj", text_low, image_block.astype(bf16), preferred_element_type=f32
        )

    def visit(state, step):
        image_block, col_top, col_sum, row_top, row_sum, positive = state
        owner = (rank - step) % devices
        logits = block_logits(image_block)
        new_col = jnp.maximum(col_top, jnp.max(logits, axis=0))
        col_sum = col_sum * jnp.exp(col_top - new_col) + jnp.sum(
            jnp.exp(logits - new_col[None, :]), axis=0
        )
        new_row = jnp.maximum(row_top, jnp.max(logits, axis=1))
        row_sum = row_sum * jnp.exp(row_top - new_row) + jnp.sum(
            jnp.exp(logits - new_row[:, None]), axis=1
        )
        targets = owner * pairs_dev + column_base
        positive = positive + jnp.sum(
            jnp.where(labels[:, None] == targets[None, :], logits, 0.0), axis=1
        )
        return (image_block, new_col, col_sum, new_row, row_sum, positive)

    def cycle_step(step, state):
        moved = pass_on(state[0], state[1], state[2])
        return visit((moved[0], moved[1], moved[2]) + tuple(state[3:]), step)

    floor = jnp.full((pairs_dev,), -1e30, f32)
    empty = jnp.zeros((pairs_dev,), f32)
    state = visit((image_low.astype(f32), floor, empty, floor, empty, empty), 0)
    state = lax.fori_loop(1, devices, cycle_step, state)
    home = pass_on(state[0], state[1], state[2])
    col_lse = home[1] + jnp.log(home[2])
    row_lse = state[3] + jnp.log(state[4])
    pair_loss = 0.5 * (row_lse + col_lse) - state[5]

    def gradient_visit(image_block, col_block, step):
        owner = (rank - step) % devices
        logits = block_logits(image_block)
        targets = owner * pairs_dev + column_base
        onehot = (labels[:, None] == targets[None, :]).astype(f32)
        grad_logits = (
            0.5 * (jnp.exp(logits - row_lse[:, None]) + jnp.exp(logits - col_block[None, :]))
            - onehot
        )
        return 64.0 * jnp.einsum(
            "pj,jd->pd",
            grad_logits.astype(bf16),
            image_block.astype(bf16),
            preferred_element_type=f32,
        )

    def back_step(step, carry):
        grad_embed, image_block, col_block = carry
        image_block, col_block = from_behind((image_block, col_block), "dp", 1)
        return (grad_embed + gradient_visit(image_block, col_block, step), image_block, col_block)

    first = gradient_visit(image_low.astype(f32), col_lse, 0)
    grad_embed = lax.fori_loop(1, devices, back_step, (first, image_low.astype(f32), col_lse))[0]
    grad_pooled = unit_back(grad_embed)[0]
    grad_final = jnp.einsum("pt,pd->td", selector, grad_pooled, precision=lax.Precision.HIGHEST)
    grad_stream, grads = block_backward(stream, text_params, saved, grad_final, allowed)
    grads = lax.psum(
        (grads[0], grads[1], grads[2], grads[3], grads[4], grads[5], grads[6], grads[7], grads[8]),
        "dp",
    )
    return (
        pair_loss,
        grad_stream,
        grads[0],
        grads[1],
        grads[2],
        grads[3],
        grads[4],
        grads[5],
        grads[6],
        grads[7],
        grads[8],
    )


def solution(mesh):
    placed = (
        P("dp", None),
        P("dp"),
        P("dp"),
        P("dp", None),
        P(),
        P(),
        P(None, None, "mp"),
        P("mp", None),
        P(),
        P(),
        P(None, "mp"),
        P("mp"),
        P("mp", None),
        P(),
        P(),
        P(None, None, "mp"),
        P("mp", None),
        P(),
        P(),
        P(None, "mp"),
        P("mp"),
        P("mp", None),
    )
    return jax.shard_map(
        per_device,
        mesh=mesh,
        in_specs=placed,
        out_specs=(
            P("dp"),
            P("dp", None),
            P(),
            P(),
            P(None, None, "mp"),
            P("mp", None),
            P(),
            P(),
            P(None, "mp"),
            P("mp"),
            P("mp", None),
        ),
        check_vma=False,
    )
```

profile of v0, /device:TPU:0, one launch (start us, length us, event | category | flops | bytes accessed | tf_op | source)
XLA Modules:
  0.0 676.8 jit_solution(960923090906602921)
XLA Ops:
  32.6 6.2 reshape.225
  38.8 4.0 fusion.192
  42.8 3.5 copy.86
  46.3 3.5 copy.87
  53.3 4.6 fusion.194
  57.9 3.6 fusion.50
  72.3 56.7 %all-reduce.18.cloned.1.call-done = (bf16[1200,768]{1,0:T(8,128)(2,1)}, bf16[256,768]{1,0:T(8,128)(2,1)}) async-done(((bf16[1200,768]{1,0:T(8,128)(2,1)}, bf16[256,768]{1,0:T(8,128)(2,1)}), (bf16[1200,768]{1,0:T(8,128)(2,1)}, bf16[256,768]{1,0:T(8,128)(2,1)})) %all-reduce.18.cloned.1.call-update) | async-done | bytes 2236432 | tf_op jit(solution)/shard_map/psum | solution.py:66
  141.1 14.2 %convolution_convert_fusion.1 = bf16[1200,768]{1,0:T(8,128)(2,1)} fusion(bf16[768,768]{1,0:T(8,128)(2,1)S(1)} %copy-done, bf16[768,768]{1,0:T(8,128)(2,1)} %param.36, bf16[1200,768]{1,0:T(8,128)(2,1)} %get-tuple-element.612, bf16[1200,768]{1,0:T(8,128)(2,1)S(1)} %copy-done.3, f32[768]{0:T(1024)} %param.37, f32[768]{0:T(1024)} %param.35, f32[768]{0:T(1024)} %param.34, ...), kind=kOutput, calls=%fused_computation.60 | convolution fusion | flops 2900275200 | bytes 7907712 | tf_op jit(solution)/shard_map/dot_general | solution.py:71
  157.8 51.7 %all-reduce.16.cloned.1.call-done = (bf16[1200,768]{1,0:T(8,128)(2,1)}, bf16[256,768]{1,0:T(8,128)(2,1)}) async-done(((bf16[1200,768]{1,0:T(8,128)(2,1)}, bf16[256,768]{1,0:T(8,128)(2,1)}), (bf16[1200,768]{1,0:T(8,128)(2,1)}, bf16[256,768]{1,0:T(8,128)(2,1)})) %all-reduce.16.cloned.1.call-update) | async-done | bytes 2236432 | tf_op jit(solution)/shard_map/psum | solution.py:72
  209.6 4.6 convert_add_fusion.1
  214.8 4.9 reshape.227
  221.6 61.7 %while.46 = (s32[]{:T(128)}, bf16[24,768]{1,0:T(8,128)(2,1)S(1)}, f32[24]{0:T(128)S(1)}, f32[24]{0:T(128)S(1)}, f32[24]{0:T(128)S(1)}, /*index=5*/f32[24]{0:T(12...) while((s32[]{:T(128)}, bf16[24,768]{1,0:T(8,128)(2,1)S(1)}, ...), condition=%wide.region_29.30_spmd.clone, body=%wide.region_23.29_spmd.clone.sunk | while | flops 890631 | bytes 303662 | solution.py:257
  226.1 5.2 collective-permute-done
  233.6 6.1 collective-permute-done
  241.5 6.6 collective-permute-done
  250.4 5.1 collective-permute-done
  259.5 6.6 collective-permute-done
  267.7 6.6 collective-permute-done
  276.1 6.6 collective-permute-done
  283.8 5.8 collective-permute-done.5
  290.4 49.6 %while.47 = (s32[]{:T(128)}, f32[24,768]{1,0:T(8,128)S(1)}, bf16[24,768]{1,0:T(8,128)(2,1)S(1)}, f32[24]{0:T(128)S(1)}, bf16[24,768]{1,0:T(8,128)(2,1)S(1)}, /*i...) while((s32[]{:T(128)}, f32[24,768]{1,0:T(8,128)S(1)}, ...), condition=%wide.region_31.32_spmd.clone, body=%wide.region_30.31_spmd.clone.sunk | while | flops 1811559 | bytes 443766 | solution.py:285
  290.6 6.1 collective-permute-done.4
  298.3 5.5 collective-permute-done.4
  304.8 6.1 collective-permute-done.4
  311.9 6.1 collective-permute-done.4
  319.0 6.1 collective-permute-done.4
  326.1 6.1 collective-permute-done.4
  333.2 6.1 collective-permute-done.4
  349.1 28.5 %all-reduce.10.cloned.1.call-done = bf16[256,768]{1,0:T(8,128)(2,1)} async-done(((bf16[256,768]{1,0:T(8,128)(2,1)}), bf16[256,768]{1,0:T(8,128)(2,1)}) %all-reduce.10.cloned.1.call-update) | async-done | bytes 393232 | tf_op jit(solution)/shard_map/psum | solution.py:88
  392.1 29.8 %all-reduce.12.cloned.1.call-done = bf16[256,768]{1,0:T(8,128)(2,1)} async-done(((bf16[256,768]{1,0:T(8,128)(2,1)}), bf16[256,768]{1,0:T(8,128)(2,1)}) %all-reduce.12.cloned.1.call-update) | async-done | bytes 393232 | tf_op jit(solution)/shard_map/psum | solution.py:131
  424.8 39.5 %all-reduce = (f32[768]{0:T(1024)}, f32[768]{0:T(1024)}, f32[768]{0:T(1024)}, f32[768]{0:T(1024)}, f32[768]{0:T(1024)}) all-reduce(f32[768]{0:T(1024)S(1)} %get-tuple-element.554, f32[768]{0:T(1024)S(1)} %get-tuple-element.558, f32[768]{0:T(1024)S(1)} %copy-done.35, f32[768]{0:T(1024)S(1)} %copy-done.34, ...), channel_id=1, replica_groups=mesh['dp'=8,'mp'=4] {'dp'}, use_global_device_ids=true, to_apply=%region_41.42 | all-reduce | flops 3840 | bytes 30720 | tf_op jit(solution)/shard_map/psum | solution.py:289
  466.6 197.1 %all-reduce.14.cloned.1.call-done = (f32[768,3,192]{0,2,1:T(8,128)}, f32[192,768]{1,0:T(8,128)}, f32[768,768]{1,0:T(8,128)}, f32[768,768]{1,0:T(8,128)}) async-done(((f32[768,3,192]{0,2,1:T(8,128)}, f32[192,768]{1,0:T(8,128)}, f32[768,768]{1,0:T(8,128)}, f32[768,768]{1,0:T(8,128)}), (f32[768,3,192]{0,2,1:T(8,128)}, f32[192,768]{1,0:T(8,128)}, f32[768,768]{1,0:T(8,128)}, ...) | async-done | bytes 7077904 | tf_op jit(solution)/shard_map/psum | solution.py:289
  (360 shorter events, 118.2 us)
Async XLA Ops:
  7.2 121.7 %all-reduce.18.cloned.1.call-start = ((), (), s32[]{:S(2)}) async-start(), calls=%async_computation.4 | async-start | bytes 4472832 | tf_op jit(solution)/shard_map/psum | solution.py:66
  72.1 137.5 %all-reduce.16.cloned.1.call-start = ((), (), s32[]{:S(2)}) async-start(), calls=%async_computation.3 | async-start | bytes 4472832 | tf_op jit(solution)/shard_map/psum | solution.py:72
  155.3 222.3 %all-reduce.10.cloned.1.call-start = ((), (), s32[]{:S(2)}) async-start(), calls=%async_computation | async-start | bytes 786432 | tf_op jit(solution)/shard_map/psum | solution.py:88
  221.6 10.2 %collective-permute-start.2 = (f32[24]{0:T(128)S(1)}, f32[24]{0:T(128)S(1)}, u32[]{:S(2)}, u32[]{:S(2)}) collective-permute-start(f32[24]{0:T(128)S(1)} %get-tuple-element.780), channel_id=1, source_target_pairs={{0,4},{4,8},{8,12},{12,16},{16,20},{20,24},{24,28},{28,0},{1,5},{5... | collective-permute-start | bytes 296 | tf_op jit(solution)/shard_map/while/body/eval_jaxpr/ppermute | solution.py:13
  223.1 8.4 %collective-permute-start.1 = (f32[24]{0:T(128)S(1)}, f32[24]{0:T(128)S(1)}, u32[]{:S(2)}, u32[]{:S(2)}) collective-permute-start(f32[24]{0:T(128)S(1)} %get-tuple-element.779), channel_id=1, source_target_pairs={{0,4},{4,8},{8,12},{12,16},{16,20},{20,24},{24,28},{28,0},{1,5},{5... | collective-permute-start | bytes 296 | tf_op jit(solution)/shard_map/while/body/eval_jaxpr/ppermute | solution.py:13
  224.6 6.7 collective-permute-start
  231.8 8.4 %collective-permute-start.2 = (f32[24]{0:T(128)S(1)}, f32[24]{0:T(128)S(1)}, u32[]{:S(2)}, u32[]{:S(2)}) collective-permute-start(f32[24]{0:T(128)S(1)} %get-tuple-element.780), channel_id=1, source_target_pairs={{0,4},{4,8},{8,12},{12,16},{16,20},{20,24},{24,28},{28,0},{1,5},{5... | collective-permute-start | bytes 296 | tf_op jit(solution)/shard_map/while/body/eval_jaxpr/ppermute | solution.py:13
  231.9 8.0 %collective-permute-start.1 = (f32[24]{0:T(128)S(1)}, f32[24]{0:T(128)S(1)}, u32[]{:S(2)}, u32[]{:S(2)}) collective-permute-start(f32[24]{0:T(128)S(1)} %get-tuple-element.779), channel_id=1, source_target_pairs={{0,4},{4,8},{8,12},{12,16},{16,20},{20,24},{24,28},{28,0},{1,5},{5... | collective-permute-start | bytes 296 | tf_op jit(solution)/shard_map/while/body/eval_jaxpr/ppermute | solution.py:13
  233.0 6.7 collective-permute-start
  240.2 8.4 %collective-permute-start.2 = (f32[24]{0:T(128)S(1)}, f32[24]{0:T(128)S(1)}, u32[]{:S(2)}, u32[]{:S(2)}) collective-permute-start(f32[24]{0:T(128)S(1)} %get-tuple-element.780), channel_id=1, source_target_pairs={{0,4},{4,8},{8,12},{12,16},{16,20},{20,24},{24,28},{28,0},{1,5},{5... | collective-permute-start | bytes 296 | tf_op jit(solution)/shard_map/while/body/eval_jaxpr/ppermute | solution.py:13
  240.3 8.1 %collective-permute-start.1 = (f32[24]{0:T(128)S(1)}, f32[24]{0:T(128)S(1)}, u32[]{:S(2)}, u32[]{:S(2)}) collective-permute-start(f32[24]{0:T(128)S(1)} %get-tuple-element.779), channel_id=1, source_target_pairs={{0,4},{4,8},{8,12},{12,16},{16,20},{20,24},{24,28},{28,0},{1,5},{5... | collective-permute-start | bytes 296 | tf_op jit(solution)/shard_map/while/body/eval_jaxpr/ppermute | solution.py:13
  241.4 6.7 collective-permute-start
  248.6 7.4 %collective-permute-start.2 = (f32[24]{0:T(128)S(1)}, f32[24]{0:T(128)S(1)}, u32[]{:S(2)}, u32[]{:S(2)}) collective-permute-start(f32[24]{0:T(128)S(1)} %get-tuple-element.780), channel_id=1, source_target_pairs={{0,4},{4,8},{8,12},{12,16},{16,20},{20,24},{24,28},{28,0},{1,5},{5... | collective-permute-start | bytes 296 | tf_op jit(solution)/shard_map/while/body/eval_jaxpr/ppermute | solution.py:13
  248.7 7.1 %collective-permute-start.1 = (f32[24]{0:T(128)S(1)}, f32[24]{0:T(128)S(1)}, u32[]{:S(2)}, u32[]{:S(2)}) collective-permute-start(f32[24]{0:T(128)S(1)} %get-tuple-element.779), channel_id=1, source_target_pairs={{0,4},{4,8},{8,12},{12,16},{16,20},{20,24},{24,28},{28,0},{1,5},{5... | collective-permute-start | bytes 296 | tf_op jit(solution)/shard_map/while/body/eval_jaxpr/ppermute | solution.py:13
  248.8 6.7 collective-permute-start
  256.0 10.5 %collective-permute-start.2 = (f32[24]{0:T(128)S(1)}, f32[24]{0:T(128)S(1)}, u32[]{:S(2)}, u32[]{:S(2)}) collective-permute-start(f32[24]{0:T(128)S(1)} %get-tuple-element.780), channel_id=1, source_target_pairs={{0,4},{4,8},{8,12},{12,16},{16,20},{20,24},{24,28},{28,0},{1,5},{5... | collective-permute-start | bytes 296 | tf_op jit(solution)/shard_map/while/body/eval_jaxpr/ppermute | solution.py:13
  256.1 10.2 %collective-permute-start.1 = (f32[24]{0:T(128)S(1)}, f32[24]{0:T(128)S(1)}, u32[]{:S(2)}, u32[]{:S(2)}) collective-permute-start(f32[24]{0:T(128)S(1)} %get-tuple-element.779), channel_id=1, source_target_pairs={{0,4},{4,8},{8,12},{12,16},{16,20},{20,24},{24,28},{28,0},{1,5},{5... | collective-permute-start | bytes 296 | tf_op jit(solution)/shard_map/while/body/eval_jaxpr/ppermute | solution.py:13
  259.4 6.7 collective-permute-start
  266.6 8.2 %collective-permute-start.2 = (f32[24]{0:T(128)S(1)}, f32[24]{0:T(128)S(1)}, u32[]{:S(2)}, u32[]{:S(2)}) collective-permute-start(f32[24]{0:T(128)S(1)} %get-tuple-element.780), channel_id=1, source_target_pairs={{0,4},{4,8},{8,12},{12,16},{16,20},{20,24},{24,28},{28,0},{1,5},{5... | collective-permute-start | bytes 296 | tf_op jit(solution)/shard_map/while/body/eval_jaxpr/ppermute | solution.py:13
  266.7 7.8 %collective-permute-start.1 = (f32[24]{0:T(128)S(1)}, f32[24]{0:T(128)S(1)}, u32[]{:S(2)}, u32[]{:S(2)}) collective-permute-start(f32[24]{0:T(128)S(1)} %get-tuple-element.779), channel_id=1, source_target_pairs={{0,4},{4,8},{8,12},{12,16},{16,20},{20,24},{24,28},{28,0},{1,5},{5... | collective-permute-start | bytes 296 | tf_op jit(solution)/shard_map/while/body/eval_jaxpr/ppermute | solution.py:13
  274.8 8.4 %collective-permute-start.2 = (f32[24]{0:T(128)S(1)}, f32[24]{0:T(128)S(1)}, u32[]{:S(2)}, u32[]{:S(2)}) collective-permute-start(f32[24]{0:T(128)S(1)} %get-tuple-element.780), channel_id=1, source_target_pairs={{0,4},{4,8},{8,12},{12,16},{16,20},{20,24},{24,28},{28,0},{1,5},{5... | collective-permute-start | bytes 296 | tf_op jit(solution)/shard_map/while/body/eval_jaxpr/ppermute | solution.py:13
  274.9 8.0 %collective-permute-start.1 = (f32[24]{0:T(128)S(1)}, f32[24]{0:T(128)S(1)}, u32[]{:S(2)}, u32[]{:S(2)}) collective-permute-start(f32[24]{0:T(128)S(1)} %get-tuple-element.779), channel_id=1, source_target_pairs={{0,4},{4,8},{8,12},{12,16},{16,20},{20,24},{24,28},{28,0},{1,5},{5... | collective-permute-start | bytes 296 | tf_op jit(solution)/shard_map/while/body/eval_jaxpr/ppermute | solution.py:13
  276.0 6.7 collective-permute-start
  290.5 6.7 collective-permute-start.3
  297.6 6.7 collective-permute-start.3
  304.7 6.7 collective-permute-start.3
  311.8 6.7 collective-permute-start.3
  318.9 6.7 collective-permute-start.3
  326.0 6.7 collective-permute-start.3
  333.1 6.7 collective-permute-start.3
  347.1 74.8 %all-reduce.12.cloned.1.call-start = ((), (), s32[]{:S(2)}) async-start(), calls=%async_computation.1 | async-start | bytes 786432 | tf_op jit(solution)/shard_map/psum | solution.py:131
  389.2 274.4 %all-reduce.14.cloned.1.call-start = ((), (), s32[]{:S(2)}) async-start(), calls=%async_computation.2 | async-start | bytes 14155776 | tf_op jit(solution)/shard_map/psum | solution.py:289
  (57 other events, 1083.2 us)
Sparse Core Ops, SparseCore 0:
  72.2 56.7 all-reduce.17
  155.4 54.0 all-reduce.15
  347.2 30.3 all-reduce.9
  389.3 32.6 all-reduce.11
  427.4 236.2 all-reduce.13
where the time goes:
time: 678 us; the launch traced here: 677 us
  waiting for transfers between devices  458 us (68%)
  matrix products  58.5 us (9%)
  local copies, waits for them, and re-layouts  53.9 us (8%)
  blocking collectives  39.5 us (6%)
  other arithmetic  33.7 us (5%)
  starting transfers between devices  17.6 us (3%)
  between operations  14.4 us (2%)
    psum x1, waiting for transfers between devices, per_device(): lax.psum((grads[0], grads[1], grads[2], grads[3], grads[4], grads[5], gra...  197 us
    ppermute x37, waiting for transfers between devices, from_behind(): lax.ppermute(value, axis, [(i, (i + by) % peers) for i in range(peers)])  94.3 us
    psum x1, waiting for transfers between devices, block_forward(): attended = lax.psum(attended.astype(jnp.bfloat16), 'mp').astype(jnp.float32)  56.7 us
    psum x1, waiting for transfers between devices, block_forward(): branch = lax.psum(branch.astype(jnp.bfloat16), 'mp').astype(jnp.float32)  51.7 us
    psum x1, blocking collectives, per_device(): lax.psum((grads[0], grads[1], grads[2], grads[3], grads[4], grads[5], gra...  39.5 us
    psum x1, waiting for transfers between devices, block_backward(): lax.psum(jnp.einsum('tke,dke->td', grad_mixed, w_qkv, preferred_element_t...  29.8 us
    psum x1, waiting for transfers between devices, block_backward(): lax.psum(jnp.einsum('tf,df->td', grad_hidden, w_up, preferred_element_typ...  28.5 us
    unnamed x106, local copies, waits for them, and re-layouts  23.3 us
  transfers between devices with their start and end apart: 42, of which 28 were waited for; matrix products, arithmetic and copies ran while one was open for 2% of the time, Pallas kernels for 0%

commit v1 on v0

v1 whole, which is shorter than its diff:
```python
import jax
import jax.numpy as jnp
from jax import lax
from jax.sharding import PartitionSpec as P

HEAD = 64
IMG_LEN = 50
F32 = jnp.float32
BF16 = jnp.bfloat16


def dot(a, b):
    return lax.dot_general(a, b, (((1,), (0,)), ((), ())), preferred_element_type=F32)


def dot_nt(a, b):
    return lax.dot_general(a, b, (((1,), (1,)), ((), ())), preferred_element_type=F32)


def dot_tn(a, b):
    return lax.dot_general(a, b, (((0,), (0,)), ((), ())), preferred_element_type=F32)


def normalized(values):
    center = values - jnp.mean(values, axis=-1, keepdims=True)
    factor = lax.rsqrt(jnp.mean(center * center, axis=-1, keepdims=True) + 1e-05)
    return center * factor, factor


def norm_back(grad, hat, factor, gain):
    scaled = grad * gain
    along = jnp.mean(scaled * hat, axis=-1, keepdims=True)
    return factor * (scaled - jnp.mean(scaled, axis=-1, keepdims=True) - hat * along)


def unit(rows):
    return rows * lax.rsqrt(jnp.sum(rows * rows, axis=-1, keepdims=True) + 1e-06)


def gelu_parts(hidden):
    cdf = 0.5 * (1.0 + lax.erf(hidden * 0.7071067811865476))
    slope = cdf + hidden * jnp.exp(-0.5 * hidden * hidden) * 0.3989422804014327
    return hidden * cdf, slope


def head_blocks(rows, width):
    lanes = lax.broadcasted_iota(jnp.int32, (1, width), 1)
    return jnp.concatenate(
        [
            jnp.where((lanes >= h * HEAD) & (lanes < (h + 1) * HEAD), rows, 0.0)
            for h in range(width // HEAD)
        ],
        axis=0,
    )


def head_pick(blocks, width):
    heads = width // HEAD
    count = blocks.shape[0] // heads
    lanes = lax.broadcasted_iota(jnp.int32, (1, width), 1)
    total = jnp.zeros((count, width), F32)
    for h in range(heads):
        own = (lanes >= h * HEAD) & (lanes < (h + 1) * HEAD)
        total = total + jnp.where(own, blocks[h * count : (h + 1) * count], 0.0)
    return total


def attend(normed_rows, normed, allowed, weights):
    width = weights.shape[1]
    heads = width // HEAD
    queries = dot_nt(normed_rows, weights[0]).astype(BF16)
    folded = dot(head_blocks(queries.astype(F32), width).astype(BF16), weights[1]).astype(BF16)
    scores = dot_nt(folded, normed) * HEAD**-0.5
    scores = jnp.where(jnp.concatenate([allowed] * heads, axis=0), scores, -1e30)
    expo = jnp.exp(scores - jnp.max(scores, axis=-1, keepdims=True))
    probs = expo / jnp.sum(expo, axis=-1, keepdims=True)
    mixed = dot(probs.astype(BF16), normed).astype(BF16)
    context = head_pick(dot_nt(mixed, weights[2]), width).astype(BF16)
    return queries, folded, probs, mixed, context


def plain_device(
    text_tokens,
    segment_ids,
    labels,
    image_tokens,
    image_gain_one,
    image_bias_one,
    image_qkv,
    image_out,
    image_gain_two,
    image_bias_two,
    image_up,
    image_up_bias,
    image_down,
    text_gain_one,
    text_bias_one,
    text_qkv,
    text_out,
    text_gain_two,
    text_bias_two,
    text_up,
    text_up_bias,
    text_down,
):
    rank = lax.axis_index("dp")
    pairs = labels.shape[0]
    tokens = segment_ids.shape[0]
    width = text_out.shape[0]
    heads = width // HEAD
    features = text_tokens.shape[1]
    image_weights = jnp.transpose(image_qkv, (1, 2, 0))
    text_weights = jnp.transpose(text_qkv, (1, 2, 0))

    image_x = image_tokens.astype(F32)
    image_n = (normalized(image_x)[0] * image_gain_one + image_bias_one).astype(BF16)
    image_first = image_x.reshape(pairs, IMG_LEN, features)[:, 0]
    first_n = (normalized(image_first)[0] * image_gain_one + image_bias_one).astype(BF16)
    owner = lax.broadcasted_iota(jnp.int32, (pairs, pairs * IMG_LEN), 0)
    place = lax.broadcasted_iota(jnp.int32, (pairs, pairs * IMG_LEN), 1)
    inside = (place >= owner * IMG_LEN) & (place < (owner + 1) * IMG_LEN)
    image_context = attend(first_n, image_n, inside, image_weights)[4]

    text_x = text_tokens.astype(F32)
    hat_one, factor_one = normalized(text_x)
    normed = (hat_one * text_gain_one + text_bias_one).astype(BF16)
    captions = rank * pairs + jnp.arange(pairs)
    mine = segment_ids[None, :] == captions[:, None]
    spot = lax.broadcasted_iota(jnp.int32, (pairs, tokens), 1)
    last = jnp.max(jnp.where(mine, spot, -1), axis=1, keepdims=True)
    pick = (spot == last).astype(BF16)
    normed_last = dot(pick, normed).astype(BF16)
    queries, folded, probs, mixed, context = attend(normed_last, normed, mine, text_weights)

    attended = jnp.concatenate([dot(image_context, image_out), dot(context, text_out)], axis=0)
    attended = lax.psum(attended.astype(BF16), "mp").astype(F32)
    middle = jnp.concatenate([image_first, dot(pick, text_tokens)], axis=0) + attended
    hat_two, factor_two = normalized(middle)
    image_n2 = (hat_two[:pairs] * image_gain_two + image_bias_two).astype(BF16)
    normed_two = (hat_two[pairs:] * text_gain_two + text_bias_two).astype(BF16)
    image_active = gelu_parts(dot(image_n2, image_up) + image_up_bias)[0].astype(BF16)
    active, slope = gelu_parts(dot(normed_two, text_up) + text_up_bias)
    active = active.astype(BF16)
    branch = jnp.concatenate([dot(image_active, image_down), dot(active, text_down)], axis=0)
    final = middle + lax.psum(branch.astype(BF16), "mp").astype(F32)

    everyone = lax.all_gather(final.astype(BF16), "dp").astype(F32)
    total = everyone.shape[0] * pairs
    image_low = unit(everyone[:, :pairs].reshape(total, features)).astype(BF16)
    pooled = final[pairs:]
    text_low = unit(everyone[:, pairs:].reshape(total, features)).astype(BF16)
    logits = 64.0 * dot_nt(text_low, image_low)
    column_lse = jax.nn.logsumexp(logits, axis=0)
    own = lax.dynamic_slice_in_dim(logits, rank * pairs, pairs, axis=0)
    row_lse = jax.nn.logsumexp(own, axis=1)
    own_columns = lax.dynamic_slice_in_dim(column_lse, rank * pairs, pairs)
    onehot = (labels[:, None] == jnp.arange(total)[None, :]).astype(F32)
    pair_loss = 0.5 * (row_lse + own_columns) - jnp.sum(own * onehot, axis=1)
    grad_logits = (
        0.5 * (jnp.exp(own - row_lse[:, None]) + jnp.exp(own - column_lse[None, :])) - onehot
    )
    grad_embed = 64.0 * dot(grad_logits.astype(BF16), image_low)
    scale = lax.rsqrt(jnp.sum(pooled * pooled, axis=-1, keepdims=True) + 1e-06)
    text_unit = pooled * scale
    grad_final = scale * (
        grad_embed - text_unit * jnp.sum(text_unit * grad_embed, axis=-1, keepdims=True)
    )

    final_low = grad_final.astype(BF16)
    grad_hidden = (dot_nt(final_low, text_down) * slope).astype(BF16)
    grad_normed_two = lax.psum(dot_nt(grad_hidden, text_up).astype(BF16), "mp").astype(F32)
    hat_two = hat_two[pairs:]
    grad_middle = grad_final + norm_back(grad_normed_two, hat_two, factor_two[pairs:], text_gain_two)
    middle_low = grad_middle.astype(BF16)
    grad_context = dot_nt(middle_low, text_out).astype(BF16)
    grad_folded = dot(head_blocks(grad_context.astype(F32), width).astype(BF16), text_weights[2])
    grad_folded = grad_folded.astype(BF16)
    grad_probs = dot_nt(grad_folded, normed)
    grad_scores = probs * (grad_probs - jnp.sum(grad_probs * probs, axis=-1, keepdims=True))
    grad_scores = (grad_scores * HEAD**-0.5).astype(BF16)
    mixed_back = dot(grad_scores, normed).astype(BF16)
    grad_queries = head_pick(dot_nt(mixed_back, text_weights[1]), width).astype(BF16)
    grad_normed = dot_tn(grad_scores, folded) + dot_tn(probs.astype(BF16), grad_folded)
    grad_normed = grad_normed + dot_tn(pick, dot(grad_queries, text_weights[0]).astype(BF16))
    grad_normed = lax.psum(grad_normed.astype(BF16), "mp").astype(F32)
    text_grad = norm_back(grad_normed, hat_one, factor_one, text_gain_one)
    text_grad = text_grad + dot_tn(pick, middle_low)

    vectors = jnp.concatenate(
        [
            jnp.sum(grad_normed * hat_one, axis=0),
            jnp.sum(grad_normed, axis=0),
            jnp.sum(grad_normed_two * hat_two, axis=0),
            jnp.sum(grad_normed_two, axis=0),
            jnp.sum(grad_hidden.astype(F32), axis=0),
        ]
    )
    vectors = jnp.sum(lax.all_gather(vectors, "dp"), axis=0)
    cuts = [features, 2 * features, 3 * features, 4 * features]
    gain_one, bias_one, gain_two, bias_two, up_bias = jnp.split(vectors, cuts)

    def by_head(blocks):
        return [blocks[h * pairs : (h + 1) * pairs] for h in range(heads)]

    pieces = [active, final_low, normed_two, grad_hidden, context, middle_low, normed_last]
    pieces += [grad_queries, queries, grad_context] + by_head(mixed_back) + by_head(mixed)
    sent = lax.all_gather(jnp.concatenate(pieces, axis=1), "dp").reshape(total, -1)
    got = []
    at = 0
    for piece in pieces:
        got.append(sent[:, at : at + piece.shape[1]])
        at += piece.shape[1]
    active, final_low, normed_two, grad_hidden, context, middle_low, normed_last = got[:7]
    grad_queries, queries, grad_context = got[7:10]
    mixed_back = got[10 : 10 + heads]
    mixed = got[10 + heads :]

    def per_head(rows, blocks):
        return jnp.concatenate(
            [dot_tn(rows[:, h * HEAD : (h + 1) * HEAD], blocks[h]) for h in range(heads)], axis=0
        )

    grad_qkv = jnp.stack(
        [
            dot_tn(grad_queries, normed_last),
            per_head(queries, mixed_back),
            per_head(grad_context, mixed),
        ]
    )
    return (
        pair_loss,
        text_grad,
        gain_one,
        bias_one,
        jnp.transpose(grad_qkv, (2, 0, 1)),
        dot_tn(context, middle_low),
        gain_two,
        bias_two,
        dot_tn(normed_two, grad_hidden),
        up_bias,
        dot_tn(active, final_low),
    )


def solution(mesh):
    placed = (
        P("dp", None),
        P("dp"),
        P("dp"),
        P("dp", None),
        P(),
        P(),
        P(None, None, "mp"),
        P("mp", None),
        P(),
        P(),
        P(None, "mp"),
        P("mp"),
        P("mp", None),
        P(),
        P(),
        P(None, None, "mp"),
        P("mp", None),
        P(),
        P(),
        P(None, "mp"),
        P("mp"),
        P("mp", None),
    )
    return jax.shard_map(
        plain_device,
        mesh=mesh,
        in_specs=placed,
        out_specs=(
            P("dp"),
            P("dp", None),
            P(),
            P(),
            P(None, None, "mp"),
            P("mp", None),
            P(),
            P(),
            P(None, "mp"),
            P("mp"),
            P("mp", None),
        ),
        check_vma=False,
    )
```

time: 678 us -> 290 us (0.43)
  waiting for transfers between devices: 458 us -> 131 us
  local copies, waits for them, and re-layouts: 53.9 us -> 12.6 us
  blocking collectives: 39.5 us -> 74.4 us
  matrix products: 58.5 us -> 38 us
  starting transfers between devices: 17.6 us -> 0.16 us
  other arithmetic: 33.7 us -> 18.6 us
    psum x5 -> x3, waiting for transfers between devices: 364 us -> 94.1 us  [the longest x1 33 us: plain_device(): grad_normed = lax.psum(grad_normed.astype(BF16), 'mp').astype(F32)]
    ppermute x37 -> x0, waiting for transfers between devices: 94.3 us -> none  [from_behind(): lax.ppermute(value, axis, [(i, (i + by) % peers) for i in range(peers)])]
    all_gather x0 -> x2, blocking collectives: none -> 63.4 us  [the longest x1 32.2 us: plain_device(): everyone = lax.all_gather(final.astype(BF16), 'dp').astype(F32)]
    all_gather x0 -> x1, waiting for transfers between devices: none -> 36.5 us  [plain_device(): lax.all_gather(jnp.concatenate(pieces, axis=1), 'dp').reshape(total, -1)]
    psum x1, blocking collectives: 39.5 us -> 11 us  [plain_device(): lax.psum(dot_nt(grad_hidden, text_up).astype(BF16), 'mp').astype(F32)]
    unnamed x106 -> x144, local copies, waits for them, and re-layouts: 23.3 us -> 3.97 us
    ppermute x37 -> x0, starting transfers between devices: 16.9 us -> none  [from_behind(): lax.ppermute(value, axis, [(i, (i + by) % peers) for i in range(peers)])]
    reshape x6 -> x1, local copies, waits for them, and re-layouts: 17.3 us -> 4.09 us  [plain_device(): image_first = image_x.reshape(pairs, IMG_LEN, features)[:, 0]]
  transfers between devices with their start and end apart: 42 -> 4, of which waited for: 28 -> 4; matrix products, arithmetic and copies ran while one was open for 2% -> 3% of each run, Pallas kernels for 0% -> 0%
where the time goes in v1:
time: 290 us; the launch traced here: 289 us
  waiting for transfers between devices  131 us (45%)
  blocking collectives  74.4 us (26%)
  matrix products  38 us (13%)
  other arithmetic  18.6 us (6%)
  between operations  15 us (5%)
  local copies, waits for them, and re-layouts  12.6 us (4%)
    all_gather x1, waiting for transfers between devices, plain_device(): lax.all_gather(jnp.concatenate(pieces, axis=1), 'dp').reshape(total, -1)  36.5 us
    psum x1, waiting for transfers between devices, plain_device(): grad_normed = lax.psum(grad_normed.astype(BF16), 'mp').astype(F32)  33 us
    all_gather x1, blocking collectives, plain_device(): everyone = lax.all_gather(final.astype(BF16), 'dp').astype(F32)  32.2 us
    psum x1, waiting for transfers between devices, plain_device(): attended = lax.psum(attended.astype(BF16), 'mp').astype(F32)  31.9 us
    all_gather x1, blocking collectives, plain_device(): vectors = jnp.sum(lax.all_gather(vectors, 'dp'), axis=0)  31.3 us
    psum x1, waiting for transfers between devices, plain_device(): final = middle + lax.psum(branch.astype(BF16), 'mp').astype(F32)  29.2 us
    dot_general x14, matrix products, dot_tn(): lax.dot_general(a, b, (((0,), (0,)), ((), ())), preferred_element_type=F32)  17.2 us
    dot_general x12, matrix products, dot_nt(): lax.dot_general(a, b, (((1,), (1,)), ((), ())), preferred_element_type=F32)  13.9 us
  transfers between devices with their start and end apart: 4, of which 4 were waited for; matrix products, arithmetic and copies ran while one was open for 3% of the time, Pallas kernels for 0%

profile of v1, /device:TPU:0, one launch (start us, length us, event | category | flops | bytes accessed | tf_op | source)
XLA Modules:
  0.0 289.5 jit_solution(146125865694107802)
XLA Ops:
  7.3 4.1 %reshape.246 = f32[24,50,768]{2,1,0:T(8,128)} reshape(bf16[1200,768]{1,0:T(8,128)(2,1)} %param.25) | data formatting | bytes 5529600 | tf_op jit(solution)/shard_map/reshape | solution.py:117
  12.0 1.3 slice_reduce_fusion
  14.4 2.0 add_convert_fusion
  16.4 1.3 select_convert_fusion.2
  17.7 3.2 %fusion.163 = (f32[72]{0:T(128)S(1)}, f32[72,1200]{1,0:T(8,128)}) fusion(bf16[1200,768]{1,0:T(8,128)(2,1)} %add_convert_fusion, bf16[3,192,768]{2,1,0:T(8,128)(2,1)} %bitcast.107, bf16[24,192]{1,0:T(8,128)(2,1)S(1)} %get-tuple-element.46, bf16[24,192]{1,0:T(8,128)(2,1)S(1)} %get-tuple-element.47, bf16[24,192]{1,0:T(8,128)(2,1)S(1)} %get-tuple-element.45, ...), kind=kOutput, calls=%fused_computation.285 | convolution fusion | flops 154514240 | bytes 2540448 | tf_op jit(solution)/shard_map/dot_general | solution.py:17
  21.0 1.3 fusion.21
  22.3 2.4 fusion.2
  26.4 1.8 fusion.111
  31.7 31.9 %all-reduce.4.cloned.1.call-done = bf16[48,768]{1,0:T(8,128)(2,1)} async-done(((bf16[48,768]{1,0:T(8,128)(2,1)}), bf16[48,768]{1,0:T(8,128)(2,1)}) %all-reduce.4.cloned.1.call-update) | async-done | bytes 73744 | tf_op jit(solution)/shard_map/psum | solution.py:136
  64.6 1.1 multiply_reduce_fusion.3
  69.2 2.2 convolution_convert_fusion.10
  72.2 1.5 fusion.159
  74.3 29.2 %all-reduce.6.cloned.1.call-done = bf16[48,768]{1,0:T(8,128)(2,1)} async-done(((bf16[48,768]{1,0:T(8,128)(2,1)}), bf16[48,768]{1,0:T(8,128)(2,1)}) %all-reduce.6.cloned.1.call-update) | async-done | bytes 73744 | tf_op jit(solution)/shard_map/psum | solution.py:145
  104.5 32.2 %all-gather = bf16[384,768]{1,0:T(8,128)(2,1)S(1)} all-gather(bf16[48,768]{1,0:T(8,128)(2,1)S(1)} %get-tuple-element.25), channel_id=2, replica_groups=mesh['dp'=8,'mp'=4] {'dp'}, dimensions={0}, use_global_device_ids=true | all-gather | bytes 663552 | tf_op jit(solution)/shard_map/all_gather | solution.py:147
  140.9 1.1 convert_reduce_fusion.4
  142.6 1.1 convolution_convert_fusion.8
  143.6 11.0 %psum.30 = bf16[24,768]{1,0:T(8,128)(2,1)S(1)} all-reduce(bf16[24,768]{1,0:T(8,128)(2,1)} %convolution_convert_fusion.8), channel_id=1, replica_groups=mesh['dp'=8,'mp'=4] {'mp'}, use_global_device_ids=true, to_apply=%region_24.25 | all-reduce | flops 18432 | bytes 73728 | tf_op jit(solution)/shard_map/psum | solution.py:171
  160.8 2.1 fusion.1
  164.0 33.0 %all-reduce.8.cloned.1.call-done = bf16[256,768]{1,0:T(8,128)(2,1)} async-done(((bf16[256,768]{1,0:T(8,128)(2,1)}), bf16[256,768]{1,0:T(8,128)(2,1)}) %all-reduce.8.cloned.1.call-update) | async-done | bytes 393232 | tf_op jit(solution)/shard_map/psum | solution.py:185
  197.0 1.4 fusion.19
  198.6 31.3 %all-gather.3 = f32[8,1,3840]{2,1,0:T(1,128)S(1)} all-gather(f32[1,1,3840]{2,1,0:T(1,128)S(1)} %reshape.254), channel_id=3, replica_groups=mesh['dp'=8,'mp'=4] {'dp'}, dimensions={0}, use_global_device_ids=true | all-gather | bytes 138240 | tf_op jit(solution)/shard_map/all_gather | solution.py:198
  230.6 2.3 convolution_add_fusion
  232.9 36.5 %all-gather.6.cloned.1.call-done = bf16[192,9984]{1,0:T(8,128)(2,1)} async-done(((bf16[24,9984]{1,0:T(8,128)(2,1)}), bf16[192,9984]{1,0:T(8,128)(2,1)}) %all-gather.6.cloned.1.call-update) | async-done | bytes 3833872 | tf_op jit(solution)/shard_map/all_gather | solution.py:207
  269.5 1.3 fusion.36
  270.8 1.3 fusion.38
  272.1 1.2 fusion.40
  273.3 1.3 fusion.30
  274.6 1.2 fusion.32
  276.6 1.3 maximum_bitcast_fusion
  277.9 1.9 fusion.22
  279.8 1.9 fusion.25
  281.7 1.2 fusion.28
  (236 shorter events, 26.6 us)
Async XLA Ops:
  7.2 60.2 %copy-start = (bf16[768,768]{1,0:T(8,128)(2,1)S(1)}, bf16[768,768]{1,0:T(8,128)(2,1)}, u32[]{:S(2)}) copy-start(bf16[768,768]{1,0:T(8,128)(2,1)} %param.41) | copy-start | bytes 3538948
  7.2 56.4 %all-reduce.4.cloned.1.call-start = ((), (), s32[]{:S(2)}) async-start(), calls=%async_computation | async-start | bytes 147456 | tf_op jit(solution)/shard_map/psum | solution.py:136
  7.3 22.3 %copy-start.44 = (pred[192]{0:T(512)(128)(4,1)}, pred[192]{0:T(512)(128)(4,1)S(1)}, u32[]{:S(2)}) copy-start(pred[192]{0:T(512)(128)(4,1)S(1)} %get-tuple-element.67) | copy-start | bytes 580
  7.3 22.3 %copy-start.46 = (pred[192]{0:T(512)(128)(4,1)}, pred[192]{0:T(512)(128)(4,1)S(1)}, u32[]{:S(2)}) copy-start(pred[192]{0:T(512)(128)(4,1)S(1)} %get-tuple-element.68) | copy-start | bytes 580
  7.3 22.3 %copy-start.48 = (pred[192]{0:T(512)(128)(4,1)}, pred[192]{0:T(512)(128)(4,1)S(1)}, u32[]{:S(2)}) copy-start(pred[192]{0:T(512)(128)(4,1)S(1)} %iota_compare_fusion.8) | copy-start | bytes 580
  12.0 19.5 %copy-start.56 = (s32[24]{0:T(128)}, s32[24]{0:T(128)S(1)}, u32[]{:S(2)}) copy-start(s32[24]{0:T(128)S(1)} %select_reduce_fusion.1) | copy-start | bytes 292
  16.4 5.9 %copy-start.3 = (bf16[1200,768]{1,0:T(8,128)(2,1)S(1)}, bf16[1200,768]{1,0:T(8,128)(2,1)}, u32[]{:S(2)}) copy-start(bf16[1200,768]{1,0:T(8,128)(2,1)} %add_convert_fusion) | copy-start | bytes 5529604
  21.0 5.0 %copy-start.37 = (f32[768]{0:T(1024)S(1)}, f32[768]{0:T(1024)}, u32[]{:S(2)}) copy-start(f32[768]{0:T(1024)} %param.35) | copy-start | bytes 9220
  21.0 5.0 %copy-start.62 = (f32[768]{0:T(1024)S(1)}, f32[768]{0:T(1024)}, u32[]{:S(2)}) copy-start(f32[768]{0:T(1024)} %param.36) | copy-start | bytes 9220
  24.8 5.8 %copy-start.10 = (bf16[192,768]{1,0:T(8,128)(2,1)S(1)}, bf16[192,768]{1,0:T(8,128)(2,1)}, u32[]{:S(2)}) copy-start(bf16[192,768]{1,0:T(8,128)(2,1)} %param.38) | copy-start | bytes 884740
  28.2 38.5 %copy-start.36 = (f32[768]{0:T(1024)S(1)}, f32[768]{0:T(1024)}, u32[]{:S(2)}) copy-start(f32[768]{0:T(1024)} %param.39) | copy-start | bytes 9220
  28.2 38.5 %copy-start.65 = (f32[768]{0:T(1024)S(1)}, f32[768]{0:T(1024)}, u32[]{:S(2)}) copy-start(f32[768]{0:T(1024)} %param.40) | copy-start | bytes 9220
  28.2 39.2 %copy-start.63 = (f32[768]{0:T(1024)S(1)}, f32[768]{0:T(1024)}, u32[]{:S(2)}) copy-start(f32[768]{0:T(1024)} %param.42) | copy-start | bytes 9220
  28.8 36.9 %copy-start.50 = (f32[72]{0:T(128)}, f32[72]{0:T(128)S(1)}, u32[]{:S(2)}) copy-start(f32[72]{0:T(128)S(1)} %get-tuple-element.52) | copy-start | bytes 868
  29.0 36.7 %copy-start.54 = (f32[72]{0:T(128)}, f32[72]{0:T(128)S(1)}, u32[]{:S(2)}) copy-start(f32[72]{0:T(128)S(1)} %fusion.68) | copy-start | bytes 868
  29.0 39.9 %copy-start.4 = (bf16[768,768]{1,0:T(8,128)(2,1)S(1)}, bf16[768,768]{1,0:T(8,128)(2,1)}, u32[]{:S(2)}) copy-start(bf16[768,768]{1,0:T(8,128)(2,1)} %param.43) | copy-start | bytes 3538948
  29.6 36.1 %copy-start.33 = (bf16[24,192]{1,0:T(8,128)(2,1)}, bf16[24,192]{1,0:T(8,128)(2,1)S(1)}, u32[]{:S(2)}) copy-start(bf16[24,192]{1,0:T(8,128)(2,1)S(1)} %fusion.121) | copy-start | bytes 27652
  31.4 72.1 %all-reduce.6.cloned.1.call-start = ((), (), s32[]{:S(2)}) async-start(), calls=%async_computation.1 | async-start | bytes 147456 | tf_op jit(solution)/shard_map/psum | solution.py:145
  72.2 124.8 %all-reduce.8.cloned.1.call-start = ((), (), s32[]{:S(2)}) async-start(), calls=%async_computation.2 | async-start | bytes 786432 | tf_op jit(solution)/shard_map/psum | solution.py:185
  138.5 17.8 %copy-start.11 = (bf16[192,768]{1,0:T(8,128)(2,1)S(1)}, bf16[192,768]{1,0:T(8,128)(2,1)}, u32[]{:S(2)}) copy-start(bf16[192,768]{1,0:T(8,128)(2,1)} %param.38) | copy-start | bytes 884740
  138.9 18.4 %copy-start.9 = (bf16[768,3,192]{0,2,1:T(8,128)(2,1)S(1)}, bf16[768,3,192]{0,2,1:T(8,128)(2,1)}, u32[]{:S(2)}) copy-start(bf16[768,3,192]{0,2,1:T(8,128)(2,1)} %param.37) | copy-start | bytes 2654212
  154.7 5.6 %copy-start.45 = (pred[192]{0:T(512)(128)(4,1)S(1)}, pred[192]{0:T(512)(128)(4,1)}, u32[]{:S(2)}) copy-start(pred[192]{0:T(512)(128)(4,1)} %copy-done.44) | copy-start | bytes 580
  154.7 5.6 %copy-start.47 = (pred[192]{0:T(512)(128)(4,1)S(1)}, pred[192]{0:T(512)(128)(4,1)}, u32[]{:S(2)}) copy-start(pred[192]{0:T(512)(128)(4,1)} %copy-done.46) | copy-start | bytes 580
  154.7 5.6 %copy-start.49 = (pred[192]{0:T(512)(128)(4,1)S(1)}, pred[192]{0:T(512)(128)(4,1)}, u32[]{:S(2)}) copy-start(pred[192]{0:T(512)(128)(4,1)} %copy-done.48) | copy-start | bytes 580
  160.3 36.7 %copy-start.38 = (f32[768]{0:T(1024)S(1)}, f32[768]{0:T(1024)}, u32[]{:S(2)}) copy-start(f32[768]{0:T(1024)} %param.35) | copy-start | bytes 9220
  160.3 36.7 %copy-start.40 = (f32[256]{0:T(256)S(1)}, f32[256]{0:T(256)}, u32[]{:S(2)}) copy-start(f32[256]{0:T(256)} %copy-done.39) | copy-start | bytes 3076
  160.3 36.7 %copy-start.53 = (f32[256]{0:T(256)S(1)}, f32[256]{0:T(256)}, u32[]{:S(2)}) copy-start(f32[256]{0:T(256)} %copy-done.52) | copy-start | bytes 3076
  160.7 37.7 %copy-start.43 = (f32[768]{0:T(1024)S(1)}, f32[768]{0:T(1024)}, u32[]{:S(2)}) copy-start(f32[768]{0:T(1024)} %get-tuple-element.19) | copy-start | bytes 9220
  160.7 37.8 %copy-start.42 = (f32[768]{0:T(1024)S(1)}, f32[768]{0:T(1024)}, u32[]{:S(2)}) copy-start(f32[768]{0:T(1024)} %get-tuple-element.22) | copy-start | bytes 9220
  160.7 37.8 %copy-start.41 = (f32[768]{0:T(1024)S(1)}, f32[768]{0:T(1024)}, u32[]{:S(2)}) copy-start(f32[768]{0:T(1024)} %get-tuple-element.65) | copy-start | bytes 9220
  162.9 106.5 %all-gather.6.cloned.1.call-start = ((), (), s32[]{:S(2)}) async-start(), calls=%async_computation.3 | async-start | bytes 4313088 | tf_op jit(solution)/shard_map/all_gather | solution.py:207
  269.5 6.3 %copy-start.6 = (bf16[192,9984]{1,0:T(8,128)(2,1)S(1)}, bf16[192,9984]{1,0:T(8,128)(2,1)}, u32[]{:S(2)}) copy-start(bf16[192,9984]{1,0:T(8,128)(2,1)} %all-gather.6.cloned.1.call-done) | copy-start | bytes 11501572
  (41 other events, 111.0 us)
Sparse Core Ops, SparseCore 0:
  31.6 32.0 all-reduce.3
  72.3 31.2 all-reduce.5
  163.0 33.9 all-reduce.7
  199.8 69.5 all-gather.5

commit v2 on v1

--- a/solution.py
+++ b/solution.py
@@ -1,6 +1,10 @@
+import functools
+
 import jax
 import jax.numpy as jnp
 from jax import lax
+from jax.experimental import pallas as pl
+from jax.experimental.pallas import tpu as pltpu
 from jax.sharding import PartitionSpec as P
 
 HEAD = 64
@@ -242,6 +246,922 @@
     )
 
 
+MESH = pl.DeviceIdType.MESH
+
+
+def to_tall(rows):
+    half = rows.shape[1] // 2
+    return jnp.concatenate([rows[:, :half], rows[:, half:]], axis=0).astype(BF16)
+
+
+def from_tall(tall):
+    count = tall.shape[0] // 2
+    wide = tall.astype(F32)
+    return jnp.concatenate([wide[:count], wide[count:]], axis=1)
+
+
+def from_tall_all(ref, n_dp):
+    talls = [ref[i].astype(F32) for i in range(n_dp)]
+    count = talls[0].shape[0] // 2
+    left = jnp.concatenate([t[:count] for t in talls], axis=0)
+    right = jnp.concatenate([t[count:] for t in talls], axis=0)
+    return jnp.concatenate([left, right], axis=1)
+
+
+def column_of(row, count):
+    shape = (count, row.shape[1])
+    same = lax.broadcasted_iota(jnp.int32, shape, 0) == lax.broadcasted_iota(jnp.int32, shape, 1)
+    return jnp.sum(jnp.where(same, row, 0), axis=1, keepdims=True)
+
+
+def caption_masks(seg, first, count):
+    captions = first + lax.broadcasted_iota(jnp.int32, (count, seg.shape[1]), 0)
+    mine = seg == captions
+    spot = lax.broadcasted_iota(jnp.int32, (count, seg.shape[1]), 1)
+    last = jnp.max(jnp.where(mine, spot, -1), axis=1, keepdims=True)
+    return mine, (spot == last).astype(F32).astype(BF16)
+
+
+def softmax_rows(scores, allowed):
+    scores = jnp.where(allowed, scores, -1e30)
+    expo = jnp.exp(scores - jnp.max(scores, axis=-1, keepdims=True))
+    return expo / jnp.sum(expo, axis=-1, keepdims=True)
+
+
+def stats_pack(top, bottom):
+    pieces = []
+    for row in (top, bottom):
+        pieces += [row[:, at : at + 128] for at in range(0, row.shape[1], 128)]
+    rows = len(pieces)
+    pieces.append(jnp.zeros((-rows % 8, 128), F32))
+    return jnp.concatenate(pieces, axis=0)
+
+
+def stats_unpack(packed, features):
+    per = features // 128
+    top = jnp.concatenate([packed[i : i + 1] for i in range(per)], axis=1)
+    bottom = jnp.concatenate([packed[per + i : per + i + 1] for i in range(per)], axis=1)
+    return top, bottom
+
+
+def step_kernel(
+    sizes,
+    text_hbm,
+    image_hbm,
+    iw_hbm,
+    io_hbm,
+    iu_hbm,
+    id_hbm,
+    tw_hbm,
+    to_hbm,
+    tu_hbm,
+    td_hbm,
+    seg_ref,
+    lab_ref,
+    ig1_ref,
+    ib1_ref,
+    ig2_ref,
+    ib2_ref,
+    iub_ref,
+    tg1_ref,
+    tb1_ref,
+    tg2_ref,
+    tb2_ref,
+    tub_ref,
+    act_o,
+    fin_o,
+    n2_o,
+    gh_o,
+    ctx_o,
+    mid_o,
+    nsel_o,
+    dq_o,
+    q_o,
+    gctx_o,
+    xk_o,
+    xv_o,
+    tg_o,
+    vec_o,
+    loss_o,
+    xi,
+    ni,
+    iw,
+    io,
+    iu,
+    idn,
+    tw,
+    to,
+    tu,
+    td,
+    tok,
+    nall,
+    ids,
+    ar,
+    gat,
+    fq,
+    fg,
+    fd,
+    stm,
+    std,
+    wide_a,
+    wide_b,
+    wide_c,
+    fold,
+    probs_all,
+    load_sem,
+    img_sem,
+    tz_s,
+    ty_s,
+    tc_s,
+    tz_r,
+    ty_r,
+    tc_r,
+    ar_s,
+    ar_r,
+    g_s,
+    g_f,
+    g_r,
+    f_s,
+    f_r,
+    sm_s,
+    sm_r,
+):
+    n_dp, n_mp, pairs, tokens, features, width = sizes
+    heads = width // HEAD
+    half_dp = n_dp // 2
+    total = n_dp * pairs
+    scale = HEAD**-0.5
+    d = lax.axis_index("dp")
+    m = lax.axis_index("mp")
+    core = lax.rem(m, 2)
+    hi = lax.div(d, 2)
+    lo = lax.rem(d, 2)
+    partner = (d, m + 1 - 2 * core)
+    beside = (hi * 2 + 1 - lo, m)
+
+    chunk = img_sem.shape[0]
+    chunk_rows = xi.shape[0] // chunk
+
+    def image_load(k):
+        rows = pl.ds(k * chunk_rows, chunk_rows)
+        return pltpu.make_async_copy(image_hbm.at[rows], xi.at[rows], img_sem.at[k])
+
+    loads = {}
+    order = [
+        ("text", text_hbm, tok.at[d]),
+        ("iw", iw_hbm, iw),
+        ("io", io_hbm, io),
+        ("tw", tw_hbm, tw),
+        ("to", to_hbm, to),
+        ("iu", iu_hbm, iu),
+        ("id", id_hbm, idn),
+        ("tu", tu_hbm, tu),
+        ("td", td_hbm, td),
+    ]
+    for k in range(chunk):
+        image_load(k).start()
+    for at, (name, src, dst) in enumerate(order):
+        loads[name] = pltpu.make_async_copy(src, dst, load_sem.at[at])
+        loads[name].start()
+
+    barrier = pltpu.get_barrier_semaphore()
+    for i in range(1, n_mp):
+        pl.semaphore_signal(
+            barrier, inc=1, device_id=(d, lax.rem(m + i, n_mp)), device_id_type=MESH
+        )
+
+    @pl.loop(1, n_dp)
+    def _(i):
+        pl.semaphore_signal(
+            barrier, inc=1, device_id=(lax.rem(d + i, n_dp), m), device_id_type=MESH
+        )
+
+    def remote(src, dst, send, recv, device):
+        return pltpu.make_async_remote_copy(
+            src_ref=src,
+            dst_ref=dst,
+            send_sem=send,
+            recv_sem=recv,
+            device_id=device,
+            device_id_type=MESH,
+        )
+
+    def mp_send(buf, send, recv):
+        for i in range(1, n_mp):
+            remote(
+                buf.at[m], buf.at[m], send.at[i], recv.at[i], (d, lax.rem(m + i, n_mp))
+            ).start()
+
+    def mp_recv(buf, send, recv):
+        for i in range(1, n_mp):
+            slot = buf.at[lax.rem(m + n_mp - i, n_mp)]
+            remote(slot, slot, send.at[i], recv.at[i], partner).wait_recv()
+
+    def mp_drain(buf, send, recv):
+        for i in range(1, n_mp):
+            remote(buf.at[m], buf.at[m], send.at[i], recv.at[i], partner).wait_send()
+
+    def split(mine, body):
+        for k in range(half_dp - 1):
+            body(2 * k + (2 - core if mine else 1 + core))
+
+        @pl.when(core == (1 if mine else 0))
+        def _():
+            body(2 * half_dp - 1)
+
+    def dp_send(at):
+        buf, send, recv = gat.at[at], g_s.at[at], g_r.at[at]
+
+        def body(i):
+            remote(
+                buf.at[d], buf.at[d], send.at[i], recv.at[i], (lax.rem(d + i, n_dp), m)
+            ).start()
+
+        split(True, body)
+
+    def dp_slot(buf, i):
+        return buf.at[lax.rem(d + n_dp - i, n_dp)]
+
+    def dp_forward(at, buf=None, send=None, recv=None, fwd=None):
+        buf, recv, fwd = gat.at[at], g_r.at[at], g_f.at[at]
+
+        def body(i):
+            slot = dp_slot(buf, i)
+            remote(slot, slot, fwd.at[i], recv.at[i], partner).wait_recv()
+            remote(slot, slot, fwd.at[i], recv.at[i], partner).start()
+
+        split(True, body)
+
+    def dp_recv(at):
+        buf, recv, fwd = gat.at[at], g_r.at[at], g_f.at[at]
+
+        def body(i):
+            slot = dp_slot(buf, i)
+            remote(slot, slot, fwd.at[i], recv.at[i], partner).wait_recv()
+
+        split(False, body)
+
+    def dp_drain(at):
+        buf, send, recv, fwd = gat.at[at], g_s.at[at], g_r.at[at], g_f.at[at]
+
+        def body(i):
+            slot = buf.at[d]
+            remote(slot, slot, send.at[i], recv.at[i], partner).wait_send()
+            remote(slot, slot, fwd.at[i], recv.at[i], partner).wait_send()
+
+        split(True, body)
+
+    def split_hi(mine, body):
+        for k in range(half_dp // 2 - 1):
+            body(2 * k + (2 - core if mine else 1 + core))
+
+        @pl.when(core == (1 if mine else 0))
+        def _():
+            body(half_dp - 1)
+
+    def tok_slot(i, across):
+        return tok.at[lax.rem(hi + half_dp - i, half_dp) * 2 + (1 - lo if across else lo)]
+
+    def tok_start():
+        def body(i):
+            slot = tok.at[d]
+            to_dev = (lax.rem(hi + i, half_dp) * 2 + lo, m)
+            remote(slot, slot, tz_s.at[i], tz_r.at[i], to_dev).start()
+
+        split_hi(True, body)
+
+        @pl.when(core == 0)
+        def _():
+            remote(tok.at[d], tok.at[d], ty_s.at[0], ty_r.at[0], beside).start()
+
+    def tok_second():
+        def body(i):
+            slot = tok_slot(i, False)
+            remote(slot, slot, tz_s.at[i], tz_r.at[i], partner).wait_recv()
+            remote(slot, slot, ty_s.at[i], ty_r.at[i], beside).start()
+            remote(slot, slot, tc_s.at[i], tc_r.at[i], partner).start()
+
+        split_hi(True, body)
+
+    def tok_third():
+        def body(i):
+            slot = tok_slot(i, True)
+            at = half_dp + i
+            remote(slot, slot, ty_s.at[i], ty_r.at[i], partner).wait_recv()
+            remote(slot, slot, tc_s.at[at], tc_r.at[at], partner).start()
+
+        split_hi(True, body)
+
+        @pl.when(core == 0)
+        def _():
+            body(0)
+
+    def tok_last():
+        def body(i):
+            slot = tok_slot(i, False)
+            remote(slot, slot, tc_s.at[i], tc_r.at[i], partner).wait_recv()
+            slot = tok_slot(i, True)
+            at = half_dp + i
+            remote(slot, slot, tc_s.at[at], tc_r.at[at], partner).wait_recv()
+
+        split_hi(False, body)
+
+        @pl.when(core == 1)
+        def _():
+            slot = tok_slot(0, True)
+            at = half_dp
+            remote(slot, slot, tc_s.at[at], tc_r.at[at], partner).wait_recv()
+
+    def tok_drain():
+        def body(i):
+            slot = tok.at[d]
+            at = half_dp + i
+            remote(slot, slot, tz_s.at[i], tz_r.at[i], partner).wait_send()
+            remote(slot, slot, ty_s.at[i], ty_r.at[i], partner).wait_send()
+            remote(slot, slot, tc_s.at[i], tc_r.at[i], partner).wait_send()
+            remote(slot, slot, tc_s.at[at], tc_r.at[at], partner).wait_send()
+
+        split_hi(True, body)
+
+        @pl.when(core == 0)
+        def _():
+            slot = tok.at[d]
+            remote(slot, slot, ty_s.at[0], ty_r.at[0], partner).wait_send()
+            at = half_dp
+            remote(slot, slot, tc_s.at[at], tc_r.at[at], partner).wait_send()
+
+    def attend_rows(queries, normed, allowed, weights):
+        stacked = head_blocks(queries.astype(F32), width).astype(BF16)
+        folded = dot(stacked, weights[1]).astype(BF16)
+        scores = dot_nt(folded, normed) * scale
+        probs = softmax_rows(scores, allowed)
+        mixed = dot(probs.astype(BF16), normed).astype(BF16)
+        context = head_pick(dot_nt(mixed, weights[2]), width).astype(BF16)
+        return folded, probs, context
+
+    gain, shift = ig1_ref[...], ib1_ref[...]
+
+    @pl.loop(0, chunk)
+    def _(k):
+        image_load(k).wait()
+        rows = pl.ds(pl.multiple_of(k * chunk_rows, 16), chunk_rows)
+        hat = normalized(xi[rows, :].astype(F32))[0]
+        ni[rows, :] = (hat * gain + shift).astype(BF16)
+
+    firsts = [i * IMG_LEN for i in range(pairs)]
+    image_first = jnp.concatenate([xi[r : r + 1, :].astype(F32) for r in firsts], axis=0)
+    first_n = (normalized(image_first)[0] * gain + shift).astype(BF16)
+    loads["iw"].wait()
+    image_q = dot_nt(first_n, iw[0]).astype(BF16)
+    shape = (pairs, xi.shape[0])
+    place = lax.broadcasted_iota(jnp.int32, shape, 1)
+    begin = lax.broadcasted_iota(jnp.int32, shape, 0) * IMG_LEN
+    inside = jnp.concatenate([(place >= begin) & (place < begin + IMG_LEN)] * heads, axis=0)
+    image_context = attend_rows(image_q, ni[...], inside, iw)[2]
+    loads["io"].wait()
+    ar[0, m] = to_tall(dot(image_context, io[...]))
+
+    ids[d, 0:1, :] = seg_ref[...]
+    ids[d, 1:2, 0:pairs] = lab_ref[...]
+    loads["text"].wait()
+    pl.semaphore_wait(barrier, n_mp - 1 + n_dp - 1)
+    mp_send(ar.at[0], ar_s.at[0], ar_r.at[0])
+    tok_start()
+
+    @pl.loop(1, n_dp)
+    def _(i):
+        remote(
+            ids.at[d], ids.at[d], sm_s.at[i], sm_r.at[i], (lax.rem(d + i, n_dp), m)
+        ).start()
+
+    x = tok[d].astype(F32)
+    hat_one, factor_one = normalized(x)
+    normed = (hat_one * tg1_ref[...] + tb1_ref[...]).astype(BF16)
+    mine, pick = caption_masks(seg_ref[...], d * pairs, pairs)
+    allowed = jnp.concatenate([mine] * heads, axis=0)
+    loads["tw"].wait()
+    queries = dot_nt(dot(pick, normed).astype(BF16), tw[0]).astype(BF16)
+    folded, probs, context = attend_rows(queries, normed, allowed, tw)
+    loads["to"].wait()
+    ar[1, m] = to_tall(dot(context, to[...]))
+    mp_send(ar.at[1], ar_s.at[1], ar_r.at[1])
+    text_last = dot(pick, tok[d])
+
+    def head_rows(blocks):
+        return [
+            jnp.sum(blocks[h * pairs : (h + 1) * pairs], axis=0, keepdims=True)
+            for h in range(heads)
+        ]
+
+    def padded(rows, small, count):
+        zeros = jnp.zeros((8 - len(small), tokens), F32)
+        foot = jnp.concatenate(small + [zeros], axis=0)
+        foot = jnp.concatenate([foot, jnp.zeros((8, features - tokens), F32)], axis=1)
+        return jnp.concatenate([rows, foot], axis=0)[:count].astype(BF16)
+
+    fq[m] = padded(folded.astype(F32), head_rows(probs), fq.shape[1])
+    mp_send(fq, f_s.at[0], f_r.at[0])
+
+    def summed(at):
+        mp_recv(ar.at[at], ar_s.at[at], ar_r.at[at])
+        full = ar[at, 0].astype(F32)
+        for i in range(1, n_mp):
+            full = full + ar[at, i].astype(F32)
+        count = full.shape[0] // 2
+        return jnp.concatenate([full[:count], full[count:]], axis=1)
+
+    image_middle = image_first + summed(0)
+    image_n2 = (normalized(image_middle)[0] * ig2_ref[...] + ib2_ref[...]).astype(BF16)
+    loads["iu"].wait()
+    image_active = gelu_parts(dot(image_n2, iu[...]) + iub_ref[...])[0].astype(BF16)
+    loads["id"].wait()
+    ar[2, m] = to_tall(dot(image_active, idn[...]))
+    mp_send(ar.at[2], ar_s.at[2], ar_r.at[2])
+
+    middle = text_last + summed(1)
+    gat[0, d] = to_tall(middle)
+    dp_send(0)
+    gain_two = tg2_ref[...]
+    hat_two, factor_two = normalized(middle)
+    normed_two = (hat_two * gain_two + tb2_ref[...]).astype(BF16)
+    loads["tu"].wait()
+    active = gelu_parts(dot(normed_two, tu[...]) + tub_ref[...])[0].astype(BF16)
+    loads["td"].wait()
+    ar[3, m] = to_tall(dot(active, td[...]))
+    mp_send(ar.at[3], ar_s.at[3], ar_r.at[3])
+
+    gat[1, d] = to_tall(unit(image_middle + summed(2)))
+    dp_send(1)
+    gat[2, d] = to_tall(middle + summed(3))
+    dp_send(2)
+
+    dp_forward(0)
+    tok_second()
+    dp_recv(0)
+    middle_all = from_tall_all(gat.at[0], n_dp)
+    hat_all, factor_all = normalized(middle_all)
+    wide_a[...] = hat_all
+    n2_all = (hat_all * gain_two + tb2_ref[...]).astype(BF16)
+    n2_o[...] = n2_all
+    act_all, slope_all = gelu_parts(dot(n2_all, tu[...]) + tub_ref[...])
+    act_o[...] = act_all.astype(BF16)
+    wide_b[...] = slope_all
+
+    dp_forward(1)
+    tok_third()
+    dp_forward(2)
+
+    @pl.loop(1, n_dp)
+    def _(i):
+        slot = dp_slot(ids, i)
+        remote(slot, slot, sm_s.at[i], sm_r.at[i], partner).wait_recv()
+
+    labels = jnp.concatenate([column_of(ids[i, 1:2, 0:128], pairs) for i in range(n_dp)], axis=0)
+    onehot = (labels == lax.broadcasted_iota(jnp.int32, (total, total), 1)).astype(F32)
+    dp_recv(1)
+    dp_recv(2)
+
+    image_low = from_tall_all(gat.at[1], n_dp).astype(BF16)
+    pooled = from_tall_all(gat.at[2], n_dp)
+    shrink = lax.rsqrt(jnp.sum(pooled * pooled, axis=-1, keepdims=True) + 1e-06)
+    text_unit = pooled * shrink
+    logits = 64.0 * dot_nt(text_unit.astype(BF16), image_low)
+    row_top = jnp.max(logits, axis=1, keepdims=True)
+    row_lse = row_top + jnp.log(jnp.sum(jnp.exp(logits - row_top), axis=1, keepdims=True))
+    col_top = jnp.max(logits, axis=0, keepdims=True)
+    col_lse = col_top + jnp.log(jnp.sum(jnp.exp(logits - col_top), axis=0, keepdims=True))
+    grad_logits = 0.5 * (jnp.exp(logits - row_lse) + jnp.exp(logits - col_lse)) - onehot
+    grad_embed = 64.0 * dot(grad_logits.astype(BF16), image_low)
+    along = jnp.sum(text_unit * grad_embed, axis=-1, keepdims=True)
+    grad_final = shrink * (grad_embed - text_unit * along)
+    final_low = grad_final.astype(BF16)
+    fin_o[...] = final_low
+    wide_c[...] = grad_final
+    grad_hidden = dot_nt(final_low, td[...]) * wide_b[...]
+    gh_o[...] = grad_hidden.astype(BF16)
+    wide_b[...] = grad_hidden
+    own = pl.ds(pl.multiple_of(d * pairs, 8), pairs)
+    ar[4, m] = to_tall(dot_nt(wide_b[own, :].astype(BF16), tu[...]))
+    mp_send(ar.at[4], ar_s.at[4], ar_r.at[4])
+
+    positive = jnp.sum(logits * onehot, axis=1, keepdims=True)
+    pair_loss = 0.5 * (row_lse + column_of(col_lse, total)) - positive
+    shape = (total, loss_o.shape[1])
+    spot = lax.broadcasted_iota(jnp.int32, shape, 1)
+    here = lax.broadcasted_iota(jnp.int32, shape, 0) == d * pairs + spot
+    loss_o[...] = jnp.sum(jnp.where(here, pair_loss, 0.0), axis=0, keepdims=True)
+    up_bias = jnp.sum(gh_o[...].astype(F32), axis=0, keepdims=True)
+
+    tok_last()
+    twice = 2 * pairs
+
+    def pair_masks(j):
+        seg = jnp.concatenate([ids[2 * j, 0:1, :], ids[2 * j + 1, 0:1, :]], axis=1)
+        return caption_masks(seg, j * twice, twice)
+
+    @pl.loop(0, half_dp)
+    def _(j):
+        rows = pl.ds(pl.multiple_of(j * twice, 16), twice)
+        both = tok[pl.ds(2 * j, 2)].reshape(2 * tokens, features).astype(F32)
+        hat = normalized(both)[0]
+        low = (hat * tg1_ref[...] + tb1_ref[...]).astype(BF16)
+        nall[j] = low
+        nsel_o[rows, :] = dot(pair_masks(j)[1], low).astype(BF16)
+
+    q_all = dot_nt(nsel_o[...], tw[0]).astype(BF16)
+    q_o[...] = q_all
+    fold[...] = dot(head_blocks(q_all.astype(F32), width).astype(BF16), tw[1]).astype(BF16).reshape(
+        heads, total, features
+    )
+
+    @pl.loop(0, half_dp)
+    def _(j):
+        rows = pl.ds(pl.multiple_of(j * twice, 16), twice)
+        low = nall[j]
+        blocks = jnp.concatenate([fold[h, rows, :] for h in range(heads)], axis=0)
+        mask = jnp.concatenate([pair_masks(j)[0]] * heads, axis=0)
+        both = softmax_rows(dot_nt(blocks, low) * scale, mask)
+        probs_all[j] = both
+        mixed = dot(both.astype(BF16), low).astype(BF16)
+        for h in range(heads):
+            xv_o[h, rows, :] = mixed[h * twice : (h + 1) * twice]
+
+    ctx_o[...] = head_pick(
+        dot_nt(xv_o[...].reshape(heads * total, features), tw[2]), width
+    ).astype(BF16)
+
+    grad_n2 = summed(4)
+    gat[3, d] = to_tall(grad_n2)
+    dp_send(3)
+    grad_middle = wide_c[own, :] + norm_back(grad_n2, hat_two, factor_two, gain_two)
+    middle_low = grad_middle.astype(BF16)
+    grad_context = dot_nt(middle_low, to[...]).astype(BF16)
+    grad_folded = dot(head_blocks(grad_context.astype(F32), width).astype(BF16), tw[2])
+    fg[m] = padded(grad_folded, [], fg.shape[1])
+    mp_send(fg, f_s.at[1], f_r.at[1])
+    grad_probs = dot_nt(grad_folded.astype(BF16), normed)
+    grad_scores = probs * (grad_probs - jnp.sum(grad_probs * probs, axis=-1, keepdims=True))
+    scaled = grad_scores * scale
+    mixed_back = dot(scaled.astype(BF16), normed).astype(BF16)
+    grad_queries = head_pick(dot_nt(mixed_back, tw[1]), width).astype(BF16)
+    fd[m] = padded(dot(grad_queries, tw[0]), head_rows(scaled), fd.shape[1])
+    mp_send(fd, f_s.at[2], f_r.at[2])
+
+    def spread(slots, ref, at):
+        parts = []
+        for i in slots:
+            foot = ref[i, at : at + 8, 0:tokens].astype(F32)
+            for h in range(heads):
+                parts.append(jnp.where(mine, foot[h : h + 1], 0.0))
+            parts.append(jnp.zeros((8, tokens), F32))
+        return jnp.concatenate(parts, axis=0).astype(BF16)
+
+    def first_norm_grad(slots, sources):
+        folds, backs, rests = sources
+        place_low = jnp.concatenate(
+            [jnp.concatenate([pick.astype(F32), jnp.zeros((8, tokens), F32)], axis=0)] * len(slots),
+            axis=0,
+        ).astype(BF16)
+        grads = dot_tn(spread(slots, fd, pairs), folds)
+        grads = grads + dot_tn(spread(slots, fq, pairs * heads), backs)
+        return grads + dot_tn(place_low, rests)
+
+    part = first_norm_grad([m], (fq[m], fg[m], fd[m]))
+    stm[m] = stats_pack(
+        jnp.sum(part * hat_one, axis=0, keepdims=True), jnp.sum(part, axis=0, keepdims=True)
+    )
+    mp_send(stm, f_s.at[3], f_r.at[3])
+
+    dp_forward(3)
+    mp_recv(stm, f_s.at[3], f_r.at[3])
+    own_stats = stm[0]
+    for i in range(1, n_mp):
+        own_stats = own_stats + stm[i]
+    std[d] = own_stats
+
+    @pl.loop(1, n_dp)
+    def _(i):
+        remote(
+            std.at[d], std.at[d], sm_s.at[n_dp + i], sm_r.at[n_dp + i], (lax.rem(d + i, n_dp), m)
+        ).start()
+
+    dp_recv(3)
+    grad_all = from_tall_all(gat.at[3], n_dp)
+    hat_all = wide_a[...]
+    back_all = norm_back(grad_all, hat_all, factor_all, gain_two)
+    mid_all = (wide_c[...] + back_all).astype(BF16)
+    mid_o[...] = mid_all
+    gain_two_grad = jnp.sum(grad_all * hat_all, axis=0, keepdims=True)
+    bias_two_grad = jnp.sum(grad_all, axis=0, keepdims=True)
+    gctx_all = dot_nt(mid_all, to[...]).astype(BF16)
+    gctx_o[...] = gctx_all
+    fold[...] = dot(
+        head_blocks(gctx_all.astype(F32), width).astype(BF16), tw[2]
+    ).astype(BF16).reshape(heads, total, features)
+
+    @pl.loop(0, half_dp)
+    def _(j):
+        rows = pl.ds(pl.multiple_of(j * twice, 16), twice)
+        low = nall[j]
+        blocks = jnp.concatenate([fold[h, rows, :] for h in range(heads)], axis=0)
+        grads = dot_nt(blocks, low)
+        both = probs_all[j]
+        grads = both * (grads - jnp.sum(grads * both, axis=-1, keepdims=True)) * scale
+        mixed = dot(grads.astype(BF16), low).astype(BF16)
+        for h in range(heads):
+            xk_o[h, rows, :] = mixed[h * twice : (h + 1) * twice]
+
+    dq_o[...] = head_pick(
+        dot_nt(xk_o[...].reshape(heads * total, features), tw[1]), width
+    ).astype(BF16)
+
+    for at, buf in ((0, fq), (1, fg), (2, fd)):
+        mp_recv(buf, f_s.at[at], f_r.at[at])
+    flat = [ref[...].reshape(n_mp * ref.shape[1], features) for ref in (fq, fg, fd)]
+    grad_normed = first_norm_grad(list(range(n_mp)), flat)
+    text_grad = norm_back(grad_normed, hat_one, factor_one, tg1_ref[...])
+    tg_o[...] = text_grad + dot_tn(pick, middle_low)
+
+    @pl.loop(1, n_dp)
+    def _(i):
+        slot = dp_slot(std, i)
+        remote(slot, slot, sm_s.at[n_dp + i], sm_r.at[n_dp + i], partner).wait_recv()
+
+    stats = std[0]
+    for i in range(1, n_dp):
+        stats = stats + std[i]
+    gain_one_grad, bias_one_grad = stats_unpack(stats, features)
+    vec_o[...] = jnp.concatenate(
+        [gain_one_grad, bias_one_grad, gain_two_grad, bias_two_grad, up_bias]
+        + [jnp.zeros((3, features), F32)],
+        axis=0,
+    )
+
+    for at in range(ar.shape[0]):
+        mp_drain(ar.at[at], ar_s.at[at], ar_r.at[at])
+    for at, buf in enumerate((fq, fg, fd, stm)):
+        mp_drain(buf, f_s.at[at], f_r.at[at])
+    for at in range(gat.shape[0]):
+        dp_drain(at)
+    tok_drain()
+
+    @pl.loop(1, n_dp)
+    def _(i):
+        remote(ids.at[d], ids.at[d], sm_s.at[i], sm_r.at[i], partner).wait_send()
+        at = n_dp + i
+        remote(std.at[d], std.at[d], sm_s.at[at], sm_r.at[at], partner).wait_send()
+
+
+def weights_kernel(
+    act,
+    fin,
+    n2,
+    gh,
+    ctx,
+    mid,
+    nsel,
+    dq,
+    q,
+    gctx,
+    xk,
+    xv,
+    tg,
+    vec,
+    loss,
+    tg_out,
+    qkv_out,
+    out_out,
+    up_out,
+    down_out,
+    loss_out,
+    g1_out,
+    b1_out,
+    g2_out,
+    b2_out,
+    ub_out,
+    qkv_buf,
+    out_buf,
+    up_buf,
+    down_buf,
+    sem,
+):
+    heads, total, features = xk.shape
+    width = q.shape[1]
+    started = []
+
+    def ship(src, dst):
+        copy = pltpu.make_async_copy(src, dst, sem.at[len(started)])
+        copy.start()
+        started.append(copy)
+
+    ship(tg, tg_out)
+    step = 256
+    for left, right, buf, dst in (
+        (act, fin, down_buf, down_out),
+        (n2, gh, up_buf, up_out),
+    ):
+        for at in range(0, features, step):
+            rows = pl.ds(at, step)
+            buf[rows, :] = dot_tn(left[:, at : at + step], right[...])
+            ship(buf.at[rows], dst.at[rows])
+    out_buf[...] = dot_tn(ctx[...], mid[...])
+    ship(out_buf, out_out)
+    qkv_buf[0] = dot_tn(dq[...], nsel[...])
+    ship(qkv_buf.at[0], qkv_out.at[0])
+    for at, rows, blocks in ((1, q, xk), (2, gctx, xv)):
+        stacked = head_blocks(rows[...].astype(F32), width).astype(BF16)
+        qkv_buf[at] = dot_tn(stacked, blocks[...].reshape(heads * total, features))
+        ship(qkv_buf.at[at], qkv_out.at[at])
+    for at, dst in enumerate((g1_out, b1_out, g2_out, b2_out, ub_out)):
+        dst[...] = vec[at : at + 1, :]
+    loss_out[...] = loss[:, 0 : loss_out.shape[1]]
+    for copy in started:
+        copy.wait()
+
+
+def kernel_device(
+    n_dp,
+    n_mp,
+    text_tokens,
+    segment_ids,
+    labels,
+    image_tokens,
+    image_gain_one,
+    image_bias_one,
+    image_qkv,
+    image_out,
+    image_gain_two,
+    image_bias_two,
+    image_up,
+    image_up_bias,
+    image_down,
+    text_gain_one,
+    text_bias_one,
+    text_qkv,
+    text_out,
+    text_gain_two,
+    text_bias_two,
+    text_up,
+    text_up_bias,
+    text_down,
+):
+    pairs = labels.shape[0]
+    tokens, features = text_tokens.shape
+    width = text_out.shape[0]
+    hidden = text_up.shape[1]
+    heads = width // HEAD
+    total = n_dp * pairs
+    half_dp = n_dp // 2
+    vmem = pltpu.VMEM
+    whole = pl.BlockSpec(memory_space=pltpu.VMEM)
+    anywhere = pl.BlockSpec(memory_space=pl.ANY)
+
+    def row(vector):
+        return vector.reshape(1, vector.shape[0])
+
+    def sems(*shape):
+        return pltpu.SemaphoreType.DMA(shape)
+
+    outs = [
+        ((total, hidden), BF16),
+        ((total, features), BF16),
+        ((total, features), BF16),
+        ((total, hidden), BF16),
+        ((total, width), BF16),
+        ((total, features), BF16),
+        ((total, features), BF16),
+        ((total, width), BF16),
+        ((total, width), BF16),
+        ((total, width), BF16),
+        ((heads, total, features), BF16),
+        ((heads, total, features), BF16),
+        ((tokens, features), F32),
+        ((8, features), F32),
+        ((1, 128), F32),
+    ]
+    tall = (2 * pairs, features // 2)
+    fold_rows = heads * pairs + 8
+    factors = pl.pallas_call(
+        functools.partial(step_kernel, (n_dp, n_mp, pairs, tokens, features, width)),
+        out_shape=[vmem(shape, dtype) for shape, dtype in outs],
+        in_specs=[anywhere] * 10 + [whole] * 12,
+        out_specs=[whole] * len(outs),
+        scratch_shapes=[
+            vmem(image_tokens.shape, BF16),
+            vmem(image_tokens.shape, BF16),
+            vmem((3, width, features), BF16),
+            vmem(image_out.shape, BF16),
+            vmem(image_up.shape, BF16),
+            vmem(image_down.shape, BF16),
+            vmem((3, width, features), BF16),
+            vmem(text_out.shape, BF16),
+            vmem(text_up.shape, BF16),
+            vmem(text_down.shape, BF16),
+            vmem((n_dp, tokens, features), BF16),
+            vmem((half_dp, 2 * tokens, features), BF16),
+            vmem((n_dp, 8, tokens), jnp.int32),
+            vmem((5, n_mp) + tall, BF16),
+            vmem((4, n_dp) + tall, BF16),
+            vmem((n_mp, fold_rows, features), BF16),
+            vmem((n_mp, fold_rows, features), BF16),
+            vmem((n_mp, pairs + 8, features), BF16),
+            vmem((n_mp, 16, 128), F32),
+            vmem((n_dp, 16, 128), F32),
+            vmem((total, features), F32),
+            vmem((total, hidden), F32),
+            vmem((total, features), F32),
+            vmem((heads, total, features), BF16),
+            vmem((half_dp, heads * 2 * pairs, 2 * tokens), F32),
+            sems(9),
+            sems(5),
+            sems(half_dp),
+            sems(half_dp),
+            sems(n_dp),
+            sems(half_dp),
+            sems(half_dp),
+            sems(n_dp),
+            sems(5, n_mp),
+            sems(5, n_mp),
+            sems(4, n_dp),
+            sems(4, n_dp),
+            sems(4, n_dp),
+            sems(4, n_mp),
+            sems(4, n_mp),
+            sems(2 * n_dp),
+            sems(2 * n_dp),
+        ],
+        compiler_params=pltpu.CompilerParams(
+            collective_id=0, has_side_effects=True, vmem_limit_bytes=48 * 2**20
+        ),
+        name="step",
+    )(
+        text_tokens,
+        image_tokens,
+        jnp.transpose(image_qkv, (1, 2, 0)),
+        image_out,
+        image_up,
+        image_down,
+        jnp.transpose(text_qkv, (1, 2, 0)),
+        text_out,
+        text_up,
+        text_down,
+        row(segment_ids),
+        row(labels),
+        row(image_gain_one),
+        row(image_bias_one),
+        row(image_gain_two),
+        row(image_bias_two),
+        row(image_up_bias),
+        row(text_gain_one),
+        row(text_bias_one),
+        row(text_gain_two),
+        row(text_bias_two),
+        row(text_up_bias),
+    )
+    vector = jax.ShapeDtypeStruct((1, features), F32)
+    results = pl.pallas_call(
+        weights_kernel,
+        out_shape=[
+            jax.ShapeDtypeStruct((tokens, features), F32),
+            jax.ShapeDtypeStruct((3, width, features), F32),
+            jax.ShapeDtypeStruct((width, features), F32),
+            jax.ShapeDtypeStruct((features, hidden), F32),
+            jax.ShapeDtypeStruct((hidden, features), F32),
+            jax.ShapeDtypeStruct((1, pairs), F32),
+            vector,
+            vector,
+            vector,
+            vector,
+            jax.ShapeDtypeStruct((1, hidden), F32),
+        ],
+        in_specs=[whole] * len(outs),
+        out_specs=[anywhere] * 5 + [whole] * 6,
+        scratch_shapes=[
+            vmem((3, width, features), F32),
+            vmem((width, features), F32),
+            vmem((features, hidden), F32),
+            vmem((hidden, features), F32),
+            sems(16),
+        ],
+        compiler_params=pltpu.CompilerParams(vmem_limit_bytes=32 * 2**20),
+        name="weights",
+    )(*[pltpu.with_memory_space_constraint(factor, pltpu.VMEM) for factor in factors])
+    text_grad, qkv, out, up, down, loss, gain_one, bias_one, gain_two, bias_two, up_bias = results
+    return (
+        loss.reshape(pairs),
+        text_grad,
+        gain_one.reshape(features),
+        bias_one.reshape(features),
+        jnp.transpose(qkv, (2, 0, 1)),
+        out,
+        gain_two.reshape(features),
+        bias_two.reshape(features),
+        up,
+        up_bias.reshape(hidden),
+        down,
+    )
+
+
 def solution(mesh):
     placed = (
         P("dp", None),
@@ -267,8 +1187,12 @@
         P("mp"),
         P("mp", None),
     )
+    n_dp, n_mp = mesh.shape["dp"], mesh.shape["mp"]
+    body = plain_device
+    if n_dp <= 16:
+        body = functools.partial(kernel_device, n_dp, n_mp)
     return jax.shard_map(
-        plain_device,
+        body,
         mesh=mesh,
         in_specs=placed,
         out_specs=(

time: 290 us -> 95.2 us (0.33)
  waiting for transfers between devices: 131 us -> 0 us
  Pallas kernels: 0 us -> 79.8 us
  blocking collectives: 74.4 us -> 0 us
  matrix products: 38 us -> 0 us
  other arithmetic: 18.6 us -> 3.03 us
  between operations: 15 us -> 0.67 us
    psum x3 -> x0, waiting for transfers between devices: 94.1 us -> none  [the longest x1 33 us: plain_device(): grad_normed = lax.psum(grad_normed.astype(BF16), 'mp').astype(F32)]
    pallas_call x0 -> x2, Pallas kernels: none -> 79.8 us  [the longest x1 75.8 us: kernel_device(): pl.pallas_call(functools.partial(step_kernel, (n_dp, n_mp, pairs, tokens,...]
    all_gather x2 -> x0, blocking collectives: 63.4 us -> none  [the longest x1 32.2 us: plain_device(): everyone = lax.all_gather(final.astype(BF16), 'dp').astype(F32)]
    dot_general x38 -> x0, matrix products: 38 us -> none  [the longest x14 17.2 us: dot_tn(): lax.dot_general(a, b, (((0,), (0,)), ((), ())), preferred_element_type=F32)]
    all_gather x1 -> x0, waiting for transfers between devices: 36.5 us -> none  [plain_device(): lax.all_gather(jnp.concatenate(pieces, axis=1), 'dp').reshape(total, -1)]
    psum x1 -> x0, blocking collectives: 11 us -> none  [plain_device(): lax.psum(dot_nt(grad_hidden, text_up).astype(BF16), 'mp').astype(F32)]
    reduce_sum x17 -> x0, other arithmetic: 9.11 us -> none  [the longest x4 2.79 us: normalized(): center = values - jnp.mean(values, axis=-1, keepdims=True)]
    convert_element_type x11 -> x0, other arithmetic: 4.58 us -> none  [the longest x1 1.96 us: plain_device(): (normalized(image_x)[0] * image_gain_one + image_bias_one).astype(BF16)]
  transfers between devices with their start and end apart: 4 -> 0, of which waited for: 4 -> 0; matrix products, arithmetic and copies ran while one was open for 3% -> 0% of each run, Pallas kernels for 0% -> 0%
where the time goes in v2:
time: 95.2 us; the launch traced here: 94.7 us
  Pallas kernels  79.8 us (84%)
  local copies, waits for them, and re-layouts  11.1 us (12%)
  other arithmetic  3.03 us (3%)
    pallas_call x1, Pallas kernels, kernel_device(): pl.pallas_call(functools.partial(step_kernel, (n_dp, n_mp, pairs, tokens,...  75.8 us
    reshape x10, local copies, waits for them, and re-layouts, row(): return vector.reshape(1, vector.shape[0])  6.89 us
    unnamed x10, local copies, waits for them, and re-layouts  4.25 us
    pallas_call x1, Pallas kernels, kernel_device(): pl.pallas_call(weights_kernel, out_shape=[jax.ShapeDtypeStruct((tokens, f...  4.01 us
    pallas_call x5, other arithmetic, kernel_device(): pl.pallas_call(weights_kernel, out_shape=[jax.ShapeDtypeStruct((tokens, f...  3.03 us

profile of v2, /device:TPU:0, one launch (start us, length us, event | category | flops | bytes accessed | tf_op | source)
XLA Modules:
  0.0 94.7 jit_solution(1048521635811937776)
XLA Ops:
  0.6 0.7 reshape.78.ig1_ref
  1.3 0.7 reshape.79.ib1_ref
  2.0 0.7 reshape.80.ig2_ref
  2.7 0.7 reshape.81.ib2_ref
  3.4 0.7 reshape.82.iub_ref
  4.1 0.7 reshape.83.tg1_ref
  4.8 0.7 reshape.84.tb1_ref
  5.5 0.7 reshape.85.tg2_ref
  6.2 0.7 reshape.86.tb2_ref
  6.8 0.7 reshape.87.tub_ref
  7.5 0.0 copy-start
  7.5 1.0 %copy-done = bf16[256,768]{1,0:T(8,128)(2,1)S(1)} copy-done((bf16[256,768]{1,0:T(8,128)(2,1)S(1)}, bf16[256,768]{1,0:T(8,128)(2,1)}, u32[]{:S(2)}) %copy-start) | copy-done | bytes 393240
  8.5 0.0 copy-start.1
  8.5 1.0 %copy-done.1 = bf16[192,768]{1,0:T(8,128)(2,1)S(1)} copy-done((bf16[192,768]{1,0:T(8,128)(2,1)S(1)}, bf16[192,768]{1,0:T(8,128)(2,1)}, u32[]{:S(2)}) %copy-start.1) | copy-done | bytes 294936
  9.5 0.0 copy-start.2
  9.5 1.0 %copy-done.2 = bf16[192,768]{1,0:T(8,128)(2,1)S(1)} copy-done((bf16[192,768]{1,0:T(8,128)(2,1)S(1)}, bf16[192,768]{1,0:T(8,128)(2,1)}, u32[]{:S(2)}) %copy-start.2) | copy-done | bytes 294936
  10.5 0.0 copy-start.3
  10.5 0.7 copy-done.3
  11.1 0.0 copy-start.4
  11.1 0.7 copy-done.4
  11.8 75.8 %step.1 = (bf16[192,768]{1,0:T(8,128)(2,1)S(1)}, bf16[192,768]{1,0:T(8,128)(2,1)S(1)}, bf16[192,768]{1,0:T(8,128)(2,1)S(1)}, bf16[192,768]{1,0:T(8,128)(2,1)S(1)...) custom-call(bf16[256,768]{1,0:T(8,128)(2,1)S(1)} %copy-done, ...), custom_call_target="tpu_custom_call" | custom-call | tf_op jit(solution)/shard_map/step/pallas_call | solution.py:1044
  87.6 4.0 %weights.1 = (f32[256,768]{1,0:T(8,128)}, f32[3,192,768]{2,1,0:T(8,128)}, f32[192,768]{1,0:T(8,128)}, f32[768,768]{1,0:T(8,128)}, f32[768,768]{1,0:T(8,128)}, /*...) custom-call(bf16[192,768]{1,0:T(8,128)(2,1)S(1)} %get-tuple-element., ...), custom_call_target="tpu_custom_call" | custom-call | tf_op jit(solution)/shard_map/weights/pallas_call | solution.py:1122
  91.6 0.6 reduce
  92.2 0.6 reduce.1
  92.9 0.6 reduce.2
  93.5 0.6 reduce.3
  94.1 0.6 reduce.4
Async XLA Ops:
  7.5 1.0 %copy-start = (bf16[256,768]{1,0:T(8,128)(2,1)S(1)}, bf16[256,768]{1,0:T(8,128)(2,1)}, u32[]{:S(2)}) copy-start(bf16[256,768]{1,0:T(8,128)(2,1)} %text_hbm.1) | copy-start | bytes 1179652
  8.5 1.0 %copy-start.1 = (bf16[192,768]{1,0:T(8,128)(2,1)S(1)}, bf16[192,768]{1,0:T(8,128)(2,1)}, u32[]{:S(2)}) copy-start(bf16[192,768]{1,0:T(8,128)(2,1)} %io_hbm.1) | copy-start | bytes 884740
  9.5 1.0 %copy-start.2 = (bf16[192,768]{1,0:T(8,128)(2,1)S(1)}, bf16[192,768]{1,0:T(8,128)(2,1)}, u32[]{:S(2)}) copy-start(bf16[192,768]{1,0:T(8,128)(2,1)} %to_hbm.1) | copy-start | bytes 884740
  10.5 0.7 copy-start.3
  11.1 0.7 copy-start.4

commit v3 on v2

--- a/solution.py
+++ b/solution.py
@@ -247,6 +247,7 @@
 
 
 MESH = pl.DeviceIdType.MESH
+TOKEN_SHARE = 64
 
 
 def to_tall(rows):
@@ -288,20 +289,20 @@
     return expo / jnp.sum(expo, axis=-1, keepdims=True)
 
 
-def stats_pack(top, bottom):
+def stats_pack(rows):
     pieces = []
-    for row in (top, bottom):
+    for row in rows:
         pieces += [row[:, at : at + 128] for at in range(0, row.shape[1], 128)]
-    rows = len(pieces)
-    pieces.append(jnp.zeros((-rows % 8, 128), F32))
+    pieces.append(jnp.zeros((-len(pieces) % 8 or 8, 128), F32))
     return jnp.concatenate(pieces, axis=0)
 
 
-def stats_unpack(packed, features):
+def stats_unpack(packed, count, features):
     per = features // 128
-    top = jnp.concatenate([packed[i : i + 1] for i in range(per)], axis=1)
-    bottom = jnp.concatenate([packed[per + i : per + i + 1] for i in range(per)], axis=1)
-    return top, bottom
+    return [
+        jnp.concatenate([packed[at * per + i : at * per + i + 1] for i in range(per)], axis=1)
+        for at in range(count)
+    ]
 
 
 def step_kernel(
@@ -316,18 +317,18 @@
     to_hbm,
     tu_hbm,
     td_hbm,
-    seg_ref,
-    lab_ref,
-    ig1_ref,
-    ib1_ref,
-    ig2_ref,
-    ib2_ref,
-    iub_ref,
-    tg1_ref,
-    tb1_ref,
-    tg2_ref,
-    tb2_ref,
-    tub_ref,
+    seg_hbm,
+    lab_hbm,
+    ig1_hbm,
+    ib1_hbm,
+    ig2_hbm,
+    ib2_hbm,
+    iub_hbm,
+    tg1_hbm,
+    tb1_hbm,
+    tg2_hbm,
+    tb2_hbm,
+    tub_hbm,
     act_o,
     fin_o,
     n2_o,
@@ -343,6 +344,7 @@
     tg_o,
     vec_o,
     loss_o,
+    xt,
     xi,
     ni,
     iw,
@@ -353,29 +355,43 @@
     to,
     tu,
     td,
+    seg_ref,
+    lab_ref,
+    ig1_ref,
+    ib1_ref,
+    ig2_ref,
+    ib2_ref,
+    iub_ref,
+    tg1_ref,
+    tb1_ref,
+    tg2_ref,
+    tb2_ref,
+    tub_ref,
     tok,
-    nall,
     ids,
+    prow,
+    drow,
+    stm,
+    std,
     ar,
     gat,
     fq,
     fg,
     fd,
-    stm,
-    std,
-    wide_a,
     wide_b,
     wide_c,
-    fold,
-    probs_all,
     load_sem,
     img_sem,
     tz_s,
+    tz_r,
     ty_s,
+    ty_r,
     tc_s,
-    tz_r,
-    ty_r,
     tc_r,
+    tx_s,
+    tx_r,
+    tf_s,
+    tf_r,
     ar_s,
     ar_r,
     g_s,
@@ -394,9 +410,11 @@
     d = lax.axis_index("dp")
     m = lax.axis_index("mp")
     core = lax.rem(m, 2)
+    side = lax.div(m, 2)
     hi = lax.div(d, 2)
     lo = lax.rem(d, 2)
     partner = (d, m + 1 - 2 * core)
+    across = (d, lax.rem(m + 2, 4))
     beside = (hi * 2 + 1 - lo, m)
 
     chunk = img_sem.shape[0]
@@ -407,22 +425,38 @@
         return pltpu.make_async_copy(image_hbm.at[rows], xi.at[rows], img_sem.at[k])
 
     loads = {}
-    order = [
-        ("text", text_hbm, tok.at[d]),
-        ("iw", iw_hbm, iw),
-        ("io", io_hbm, io),
-        ("tw", tw_hbm, tw),
-        ("to", to_hbm, to),
-        ("iu", iu_hbm, iu),
-        ("id", id_hbm, idn),
-        ("tu", tu_hbm, tu),
-        ("td", td_hbm, td),
-    ]
+
+    def load(name, src, dst):
+        loads[name] = pltpu.make_async_copy(src, dst, load_sem.at[len(loads)])
+        loads[name].start()
+
+    load("text", text_hbm, xt)
+    load("tg1", tg1_hbm, tg1_ref)
+    load("tb1", tb1_hbm, tb1_ref)
+    load("seg", seg_hbm, seg_ref)
+    load("lab", lab_hbm, lab_ref)
+    load("ig1", ig1_hbm, ig1_ref)
+    load("ib1", ib1_hbm, ib1_ref)
     for k in range(chunk):
         image_load(k).start()
-    for at, (name, src, dst) in enumerate(order):
-        loads[name] = pltpu.make_async_copy(src, dst, load_sem.at[at])
-        loads[name].start()
+    load("iw", iw_hbm, iw)
+    load("io", io_hbm, io)
+    load("tw", tw_hbm, tw)
+    load("to", to_hbm, to)
+    load("ig2", ig2_hbm, ig2_ref)
+    load("ib2", ib2_hbm, ib2_ref)
+    load("iub", iub_hbm, iub_ref)
+    load("tg2", tg2_hbm, tg2_ref)
+    load("tb2", tb2_hbm, tb2_ref)
+    load("tub", tub_hbm, tub_ref)
+    load("iu", iu_hbm, iu)
+    load("id", id_hbm, idn)
+    load("tu", tu_hbm, tu)
+    load("td", td_hbm, td)
+
+    def vector(name, ref):
+        loads[name].wait()
+        return ref[...].reshape(1, ref.shape[0])
 
     barrier = pltpu.get_barrier_semaphore()
     for i in range(1, n_mp):
@@ -461,6 +495,21 @@
         for i in range(1, n_mp):
             remote(buf.at[m], buf.at[m], send.at[i], recv.at[i], partner).wait_send()
 
+    def far_send(buf, send, recv):
+        slot = buf.at[m]
+        remote(slot, slot, send.at[2], recv.at[2], across).start()
+        remote(slot, slot, send.at[1], recv.at[1], partner).start()
+
+    def far_pass(buf, send, recv):
+        slot = buf.at[lax.rem(m + 2, 4)]
+        remote(slot, slot, send.at[3], recv.at[2], partner).wait_recv()
+        remote(slot, slot, send.at[3], recv.at[3], partner).start()
+
+    def far_recv(buf, send, recv):
+        slot = buf.at[m]
+        for i in (1, 3):
+            remote(slot, slot, send.at[i], recv.at[i], partner).wait_recv()
+
     def split(mine, body):
         for k in range(half_dp - 1):
             body(2 * k + (2 - core if mine else 1 + core))
@@ -468,6 +517,9 @@
         @pl.when(core == (1 if mine else 0))
         def _():
             body(2 * half_dp - 1)
+
+    def dp_slot(buf, i):
+        return buf.at[lax.rem(d + n_dp - i, n_dp)]
 
     def dp_send(at):
         buf, send, recv = gat.at[at], g_s.at[at], g_r.at[at]
@@ -479,10 +531,7 @@
 
         split(True, body)
 
-    def dp_slot(buf, i):
-        return buf.at[lax.rem(d + n_dp - i, n_dp)]
-
-    def dp_forward(at, buf=None, send=None, recv=None, fwd=None):
+    def dp_forward(at):
         buf, recv, fwd = gat.at[at], g_r.at[at], g_f.at[at]
 
         def body(i):
@@ -511,6 +560,31 @@
 
         split(True, body)
 
+    def small_send(at, buf):
+        @pl.loop(1, n_dp)
+        def _(i):
+            remote(
+                buf.at[d],
+                buf.at[d],
+                sm_s.at[at, i],
+                sm_r.at[at, i],
+                (lax.rem(d + i, n_dp), m),
+            ).start()
+
+    def small_recv(at, buf):
+        @pl.loop(1, n_dp)
+        def _(i):
+            slot = dp_slot(buf, i)
+            remote(slot, slot, sm_s.at[at, i], sm_r.at[at, i], partner).wait_recv()
+
+    def small_drain(at, buf):
+        @pl.loop(1, n_dp)
+        def _(i):
+            remote(buf.at[d], buf.at[d], sm_s.at[at, i], sm_r.at[at, i], partner).wait_send()
+
+    shared = TOKEN_SHARE * tokens // 256
+    kept = tokens - shared
+
     def split_hi(mine, body):
         for k in range(half_dp // 2 - 1):
             body(2 * k + (2 - core if mine else 1 + core))
@@ -519,36 +593,57 @@
         def _():
             body(half_dp - 1)
 
-    def tok_slot(i, across):
-        return tok.at[lax.rem(hi + half_dp - i, half_dp) * 2 + (1 - lo if across else lo)]
+    def split_both(mine, body):
+        def near(i):
+            body(i, lax.rem(hi + half_dp - i, half_dp) * 2 + lo)
+
+        def far(i):
+            body(half_dp + i, lax.rem(hi + half_dp - i, half_dp) * 2 + 1 - lo)
+
+        split_hi(mine, near)
+        split_hi(mine, far)
+
+        @pl.when(core == (0 if mine else 1))
+        def _():
+            far(0)
+
+    def kept_rows(slot):
+        return tok.at[slot, pl.ds(pl.multiple_of(side * shared, 16), kept)]
+
+    def given_rows(slot):
+        return tok.at[slot, pl.ds(pl.multiple_of(side * kept, 16), shared)]
+
+    def taken_rows(slot):
+        return tok.at[slot, pl.ds(pl.multiple_of((1 - side) * kept, 16), shared)]
 
     def tok_start():
+        rows = kept_rows(d)
+
         def body(i):
-            slot = tok.at[d]
             to_dev = (lax.rem(hi + i, half_dp) * 2 + lo, m)
-            remote(slot, slot, tz_s.at[i], tz_r.at[i], to_dev).start()
+            remote(rows, rows, tz_s.at[i], tz_r.at[i], to_dev).start()
 
         split_hi(True, body)
 
         @pl.when(core == 0)
         def _():
-            remote(tok.at[d], tok.at[d], ty_s.at[0], ty_r.at[0], beside).start()
+            remote(rows, rows, ty_s.at[0], ty_r.at[0], beside).start()
 
     def tok_second():
         def body(i):
-            slot = tok_slot(i, False)
-            remote(slot, slot, tz_s.at[i], tz_r.at[i], partner).wait_recv()
-            remote(slot, slot, ty_s.at[i], ty_r.at[i], beside).start()
-            remote(slot, slot, tc_s.at[i], tc_r.at[i], partner).start()
+            rows = kept_rows(lax.rem(hi + half_dp - i, half_dp) * 2 + lo)
+            remote(rows, rows, tz_s.at[i], tz_r.at[i], partner).wait_recv()
+            remote(rows, rows, ty_s.at[i], ty_r.at[i], beside).start()
+            remote(rows, rows, tc_s.at[i], tc_r.at[i], partner).start()
 
         split_hi(True, body)
 
     def tok_third():
         def body(i):
-            slot = tok_slot(i, True)
+            rows = kept_rows(lax.rem(hi + half_dp - i, half_dp) * 2 + 1 - lo)
             at = half_dp + i
-            remote(slot, slot, ty_s.at[i], ty_r.at[i], partner).wait_recv()
-            remote(slot, slot, tc_s.at[at], tc_r.at[at], partner).start()
+            remote(rows, rows, ty_s.at[i], ty_r.at[i], partner).wait_recv()
+            remote(rows, rows, tc_s.at[at], tc_r.at[at], partner).start()
 
         split_hi(True, body)
 
@@ -556,39 +651,67 @@
         def _():
             body(0)
 
+    def tok_near_across():
+        def body(i):
+            rows = given_rows(lax.rem(hi + half_dp - i, half_dp) * 2 + lo)
+            remote(rows, rows, tx_s.at[i], tx_r.at[i], across).start()
+
+        if shared:
+            split_hi(True, body)
+
+    def tok_far_across():
+        def body(i):
+            rows = given_rows(lax.rem(hi + half_dp - i, half_dp) * 2 + 1 - lo)
+            at = half_dp + i
+            remote(rows, rows, tx_s.at[at], tx_r.at[at], across).start()
+
+        if shared:
+            split_hi(True, body)
+
+            @pl.when(core == 0)
+            def _():
+                body(0)
+
+    def tok_pass():
+        def body(at, slot):
+            rows = taken_rows(slot)
+            remote(rows, rows, tx_s.at[at], tx_r.at[at], partner).wait_recv()
+            remote(rows, rows, tf_s.at[at], tf_r.at[at], partner).start()
+
+        if shared:
+            split_both(True, body)
+
     def tok_last():
-        def body(i):
-            slot = tok_slot(i, False)
-            remote(slot, slot, tc_s.at[i], tc_r.at[i], partner).wait_recv()
-            slot = tok_slot(i, True)
-            at = half_dp + i
-            remote(slot, slot, tc_s.at[at], tc_r.at[at], partner).wait_recv()
-
-        split_hi(False, body)
-
-        @pl.when(core == 1)
-        def _():
-            slot = tok_slot(0, True)
-            at = half_dp
-            remote(slot, slot, tc_s.at[at], tc_r.at[at], partner).wait_recv()
+        def body(at, slot):
+            rows = kept_rows(slot)
+            remote(rows, rows, tc_s.at[at], tc_r.at[at], partner).wait_recv()
+            if shared:
+                rows = taken_rows(slot)
+                remote(rows, rows, tf_s.at[at], tf_r.at[at], partner).wait_recv()
+
+        split_both(False, body)
 
     def tok_drain():
-        def body(i):
-            slot = tok.at[d]
-            at = half_dp + i
-            remote(slot, slot, tz_s.at[i], tz_r.at[i], partner).wait_send()
-            remote(slot, slot, ty_s.at[i], ty_r.at[i], partner).wait_send()
-            remote(slot, slot, tc_s.at[i], tc_r.at[i], partner).wait_send()
-            remote(slot, slot, tc_s.at[at], tc_r.at[at], partner).wait_send()
-
-        split_hi(True, body)
+        rows = kept_rows(d)
+
+        def body(at, slot):
+            remote(rows, rows, tc_s.at[at], tc_r.at[at], partner).wait_send()
+            if shared:
+                few = taken_rows(d)
+                remote(few, few, tx_s.at[at], tx_r.at[at], partner).wait_send()
+                remote(few, few, tf_s.at[at], tf_r.at[at], partner).wait_send()
+
+        split_both(True, body)
+
+        def both(i):
+            remote(rows, rows, tz_s.at[i], tz_r.at[i], partner).wait_send()
+            remote(rows, rows, ty_s.at[i], ty_r.at[i], partner).wait_send()
+
+        split_hi(True, both)
 
         @pl.when(core == 0)
         def _():
-            slot = tok.at[d]
-            remote(slot, slot, ty_s.at[0], ty_r.at[0], partner).wait_send()
-            at = half_dp
-            remote(slot, slot, tc_s.at[at], tc_r.at[at], partner).wait_send()
+            remote(rows, rows, ty_s.at[0], ty_r.at[0], partner).wait_send()
 
     def attend_rows(queries, normed, allowed, weights):
         stacked = head_blocks(queries.astype(F32), width).astype(BF16)
@@ -599,7 +722,18 @@
         context = head_pick(dot_nt(mixed, weights[2]), width).astype(BF16)
         return folded, probs, context
 
-    gain, shift = ig1_ref[...], ib1_ref[...]
+    loads["text"].wait()
+    gain_one = vector("tg1", tg1_ref)
+    hat_one, factor_one = normalized(xt[...].astype(F32))
+    tok[d] = (hat_one * gain_one + vector("tb1", tb1_ref)).astype(BF16)
+    seg = vector("seg", seg_ref)
+    ids[d, 0:1, :] = seg
+    ids[d, 1:2, 0:pairs] = vector("lab", lab_ref)
+    pl.semaphore_wait(barrier, n_mp - 1 + n_dp - 1)
+    tok_start()
+    small_send(0, ids)
+
+    gain, shift = vector("ig1", ig1_ref), vector("ib1", ib1_ref)
 
     @pl.loop(0, chunk)
     def _(k):
@@ -620,24 +754,10 @@
     image_context = attend_rows(image_q, ni[...], inside, iw)[2]
     loads["io"].wait()
     ar[0, m] = to_tall(dot(image_context, io[...]))
-
-    ids[d, 0:1, :] = seg_ref[...]
-    ids[d, 1:2, 0:pairs] = lab_ref[...]
-    loads["text"].wait()
-    pl.semaphore_wait(barrier, n_mp - 1 + n_dp - 1)
     mp_send(ar.at[0], ar_s.at[0], ar_r.at[0])
-    tok_start()
-
-    @pl.loop(1, n_dp)
-    def _(i):
-        remote(
-            ids.at[d], ids.at[d], sm_s.at[i], sm_r.at[i], (lax.rem(d + i, n_dp), m)
-        ).start()
-
-    x = tok[d].astype(F32)
-    hat_one, factor_one = normalized(x)
-    normed = (hat_one * tg1_ref[...] + tb1_ref[...]).astype(BF16)
-    mine, pick = caption_masks(seg_ref[...], d * pairs, pairs)
+
+    normed = tok[d]
+    mine, pick = caption_masks(seg, d * pairs, pairs)
     allowed = jnp.concatenate([mine] * heads, axis=0)
     loads["tw"].wait()
     queries = dot_nt(dot(pick, normed).astype(BF16), tw[0]).astype(BF16)
@@ -645,22 +765,25 @@
     loads["to"].wait()
     ar[1, m] = to_tall(dot(context, to[...]))
     mp_send(ar.at[1], ar_s.at[1], ar_r.at[1])
-    text_last = dot(pick, tok[d])
+    text_last = dot(pick, xt[...])
 
     def head_rows(blocks):
-        return [
+        rows = [
             jnp.sum(blocks[h * pairs : (h + 1) * pairs], axis=0, keepdims=True)
             for h in range(heads)
         ]
-
-    def padded(rows, small, count):
-        zeros = jnp.zeros((8 - len(small), tokens), F32)
-        foot = jnp.concatenate(small + [zeros], axis=0)
+        return jnp.concatenate(rows + [jnp.zeros((8 - heads, tokens), F32)], axis=0)
+
+    def padded(rows, foot):
         foot = jnp.concatenate([foot, jnp.zeros((8, features - tokens), F32)], axis=1)
-        return jnp.concatenate([rows, foot], axis=0)[:count].astype(BF16)
-
-    fq[m] = padded(folded.astype(F32), head_rows(probs), fq.shape[1])
-    mp_send(fq, f_s.at[0], f_r.at[0])
+        return jnp.concatenate([rows, foot], axis=0).astype(BF16)
+
+    no_foot = jnp.zeros((8, tokens), F32)
+    prob_rows = head_rows(probs)
+    prow[d] = prob_rows
+    small_send(1, prow)
+    fq[m] = padded(folded.astype(F32), prob_rows)
+    far_send(fq, f_s.at[0], f_r.at[0])
 
     def summed(at):
         mp_recv(ar.at[at], ar_s.at[at], ar_r.at[at])
@@ -671,9 +794,11 @@
         return jnp.concatenate([full[:count], full[count:]], axis=1)
 
     image_middle = image_first + summed(0)
-    image_n2 = (normalized(image_middle)[0] * ig2_ref[...] + ib2_ref[...]).astype(BF16)
+    gain, shift = vector("ig2", ig2_ref), vector("ib2", ib2_ref)
+    image_n2 = (normalized(image_middle)[0] * gain + shift).astype(BF16)
     loads["iu"].wait()
-    image_active = gelu_parts(dot(image_n2, iu[...]) + iub_ref[...])[0].astype(BF16)
+    image_hidden = dot(image_n2, iu[...]) + vector("iub", iub_ref)
+    image_active = gelu_parts(image_hidden)[0].astype(BF16)
     loads["id"].wait()
     ar[2, m] = to_tall(dot(image_active, idn[...]))
     mp_send(ar.at[2], ar_s.at[2], ar_r.at[2])
@@ -681,11 +806,12 @@
     middle = text_last + summed(1)
     gat[0, d] = to_tall(middle)
     dp_send(0)
-    gain_two = tg2_ref[...]
+    gain_two, shift_two = vector("tg2", tg2_ref), vector("tb2", tb2_ref)
     hat_two, factor_two = normalized(middle)
-    normed_two = (hat_two * gain_two + tb2_ref[...]).astype(BF16)
+    normed_two = (hat_two * gain_two + shift_two).astype(BF16)
     loads["tu"].wait()
-    active = gelu_parts(dot(normed_two, tu[...]) + tub_ref[...])[0].astype(BF16)
+    up_shift = vector("tub", tub_ref)
+    active = gelu_parts(dot(normed_two, tu[...]) + up_shift)[0].astype(BF16)
     loads["td"].wait()
     ar[3, m] = to_tall(dot(active, td[...]))
     mp_send(ar.at[3], ar_s.at[3], ar_r.at[3])
@@ -697,27 +823,20 @@
 
     dp_forward(0)
     tok_second()
+    tok_near_across()
+    far_pass(fq, f_s.at[0], f_r.at[0])
+    small_recv(0, ids)
+    labels = jnp.concatenate([column_of(ids[i, 1:2, 0:128], pairs) for i in range(n_dp)], axis=0)
+    onehot = (labels == lax.broadcasted_iota(jnp.int32, (total, total), 1)).astype(F32)
     dp_recv(0)
     middle_all = from_tall_all(gat.at[0], n_dp)
-    hat_all, factor_all = normalized(middle_all)
-    wide_a[...] = hat_all
-    n2_all = (hat_all * gain_two + tb2_ref[...]).astype(BF16)
+    n2_all = (normalized(middle_all)[0] * gain_two + shift_two).astype(BF16)
     n2_o[...] = n2_all
-    act_all, slope_all = gelu_parts(dot(n2_all, tu[...]) + tub_ref[...])
+    act_all, slope_all = gelu_parts(dot(n2_all, tu[...]) + up_shift)
     act_o[...] = act_all.astype(BF16)
     wide_b[...] = slope_all
-
     dp_forward(1)
-    tok_third()
     dp_forward(2)
-
-    @pl.loop(1, n_dp)
-    def _(i):
-        slot = dp_slot(ids, i)
-        remote(slot, slot, sm_s.at[i], sm_r.at[i], partner).wait_recv()
-
-    labels = jnp.concatenate([column_of(ids[i, 1:2, 0:128], pairs) for i in range(n_dp)], axis=0)
-    onehot = (labels == lax.broadcasted_iota(jnp.int32, (total, total), 1)).astype(F32)
     dp_recv(1)
     dp_recv(2)
 
@@ -744,6 +863,8 @@
     ar[4, m] = to_tall(dot_nt(wide_b[own, :].astype(BF16), tu[...]))
     mp_send(ar.at[4], ar_s.at[4], ar_r.at[4])
 
+    tok_third()
+    tok_far_across()
     positive = jnp.sum(logits * onehot, axis=1, keepdims=True)
     pair_loss = 0.5 * (row_lse + column_of(col_lse, total)) - positive
     shape = (total, loss_o.shape[1])
@@ -752,60 +873,25 @@
     loss_o[...] = jnp.sum(jnp.where(here, pair_loss, 0.0), axis=0, keepdims=True)
     up_bias = jnp.sum(gh_o[...].astype(F32), axis=0, keepdims=True)
 
-    tok_last()
-    twice = 2 * pairs
-
-    def pair_masks(j):
-        seg = jnp.concatenate([ids[2 * j, 0:1, :], ids[2 * j + 1, 0:1, :]], axis=1)
-        return caption_masks(seg, j * twice, twice)
-
-    @pl.loop(0, half_dp)
-    def _(j):
-        rows = pl.ds(pl.multiple_of(j * twice, 16), twice)
-        both = tok[pl.ds(2 * j, 2)].reshape(2 * tokens, features).astype(F32)
-        hat = normalized(both)[0]
-        low = (hat * tg1_ref[...] + tb1_ref[...]).astype(BF16)
-        nall[j] = low
-        nsel_o[rows, :] = dot(pair_masks(j)[1], low).astype(BF16)
-
-    q_all = dot_nt(nsel_o[...], tw[0]).astype(BF16)
-    q_o[...] = q_all
-    fold[...] = dot(head_blocks(q_all.astype(F32), width).astype(BF16), tw[1]).astype(BF16).reshape(
-        heads, total, features
-    )
-
-    @pl.loop(0, half_dp)
-    def _(j):
-        rows = pl.ds(pl.multiple_of(j * twice, 16), twice)
-        low = nall[j]
-        blocks = jnp.concatenate([fold[h, rows, :] for h in range(heads)], axis=0)
-        mask = jnp.concatenate([pair_masks(j)[0]] * heads, axis=0)
-        both = softmax_rows(dot_nt(blocks, low) * scale, mask)
-        probs_all[j] = both
-        mixed = dot(both.astype(BF16), low).astype(BF16)
-        for h in range(heads):
-            xv_o[h, rows, :] = mixed[h * twice : (h + 1) * twice]
-
-    ctx_o[...] = head_pick(
-        dot_nt(xv_o[...].reshape(heads * total, features), tw[2]), width
-    ).astype(BF16)
-
     grad_n2 = summed(4)
-    gat[3, d] = to_tall(grad_n2)
+    grad_middle = wide_c[own, :] + norm_back(grad_n2, hat_two, factor_two, gain_two)
+    gat[3, d] = to_tall(grad_middle)
     dp_send(3)
-    grad_middle = wide_c[own, :] + norm_back(grad_n2, hat_two, factor_two, gain_two)
     middle_low = grad_middle.astype(BF16)
     grad_context = dot_nt(middle_low, to[...]).astype(BF16)
     grad_folded = dot(head_blocks(grad_context.astype(F32), width).astype(BF16), tw[2])
-    fg[m] = padded(grad_folded, [], fg.shape[1])
-    mp_send(fg, f_s.at[1], f_r.at[1])
+    fg[m] = padded(grad_folded, no_foot)
+    far_send(fg, f_s.at[1], f_r.at[1])
     grad_probs = dot_nt(grad_folded.astype(BF16), normed)
     grad_scores = probs * (grad_probs - jnp.sum(grad_probs * probs, axis=-1, keepdims=True))
     scaled = grad_scores * scale
+    score_rows = head_rows(scaled)
+    drow[d] = score_rows
+    small_send(2, drow)
     mixed_back = dot(scaled.astype(BF16), normed).astype(BF16)
     grad_queries = head_pick(dot_nt(mixed_back, tw[1]), width).astype(BF16)
-    fd[m] = padded(dot(grad_queries, tw[0]), head_rows(scaled), fd.shape[1])
-    mp_send(fd, f_s.at[2], f_r.at[2])
+    fd[m] = padded(dot(grad_queries, tw[0]), score_rows)
+    far_send(fd, f_s.at[2], f_r.at[2])
 
     def spread(slots, ref, at):
         parts = []
@@ -828,73 +914,77 @@
 
     part = first_norm_grad([m], (fq[m], fg[m], fd[m]))
     stm[m] = stats_pack(
-        jnp.sum(part * hat_one, axis=0, keepdims=True), jnp.sum(part, axis=0, keepdims=True)
+        [jnp.sum(part * hat_one, axis=0, keepdims=True), jnp.sum(part, axis=0, keepdims=True)]
     )
     mp_send(stm, f_s.at[3], f_r.at[3])
-
+    stats_two = [
+        jnp.sum(grad_n2 * hat_two, axis=0, keepdims=True),
+        jnp.sum(grad_n2, axis=0, keepdims=True),
+    ]
+
+    tok_pass()
+    small_recv(1, prow)
+    tok_last()
+    twice = 2 * pairs
+
+    def pair_of(j, rows_ref):
+        seg = jnp.concatenate([ids[2 * j, 0:1, :], ids[2 * j + 1, 0:1, :]], axis=1)
+        here, picks = caption_masks(seg, j * twice, twice)
+        values = jnp.concatenate([rows_ref[2 * j], rows_ref[2 * j + 1]], axis=1)
+        parts = [jnp.where(here, values[h : h + 1], 0.0) for h in range(heads)]
+        low = tok[2 * j : 2 * j + 2].reshape(2 * tokens, features)
+        return jnp.concatenate(parts, axis=0).astype(BF16), picks, low
+
+    for j in range(half_dp):
+        values, picks, low = pair_of(j, prow)
+        rows = slice(j * twice, (j + 1) * twice)
+        mixed = dot(values, low).astype(BF16)
+        for h in range(heads):
+            xv_o[h, rows, :] = mixed[h * twice : (h + 1) * twice]
+        nsel_o[rows, :] = dot(picks, low).astype(BF16)
+
+    far_pass(fg, f_s.at[1], f_r.at[1])
+    far_pass(fd, f_s.at[2], f_r.at[2])
     dp_forward(3)
     mp_recv(stm, f_s.at[3], f_r.at[3])
     own_stats = stm[0]
     for i in range(1, n_mp):
         own_stats = own_stats + stm[i]
-    std[d] = own_stats
-
-    @pl.loop(1, n_dp)
-    def _(i):
-        remote(
-            std.at[d], std.at[d], sm_s.at[n_dp + i], sm_r.at[n_dp + i], (lax.rem(d + i, n_dp), m)
-        ).start()
-
-    dp_recv(3)
-    grad_all = from_tall_all(gat.at[3], n_dp)
-    hat_all = wide_a[...]
-    back_all = norm_back(grad_all, hat_all, factor_all, gain_two)
-    mid_all = (wide_c[...] + back_all).astype(BF16)
-    mid_o[...] = mid_all
-    gain_two_grad = jnp.sum(grad_all * hat_all, axis=0, keepdims=True)
-    bias_two_grad = jnp.sum(grad_all, axis=0, keepdims=True)
-    gctx_all = dot_nt(mid_all, to[...]).astype(BF16)
-    gctx_o[...] = gctx_all
-    fold[...] = dot(
-        head_blocks(gctx_all.astype(F32), width).astype(BF16), tw[2]
-    ).astype(BF16).reshape(heads, total, features)
-
-    @pl.loop(0, half_dp)
-    def _(j):
-        rows = pl.ds(pl.multiple_of(j * twice, 16), twice)
-        low = nall[j]
-        blocks = jnp.concatenate([fold[h, rows, :] for h in range(heads)], axis=0)
-        grads = dot_nt(blocks, low)
-        both = probs_all[j]
-        grads = both * (grads - jnp.sum(grads * both, axis=-1, keepdims=True)) * scale
-        mixed = dot(grads.astype(BF16), low).astype(BF16)
+    std[d] = stats_pack(stats_unpack(own_stats, 2, features) + stats_two)
+    small_send(3, std)
+    q_o[...] = dot_nt(nsel_o[...], tw[0]).astype(BF16)
+    ctx_o[...] = head_pick(
+        dot_nt(xv_o[...].reshape(heads * total, features), tw[2]), width
+    ).astype(BF16)
+
+    small_recv(2, drow)
+    for j in range(half_dp):
+        values, picks, low = pair_of(j, drow)
+        rows = slice(j * twice, (j + 1) * twice)
+        mixed = dot(values, low).astype(BF16)
         for h in range(heads):
             xk_o[h, rows, :] = mixed[h * twice : (h + 1) * twice]
-
     dq_o[...] = head_pick(
         dot_nt(xk_o[...].reshape(heads * total, features), tw[1]), width
     ).astype(BF16)
+    dp_recv(3)
+    mid_all = from_tall_all(gat.at[3], n_dp).astype(BF16)
+    mid_o[...] = mid_all
+    gctx_o[...] = dot_nt(mid_all, to[...]).astype(BF16)
 
     for at, buf in ((0, fq), (1, fg), (2, fd)):
-        mp_recv(buf, f_s.at[at], f_r.at[at])
+        far_recv(buf, f_s.at[at], f_r.at[at])
     flat = [ref[...].reshape(n_mp * ref.shape[1], features) for ref in (fq, fg, fd)]
     grad_normed = first_norm_grad(list(range(n_mp)), flat)
-    text_grad = norm_back(grad_normed, hat_one, factor_one, tg1_ref[...])
+    text_grad = norm_back(grad_normed, hat_one, factor_one, gain_one)
     tg_o[...] = text_grad + dot_tn(pick, middle_low)
 
-    @pl.loop(1, n_dp)
-    def _(i):
-        slot = dp_slot(std, i)
-        remote(slot, slot, sm_s.at[n_dp + i], sm_r.at[n_dp + i], partner).wait_recv()
-
+    small_recv(3, std)
     stats = std[0]
     for i in range(1, n_dp):
         stats = stats + std[i]
-    gain_one_grad, bias_one_grad = stats_unpack(stats, features)
     vec_o[...] = jnp.concatenate(
-        [gain_one_grad, bias_one_grad, gain_two_grad, bias_two_grad, up_bias]
-        + [jnp.zeros((3, features), F32)],
-        axis=0,
+        stats_unpack(stats, 4, features) + [up_bias, jnp.zeros((3, features), F32)], axis=0
     )
 
     for at in range(ar.shape[0]):
@@ -903,13 +993,9 @@
         mp_drain(buf, f_s.at[at], f_r.at[at])
     for at in range(gat.shape[0]):
         dp_drain(at)
+    for at, buf in enumerate((ids, prow, drow, std)):
+        small_drain(at, buf)
     tok_drain()
-
-    @pl.loop(1, n_dp)
-    def _(i):
-        remote(ids.at[d], ids.at[d], sm_s.at[i], sm_r.at[i], partner).wait_send()
-        at = n_dp + i
-        remote(std.at[d], std.at[d], sm_s.at[at], sm_r.at[at], partner).wait_send()
 
 
 def weights_kernel(
@@ -973,8 +1059,8 @@
         qkv_buf[at] = dot_tn(stacked, blocks[...].reshape(heads * total, features))
         ship(qkv_buf.at[at], qkv_out.at[at])
     for at, dst in enumerate((g1_out, b1_out, g2_out, b2_out, ub_out)):
-        dst[...] = vec[at : at + 1, :]
-    loss_out[...] = loss[:, 0 : loss_out.shape[1]]
+        dst[...] = vec[at, :]
+    loss_out[...] = loss[0, 0 : loss_out.shape[0]]
     for copy in started:
         copy.wait()
 
@@ -1016,9 +1102,6 @@
     whole = pl.BlockSpec(memory_space=pltpu.VMEM)
     anywhere = pl.BlockSpec(memory_space=pl.ANY)
 
-    def row(vector):
-        return vector.reshape(1, vector.shape[0])
-
     def sems(*shape):
         return pltpu.SemaphoreType.DMA(shape)
 
@@ -1041,12 +1124,39 @@
     ]
     tall = (2 * pairs, features // 2)
     fold_rows = heads * pairs + 8
+    vectors = (
+        segment_ids,
+        labels,
+        image_gain_one,
+        image_bias_one,
+        image_gain_two,
+        image_bias_two,
+        image_up_bias,
+        text_gain_one,
+        text_bias_one,
+        text_gain_two,
+        text_bias_two,
+        text_up_bias,
+    )
+    operands = (
+        text_tokens,
+        image_tokens,
+        jnp.transpose(image_qkv, (1, 2, 0)),
+        image_out,
+        image_up,
+        image_down,
+        jnp.transpose(text_qkv, (1, 2, 0)),
+        text_out,
+        text_up,
+        text_down,
+    ) + vectors
     factors = pl.pallas_call(
         functools.partial(step_kernel, (n_dp, n_mp, pairs, tokens, features, width)),
         out_shape=[vmem(shape, dtype) for shape, dtype in outs],
-        in_specs=[anywhere] * 10 + [whole] * 12,
+        in_specs=[anywhere] * len(operands),
         out_specs=[whole] * len(outs),
         scratch_shapes=[
+            vmem(text_tokens.shape, BF16),
             vmem(image_tokens.shape, BF16),
             vmem(image_tokens.shape, BF16),
             vmem((3, width, features), BF16),
@@ -1057,29 +1167,28 @@
             vmem(text_out.shape, BF16),
             vmem(text_up.shape, BF16),
             vmem(text_down.shape, BF16),
+        ]
+        + [vmem(array.shape, array.dtype) for array in vectors]
+        + [
             vmem((n_dp, tokens, features), BF16),
-            vmem((half_dp, 2 * tokens, features), BF16),
             vmem((n_dp, 8, tokens), jnp.int32),
+            vmem((n_dp, 8, tokens), F32),
+            vmem((n_dp, 8, tokens), F32),
+            vmem((n_mp, 16, 128), F32),
+            vmem((n_dp, 32, 128), F32),
             vmem((5, n_mp) + tall, BF16),
             vmem((4, n_dp) + tall, BF16),
             vmem((n_mp, fold_rows, features), BF16),
             vmem((n_mp, fold_rows, features), BF16),
             vmem((n_mp, pairs + 8, features), BF16),
-            vmem((n_mp, 16, 128), F32),
-            vmem((n_dp, 16, 128), F32),
-            vmem((total, features), F32),
             vmem((total, hidden), F32),
             vmem((total, features), F32),
-            vmem((heads, total, features), BF16),
-            vmem((half_dp, heads * 2 * pairs, 2 * tokens), F32),
-            sems(9),
+            sems(22),
             sems(5),
-            sems(half_dp),
-            sems(half_dp),
-            sems(n_dp),
-            sems(half_dp),
-            sems(half_dp),
-            sems(n_dp),
+        ]
+        + [sems(half_dp)] * 4
+        + [sems(n_dp)] * 6
+        + [
             sems(5, n_mp),
             sems(5, n_mp),
             sems(4, n_dp),
@@ -1087,38 +1196,15 @@
             sems(4, n_dp),
             sems(4, n_mp),
             sems(4, n_mp),
-            sems(2 * n_dp),
-            sems(2 * n_dp),
+            sems(4, n_dp),
+            sems(4, n_dp),
         ],
         compiler_params=pltpu.CompilerParams(
             collective_id=0, has_side_effects=True, vmem_limit_bytes=48 * 2**20
         ),
         name="step",
-    )(
-        text_tokens,
-        image_tokens,
-        jnp.transpose(image_qkv, (1, 2, 0)),
-        image_out,
-        image_up,
-        image_down,
-        jnp.transpose(text_qkv, (1, 2, 0)),
-        text_out,
-        text_up,
-        text_down,
-        row(segment_ids),
-        row(labels),
-        row(image_gain_one),
-        row(image_bias_one),
-        row(image_gain_two),
-        row(image_bias_two),
-        row(image_up_bias),
-        row(text_gain_one),
-        row(text_bias_one),
-        row(text_gain_two),
-        row(text_bias_two),
-        row(text_up_bias),
-    )
-    vector = jax.ShapeDtypeStruct((1, features), F32)
+    )(*[pltpu.with_memory_space_constraint(operand, pltpu.HBM) for operand in operands])
+    vector = jax.ShapeDtypeStruct((features,), F32)
     results = pl.pallas_call(
         weights_kernel,
         out_shape=[
@@ -1127,12 +1213,12 @@
             jax.ShapeDtypeStruct((width, features), F32),
             jax.ShapeDtypeStruct((features, hidden), F32),
             jax.ShapeDtypeStruct((hidden, features), F32),
-            jax.ShapeDtypeStruct((1, pairs), F32),
+            jax.ShapeDtypeStruct((pairs,), F32),
             vector,
             vector,
             vector,
             vector,
-            jax.ShapeDtypeStruct((1, hidden), F32),
+            jax.ShapeDtypeStruct((hidden,), F32),
         ],
         in_specs=[whole] * len(outs),
         out_specs=[anywhere] * 5 + [whole] * 6,
@@ -1148,16 +1234,16 @@
     )(*[pltpu.with_memory_space_constraint(factor, pltpu.VMEM) for factor in factors])
     text_grad, qkv, out, up, down, loss, gain_one, bias_one, gain_two, bias_two, up_bias = results
     return (
-        loss.reshape(pairs),
+        loss,
         text_grad,
-        gain_one.reshape(features),
-        bias_one.reshape(features),
+        gain_one,
+        bias_one,
         jnp.transpose(qkv, (2, 0, 1)),
         out,
-        gain_two.reshape(features),
-        bias_two.reshape(features),
+        gain_two,
+        bias_two,
         up,
-        up_bias.reshape(hidden),
+        up_bias,
         down,
     )
 
@@ -1189,7 +1275,7 @@
     )
     n_dp, n_mp = mesh.shape["dp"], mesh.shape["mp"]
     body = plain_device
-    if n_dp <= 16:
+    if n_dp <= 16 and n_dp % 4 == 0 and n_mp == 4:
         body = functools.partial(kernel_device, n_dp, n_mp)
     return jax.shard_map(
         body,

time: 95.2 us -> 62.7 us (0.66)
  Pallas kernels: 79.8 us -> 61.8 us
  local copies, waits for them, and re-layouts: 11.1 us -> 0 us
  other arithmetic: 3.03 us -> 0 us
    pallas_call x1, Pallas kernels: 75.8 us -> 57.7 us  [kernel_device(): pl.pallas_call(functools.partial(step_kernel, (n_dp, n_mp, pairs, tokens,...]
    reshape x10 -> x0, local copies, waits for them, and re-layouts: 6.89 us -> none  [row(): return vector.reshape(1, vector.shape[0])]
    unnamed x10 -> x0, local copies, waits for them, and re-layouts: 4.25 us -> none
    pallas_call x5 -> x0, other arithmetic: 3.03 us -> none  [kernel_device(): pl.pallas_call(weights_kernel, out_shape=[jax.ShapeDtypeStruct((tokens, f...]
where the time goes in v3:
time: 62.7 us; the launch traced here: 62.5 us
  Pallas kernels  61.8 us (99%)
  between operations  0.66 us (1%)
    pallas_call x1, Pallas kernels, kernel_device(): pl.pallas_call(functools.partial(step_kernel, (n_dp, n_mp, pairs, tokens,...  57.7 us
    pallas_call x1, Pallas kernels, kernel_device(): pl.pallas_call(weights_kernel, out_shape=[jax.ShapeDtypeStruct((tokens, f...  4.1 us

profile of v3, /device:TPU:0, one launch (start us, length us, event | category | flops | bytes accessed | tf_op | source)
XLA Modules:
  0.0 62.5 jit_solution(15006523610910180913)
XLA Ops:
  0.7 57.7 %step.1 = (bf16[192,768]{1,0:T(8,128)(2,1)S(1)}, bf16[192,768]{1,0:T(8,128)(2,1)S(1)}, bf16[192,768]{1,0:T(8,128)(2,1)S(1)}, bf16[192,768]{1,0:T(8,128)(2,1)S(1)...) custom-call(bf16[256,768]{1,0:T(8,128)(2,1)} %text_hbm.1, ...), custom_call_target="tpu_custom_call" | custom-call | tf_op jit(solution)/shard_map/step/pallas_call | solution.py:1153
  58.4 4.1 %weights.1 = (f32[256,768]{1,0:T(8,128)}, f32[3,192,768]{2,1,0:T(8,128)}, f32[192,768]{1,0:T(8,128)}, f32[768,768]{1,0:T(8,128)}, f32[768,768]{1,0:T(8,128)}, /*...) custom-call(bf16[192,768]{1,0:T(8,128)(2,1)S(1)} %get-tuple-element.37.a, ...), custom_call_target="tpu_custom_call" | custom-call | tf_op jit(solution)/shard_map/weights/pallas_call | solution.py:1208

commit v4 on v3

--- a/solution.py
+++ b/solution.py
@@ -247,7 +247,15 @@
 
 
 MESH = pl.DeviceIdType.MESH
-TOKEN_SHARE = 64
+TOKEN_PARTS = 2
+STEPS = {
+    0: (("start", 0), ("start", 1)),
+    3: (("second", 0), ("near", 0)),
+    4: (("second", 1), ("near", 1)),
+    5: (("third", 0), ("far", 0), ("pass", 0)),
+    6: (("third", 1), ("far", 1), ("pass", 1)),
+    8: (("last", 0), ("last", 1)),
+}
 
 
 def to_tall(rows):
@@ -259,14 +267,6 @@
     count = tall.shape[0] // 2
     wide = tall.astype(F32)
     return jnp.concatenate([wide[:count], wide[count:]], axis=1)
-
-
-def from_tall_all(ref, n_dp):
-    talls = [ref[i].astype(F32) for i in range(n_dp)]
-    count = talls[0].shape[0] // 2
-    left = jnp.concatenate([t[:count] for t in talls], axis=0)
-    right = jnp.concatenate([t[count:] for t in talls], axis=0)
-    return jnp.concatenate([left, right], axis=1)
 
 
 def column_of(row, count):
@@ -293,7 +293,8 @@
     pieces = []
     for row in rows:
         pieces += [row[:, at : at + 128] for at in range(0, row.shape[1], 128)]
-    pieces.append(jnp.zeros((-len(pieces) % 8 or 8, 128), F32))
+    if len(pieces) % 8:
+        pieces.append(jnp.zeros((-len(pieces) % 8, 128), F32))
     return jnp.concatenate(pieces, axis=0)
 
 
@@ -370,7 +371,6 @@
     tok,
     ids,
     prow,
-    drow,
     stm,
     std,
     ar,
@@ -378,27 +378,24 @@
     fq,
     fg,
     fd,
-    wide_b,
-    wide_c,
     load_sem,
     img_sem,
-    tz_s,
+    t_s,
     tz_r,
-    ty_s,
     ty_r,
-    tc_s,
-    tc_r,
-    tx_s,
     tx_r,
-    tf_s,
-    tf_r,
+    tl_r,
     ar_s,
     ar_r,
     g_s,
+    g_r,
     g_f,
-    g_r,
+    g_c,
     f_s,
-    f_r,
+    f_x,
+    f_c,
+    st_s,
+    st_r,
     sm_s,
     sm_r,
 ):
@@ -441,18 +438,12 @@
         image_load(k).start()
     load("iw", iw_hbm, iw)
     load("io", io_hbm, io)
-    load("tw", tw_hbm, tw)
-    load("to", to_hbm, to)
     load("ig2", ig2_hbm, ig2_ref)
     load("ib2", ib2_hbm, ib2_ref)
     load("iub", iub_hbm, iub_ref)
     load("tg2", tg2_hbm, tg2_ref)
     load("tb2", tb2_hbm, tb2_ref)
     load("tub", tub_hbm, tub_ref)
-    load("iu", iu_hbm, iu)
-    load("id", id_hbm, idn)
-    load("tu", tu_hbm, tu)
-    load("td", td_hbm, td)
 
     def vector(name, ref):
         loads[name].wait()
@@ -482,108 +473,107 @@
 
     def mp_send(buf, send, recv):
         for i in range(1, n_mp):
-            remote(
-                buf.at[m], buf.at[m], send.at[i], recv.at[i], (d, lax.rem(m + i, n_mp))
-            ).start()
+            remote(buf.at[m], buf.at[m], send, recv, (d, lax.rem(m + i, n_mp))).start()
 
     def mp_recv(buf, send, recv):
-        for i in range(1, n_mp):
-            slot = buf.at[lax.rem(m + n_mp - i, n_mp)]
-            remote(slot, slot, send.at[i], recv.at[i], partner).wait_recv()
+        slots = buf.at[pl.ds(0, n_mp - 1)]
+        remote(slots, slots, send, recv, partner).wait_recv()
 
     def mp_drain(buf, send, recv):
-        for i in range(1, n_mp):
-            remote(buf.at[m], buf.at[m], send.at[i], recv.at[i], partner).wait_send()
-
-    def far_send(buf, send, recv):
+        slots = buf.at[pl.ds(0, n_mp - 1)]
+        remote(slots, slots, send, recv, partner).wait_send()
+
+    def far_send(buf, at):
         slot = buf.at[m]
-        remote(slot, slot, send.at[2], recv.at[2], across).start()
-        remote(slot, slot, send.at[1], recv.at[1], partner).start()
-
-    def far_pass(buf, send, recv):
+        remote(slot, slot, f_s.at[at], f_x.at[at], across).start()
+        remote(slot, slot, f_s.at[at], f_c.at[at], partner).start()
+
+    def far_pass(buf, at):
         slot = buf.at[lax.rem(m + 2, 4)]
-        remote(slot, slot, send.at[3], recv.at[2], partner).wait_recv()
-        remote(slot, slot, send.at[3], recv.at[3], partner).start()
-
-    def far_recv(buf, send, recv):
-        slot = buf.at[m]
-        for i in (1, 3):
-            remote(slot, slot, send.at[i], recv.at[i], partner).wait_recv()
-
-    def split(mine, body):
-        for k in range(half_dp - 1):
-            body(2 * k + (2 - core if mine else 1 + core))
-
-        @pl.when(core == (1 if mine else 0))
+        remote(slot, slot, f_s.at[at], f_x.at[at], partner).wait_recv()
+        remote(slot, slot, f_s.at[at], f_c.at[at], partner).start()
+
+    def far_recv(buf, at):
+        slots = buf.at[pl.ds(0, 2)]
+        remote(slots, slots, f_s.at[at], f_c.at[at], partner).wait_recv()
+
+    def far_drain(buf, at):
+        slots = buf.at[pl.ds(0, 3)]
+        remote(slots, slots, f_s.at[at], f_c.at[at], partner).wait_send()
+
+    def on_core(which):
+        return pl.when(core == which)
+
+    def dp_send(at):
+        slot = gat.at[at, lo, hi]
+        other = lo + core * (1 - 2 * lo)
+
+        def send(k):
+            to_dev = (lax.rem(hi + k, half_dp) * 2 + other, m)
+            remote(slot, slot, g_s.at[at], g_r.at[at], to_dev).start()
+
+        for k in range(1, half_dp):
+            send(k)
+        on_core(1)(lambda: send(0))
+
+    def dp_forward(at):
+        @on_core(1)
         def _():
-            body(2 * half_dp - 1)
-
-    def dp_slot(buf, i):
-        return buf.at[lax.rem(d + n_dp - i, n_dp)]
-
-    def dp_send(at):
-        buf, send, recv = gat.at[at], g_s.at[at], g_r.at[at]
-
-        def body(i):
-            remote(
-                buf.at[d], buf.at[d], send.at[i], recv.at[i], (lax.rem(d + i, n_dp), m)
-            ).start()
-
-        split(True, body)
-
-    def dp_forward(at):
-        buf, recv, fwd = gat.at[at], g_r.at[at], g_f.at[at]
-
-        def body(i):
-            slot = dp_slot(buf, i)
-            remote(slot, slot, fwd.at[i], recv.at[i], partner).wait_recv()
-            remote(slot, slot, fwd.at[i], recv.at[i], partner).start()
-
-        split(True, body)
+            slots = gat.at[at, 1 - lo]
+            remote(slots, slots, g_f.at[at], g_r.at[at], partner).wait_recv()
+            remote(slots, slots, g_f.at[at], g_c.at[at], partner).start()
+
+        @on_core(0)
+        def _():
+            slots = gat.at[at, 0, pl.ds(0, half_dp - 1)]
+            remote(slots, slots, g_f.at[at], g_r.at[at], partner).wait_recv()
+            for k in range(1, half_dp):
+                slot = gat.at[at, lo, lax.rem(hi + k, half_dp)]
+                remote(slot, slot, g_f.at[at], g_c.at[at], partner).start()
+
+    def dp_wait(at, first, wait):
+        for which in (0, 1):
+
+            @on_core(which)
+            def _(which=which):
+                slots = gat.at[at, 0, pl.ds(0, half_dp - (1 if which == first else 0))]
+                wait(slots)
 
     def dp_recv(at):
-        buf, recv, fwd = gat.at[at], g_r.at[at], g_f.at[at]
-
-        def body(i):
-            slot = dp_slot(buf, i)
-            remote(slot, slot, fwd.at[i], recv.at[i], partner).wait_recv()
-
-        split(False, body)
+        dp_wait(
+            at,
+            1,
+            lambda slots: remote(slots, slots, g_f.at[at], g_c.at[at], partner).wait_recv(),
+        )
 
     def dp_drain(at):
-        buf, send, recv, fwd = gat.at[at], g_s.at[at], g_r.at[at], g_f.at[at]
-
-        def body(i):
-            slot = buf.at[d]
-            remote(slot, slot, send.at[i], recv.at[i], partner).wait_send()
-            remote(slot, slot, fwd.at[i], recv.at[i], partner).wait_send()
-
-        split(True, body)
+        def wait(slots):
+            remote(slots, slots, g_s.at[at], g_c.at[at], partner).wait_send()
+            remote(slots, slots, g_f.at[at], g_c.at[at], partner).wait_send()
+
+        dp_wait(at, 0, wait)
+
+    def gathered(at):
+        talls = [gat[at, i % 2, i // 2].astype(F32) for i in range(n_dp)]
+        left = jnp.concatenate([t[:pairs] for t in talls], axis=0)
+        right = jnp.concatenate([t[pairs:] for t in talls], axis=0)
+        return jnp.concatenate([left, right], axis=1)
 
     def small_send(at, buf):
         @pl.loop(1, n_dp)
         def _(i):
-            remote(
-                buf.at[d],
-                buf.at[d],
-                sm_s.at[at, i],
-                sm_r.at[at, i],
-                (lax.rem(d + i, n_dp), m),
-            ).start()
+            to_dev = (lax.rem(d + i, n_dp), m)
+            remote(buf.at[d], buf.at[d], sm_s.at[at], sm_r.at[at], to_dev).start()
 
     def small_recv(at, buf):
-        @pl.loop(1, n_dp)
-        def _(i):
-            slot = dp_slot(buf, i)
-            remote(slot, slot, sm_s.at[at, i], sm_r.at[at, i], partner).wait_recv()
+        slots = buf.at[pl.ds(0, n_dp - 1)]
+        remote(slots, slots, sm_s.at[at], sm_r.at[at], partner).wait_recv()
 
     def small_drain(at, buf):
-        @pl.loop(1, n_dp)
-        def _(i):
-            remote(buf.at[d], buf.at[d], sm_s.at[at, i], sm_r.at[at, i], partner).wait_send()
-
-    shared = TOKEN_SHARE * tokens // 256
-    kept = tokens - shared
+        slots = buf.at[pl.ds(0, n_dp - 1)]
+        remote(slots, slots, sm_s.at[at], sm_r.at[at], partner).wait_send()
+
+    part_rows = tokens // (2 * TOKEN_PARTS)
 
     def split_hi(mine, body):
         for k in range(half_dp // 2 - 1):
@@ -593,125 +583,115 @@
         def _():
             body(half_dp - 1)
 
-    def split_both(mine, body):
-        def near(i):
-            body(i, lax.rem(hi + half_dp - i, half_dp) * 2 + lo)
-
-        def far(i):
-            body(half_dp + i, lax.rem(hi + half_dp - i, half_dp) * 2 + 1 - lo)
-
-        split_hi(mine, near)
-        split_hi(mine, far)
+    def near_slot(i):
+        return lax.rem(hi + half_dp - i, half_dp) * 2 + lo
+
+    def far_slot(i):
+        return lax.rem(hi + half_dp - i, half_dp) * 2 + 1 - lo
+
+    def split_far(mine, body):
+        split_hi(mine, lambda i: body(half_dp + i, far_slot(i)))
 
         @pl.when(core == (0 if mine else 1))
         def _():
-            far(0)
-
-    def kept_rows(slot):
-        return tok.at[slot, pl.ds(pl.multiple_of(side * shared, 16), kept)]
-
-    def given_rows(slot):
-        return tok.at[slot, pl.ds(pl.multiple_of(side * kept, 16), shared)]
-
-    def taken_rows(slot):
-        return tok.at[slot, pl.ds(pl.multiple_of((1 - side) * kept, 16), shared)]
-
-    def tok_start():
-        rows = kept_rows(d)
+            body(half_dp, far_slot(0))
+
+    def split_near(mine, body):
+        split_hi(mine, lambda i: body(i, near_slot(i)))
+
+    def rows_of(slot, part, which):
+        start = (which * TOKEN_PARTS + part) * part_rows
+        return tok.at[slot, pl.ds(pl.multiple_of(start, 16), part_rows)]
+
+    def tok_push(rows, recv, device):
+        remote(rows, rows, t_s.at[0], recv, device).start()
+
+    def tok_wait(recv, counts):
+        for which in (0, 1):
+            if counts[which]:
+
+                @on_core(which)
+                def _(which=which):
+                    rows = tok.at[0, pl.ds(0, counts[which] * part_rows)]
+                    remote(rows, rows, t_s.at[0], recv, partner).wait_recv()
+
+    quarter = half_dp // 2
+    near_counts = (quarter - 1, quarter)
+    far_counts = (quarter, quarter)
+
+    def tok_start(part):
+        rows = rows_of(d, part, side)
 
         def body(i):
-            to_dev = (lax.rem(hi + i, half_dp) * 2 + lo, m)
-            remote(rows, rows, tz_s.at[i], tz_r.at[i], to_dev).start()
+            tok_push(rows, tz_r.at[part], (lax.rem(hi + i, half_dp) * 2 + lo, m))
 
         split_hi(True, body)
-
-        @pl.when(core == 0)
-        def _():
-            remote(rows, rows, ty_s.at[0], ty_r.at[0], beside).start()
-
-    def tok_second():
-        def body(i):
-            rows = kept_rows(lax.rem(hi + half_dp - i, half_dp) * 2 + lo)
-            remote(rows, rows, tz_s.at[i], tz_r.at[i], partner).wait_recv()
-            remote(rows, rows, ty_s.at[i], ty_r.at[i], beside).start()
-            remote(rows, rows, tc_s.at[i], tc_r.at[i], partner).start()
-
-        split_hi(True, body)
-
-    def tok_third():
-        def body(i):
-            rows = kept_rows(lax.rem(hi + half_dp - i, half_dp) * 2 + 1 - lo)
-            at = half_dp + i
-            remote(rows, rows, ty_s.at[i], ty_r.at[i], partner).wait_recv()
-            remote(rows, rows, tc_s.at[at], tc_r.at[at], partner).start()
-
-        split_hi(True, body)
-
-        @pl.when(core == 0)
-        def _():
-            body(0)
-
-    def tok_near_across():
-        def body(i):
-            rows = given_rows(lax.rem(hi + half_dp - i, half_dp) * 2 + lo)
-            remote(rows, rows, tx_s.at[i], tx_r.at[i], across).start()
-
-        if shared:
-            split_hi(True, body)
-
-    def tok_far_across():
-        def body(i):
-            rows = given_rows(lax.rem(hi + half_dp - i, half_dp) * 2 + 1 - lo)
-            at = half_dp + i
-            remote(rows, rows, tx_s.at[at], tx_r.at[at], across).start()
-
-        if shared:
-            split_hi(True, body)
-
-            @pl.when(core == 0)
-            def _():
-                body(0)
-
-    def tok_pass():
-        def body(at, slot):
-            rows = taken_rows(slot)
-            remote(rows, rows, tx_s.at[at], tx_r.at[at], partner).wait_recv()
-            remote(rows, rows, tf_s.at[at], tf_r.at[at], partner).start()
-
-        if shared:
-            split_both(True, body)
+        on_core(0)(lambda: tok_push(rows, ty_r.at[part], beside))
+
+    def tok_second(part):
+        tok_wait(tz_r.at[part], near_counts)
+
+        def body(i, slot):
+            rows = rows_of(slot, part, side)
+            tok_push(rows, ty_r.at[part], beside)
+            tok_push(rows, tl_r.at[0], partner)
+
+        split_near(True, body)
+
+    def tok_third(part):
+        tok_wait(ty_r.at[part], far_counts)
+        split_far(True, lambda at, slot: tok_push(rows_of(slot, part, side), tl_r.at[0], partner))
+
+    def tok_near(part):
+        split_near(
+            True, lambda at, slot: tok_push(rows_of(slot, part, side), tx_r.at[part, 0], across)
+        )
+
+    def tok_far(part):
+        split_far(
+            True, lambda at, slot: tok_push(rows_of(slot, part, side), tx_r.at[part, 1], across)
+        )
+
+    def tok_pass_near(part):
+        tok_wait(tx_r.at[part, 0], near_counts)
+        split_near(
+            True, lambda at, slot: tok_push(rows_of(slot, part, 1 - side), tl_r.at[0], partner)
+        )
+
+    def tok_pass_far(part):
+        tok_wait(tx_r.at[part, 1], far_counts)
+        split_far(
+            True, lambda at, slot: tok_push(rows_of(slot, part, 1 - side), tl_r.at[0], partner)
+        )
 
     def tok_last():
-        def body(at, slot):
-            rows = kept_rows(slot)
-            remote(rows, rows, tc_s.at[at], tc_r.at[at], partner).wait_recv()
-            if shared:
-                rows = taken_rows(slot)
-                remote(rows, rows, tf_s.at[at], tf_r.at[at], partner).wait_recv()
-
-        split_both(False, body)
+        for which, count in ((0, 2 * quarter), (1, 2 * quarter - 1)):
+
+            @on_core(which)
+            def _(count=count):
+                slots = tok.at[pl.ds(0, count)]
+                remote(slots, slots, t_s.at[0], tl_r.at[0], partner).wait_recv()
 
     def tok_drain():
-        rows = kept_rows(d)
-
-        def body(at, slot):
-            remote(rows, rows, tc_s.at[at], tc_r.at[at], partner).wait_send()
-            if shared:
-                few = taken_rows(d)
-                remote(few, few, tx_s.at[at], tx_r.at[at], partner).wait_send()
-                remote(few, few, tf_s.at[at], tf_r.at[at], partner).wait_send()
-
-        split_both(True, body)
-
-        def both(i):
-            remote(rows, rows, tz_s.at[i], tz_r.at[i], partner).wait_send()
-            remote(rows, rows, ty_s.at[i], ty_r.at[i], partner).wait_send()
-
-        split_hi(True, both)
-
-        @pl.when(core == 0)
-        def _():
-            remote(rows, rows, ty_s.at[0], ty_r.at[0], partner).wait_send()
+        for which, count in ((0, n_dp - 2), (1, n_dp)):
+
+            @on_core(which)
+            def _(count=count):
+                slots = tok.at[pl.ds(0, count)]
+                remote(slots, slots, t_s.at[0], tl_r.at[0], partner).wait_send()
+
+    def token_steps(at):
+        steps = {
+            "start": tok_start,
+            "second": tok_second,
+            "third": tok_third,
+            "near": tok_near,
+            "far": tok_far,
+            "pass": tok_pass_near,
+            "last": tok_pass_far,
+        }
+        for name, part in STEPS.get(at, ()):
+            steps[name](part)
 
     def attend_rows(queries, normed, allowed, weights):
         stacked = head_blocks(queries.astype(F32), width).astype(BF16)
@@ -727,11 +707,10 @@
     hat_one, factor_one = normalized(xt[...].astype(F32))
     tok[d] = (hat_one * gain_one + vector("tb1", tb1_ref)).astype(BF16)
     seg = vector("seg", seg_ref)
-    ids[d, 0:1, :] = seg
-    ids[d, 1:2, 0:pairs] = vector("lab", lab_ref)
-    pl.semaphore_wait(barrier, n_mp - 1 + n_dp - 1)
-    tok_start()
-    small_send(0, ids)
+    seg_rows = tokens // 128
+    for i in range(seg_rows):
+        ids[d, i : i + 1, :] = seg[:, i * 128 : (i + 1) * 128]
+    ids[d, seg_rows : seg_rows + 1, 0:pairs] = vector("lab", lab_ref)
 
     gain, shift = vector("ig1", ig1_ref), vector("ib1", ib1_ref)
 
@@ -742,6 +721,12 @@
         hat = normalized(xi[rows, :].astype(F32))[0]
         ni[rows, :] = (hat * gain + shift).astype(BF16)
 
+    load("tw", tw_hbm, tw)
+    load("to", to_hbm, to)
+    load("iu", iu_hbm, iu)
+    load("id", id_hbm, idn)
+    load("tu", tu_hbm, tu)
+    load("td", td_hbm, td)
     firsts = [i * IMG_LEN for i in range(pairs)]
     image_first = jnp.concatenate([xi[r : r + 1, :].astype(F32) for r in firsts], axis=0)
     first_n = (normalized(image_first)[0] * gain + shift).astype(BF16)
@@ -754,7 +739,11 @@
     image_context = attend_rows(image_q, ni[...], inside, iw)[2]
     loads["io"].wait()
     ar[0, m] = to_tall(dot(image_context, io[...]))
+
+    pl.semaphore_wait(barrier, n_mp - 1 + n_dp - 1)
     mp_send(ar.at[0], ar_s.at[0], ar_r.at[0])
+    token_steps(0)
+    small_send(0, ids)
 
     normed = tok[d]
     mine, pick = caption_masks(seg, d * pairs, pairs)
@@ -780,10 +769,8 @@
 
     no_foot = jnp.zeros((8, tokens), F32)
     prob_rows = head_rows(probs)
-    prow[d] = prob_rows
-    small_send(1, prow)
     fq[m] = padded(folded.astype(F32), prob_rows)
-    far_send(fq, f_s.at[0], f_r.at[0])
+    token_steps(1)
 
     def summed(at):
         mp_recv(ar.at[at], ar_s.at[at], ar_r.at[at])
@@ -802,96 +789,96 @@
     loads["id"].wait()
     ar[2, m] = to_tall(dot(image_active, idn[...]))
     mp_send(ar.at[2], ar_s.at[2], ar_r.at[2])
+    token_steps(2)
 
     middle = text_last + summed(1)
-    gat[0, d] = to_tall(middle)
-    dp_send(0)
+    gat[0, lo, hi] = to_tall(middle)
     gain_two, shift_two = vector("tg2", tg2_ref), vector("tb2", tb2_ref)
     hat_two, factor_two = normalized(middle)
     normed_two = (hat_two * gain_two + shift_two).astype(BF16)
     loads["tu"].wait()
     up_shift = vector("tub", tub_ref)
-    active = gelu_parts(dot(normed_two, tu[...]) + up_shift)[0].astype(BF16)
+    active, slope = gelu_parts(dot(normed_two, tu[...]) + up_shift)
     loads["td"].wait()
-    ar[3, m] = to_tall(dot(active, td[...]))
+    ar[3, m] = to_tall(dot(active.astype(BF16), td[...]))
     mp_send(ar.at[3], ar_s.at[3], ar_r.at[3])
-
-    gat[1, d] = to_tall(unit(image_middle + summed(2)))
+    token_steps(3)
+
+    gat[1, lo, hi] = to_tall(unit(image_middle + summed(2)))
     dp_send(1)
-    gat[2, d] = to_tall(middle + summed(3))
+    gat[2, lo, hi] = to_tall(middle + summed(3))
     dp_send(2)
-
-    dp_forward(0)
-    tok_second()
-    tok_near_across()
-    far_pass(fq, f_s.at[0], f_r.at[0])
-    small_recv(0, ids)
-    labels = jnp.concatenate([column_of(ids[i, 1:2, 0:128], pairs) for i in range(n_dp)], axis=0)
-    onehot = (labels == lax.broadcasted_iota(jnp.int32, (total, total), 1)).astype(F32)
-    dp_recv(0)
-    middle_all = from_tall_all(gat.at[0], n_dp)
-    n2_all = (normalized(middle_all)[0] * gain_two + shift_two).astype(BF16)
-    n2_o[...] = n2_all
-    act_all, slope_all = gelu_parts(dot(n2_all, tu[...]) + up_shift)
-    act_o[...] = act_all.astype(BF16)
-    wide_b[...] = slope_all
+    far_send(fq, 0)
+
+    token_steps(4)
     dp_forward(1)
     dp_forward(2)
+    dp_send(0)
+    far_pass(fq, 0)
+    token_steps(5)
     dp_recv(1)
     dp_recv(2)
 
-    image_low = from_tall_all(gat.at[1], n_dp).astype(BF16)
-    pooled = from_tall_all(gat.at[2], n_dp)
-    shrink = lax.rsqrt(jnp.sum(pooled * pooled, axis=-1, keepdims=True) + 1e-06)
-    text_unit = pooled * shrink
-    logits = 64.0 * dot_nt(text_unit.astype(BF16), image_low)
-    row_top = jnp.max(logits, axis=1, keepdims=True)
-    row_lse = row_top + jnp.log(jnp.sum(jnp.exp(logits - row_top), axis=1, keepdims=True))
+    image_low = gathered(1).astype(BF16)
+
+    def embedded(rows):
+        shrink = lax.rsqrt(jnp.sum(rows * rows, axis=-1, keepdims=True) + 1e-06)
+        text_unit = rows * shrink
+        return shrink, text_unit, 64.0 * dot_nt(text_unit.astype(BF16), image_low)
+
+    def final_grad(shrink, text_unit, logits, labels):
+        lanes = lax.broadcasted_iota(jnp.int32, logits.shape, 1)
+        onehot = (labels == lanes).astype(F32)
+        top = jnp.max(logits, axis=1, keepdims=True)
+        lse = top + jnp.log(jnp.sum(jnp.exp(logits - top), axis=1, keepdims=True))
+        grads = 0.5 * (jnp.exp(logits - lse) + jnp.exp(logits - col_lse)) - onehot
+        grads = 64.0 * dot(grads.astype(BF16), image_low)
+        along = jnp.sum(text_unit * grads, axis=-1, keepdims=True)
+        positive = jnp.sum(logits * onehot, axis=1, keepdims=True)
+        return shrink * (grads - text_unit * along), lse, positive
+
+    shrink_all, unit_all, logits = embedded(gathered(2))
     col_top = jnp.max(logits, axis=0, keepdims=True)
     col_lse = col_top + jnp.log(jnp.sum(jnp.exp(logits - col_top), axis=0, keepdims=True))
-    grad_logits = 0.5 * (jnp.exp(logits - row_lse) + jnp.exp(logits - col_lse)) - onehot
-    grad_embed = 64.0 * dot(grad_logits.astype(BF16), image_low)
-    along = jnp.sum(text_unit * grad_embed, axis=-1, keepdims=True)
-    grad_final = shrink * (grad_embed - text_unit * along)
-    final_low = grad_final.astype(BF16)
-    fin_o[...] = final_low
-    wide_c[...] = grad_final
-    grad_hidden = dot_nt(final_low, td[...]) * wide_b[...]
-    gh_o[...] = grad_hidden.astype(BF16)
-    wide_b[...] = grad_hidden
-    own = pl.ds(pl.multiple_of(d * pairs, 8), pairs)
-    ar[4, m] = to_tall(dot_nt(wide_b[own, :].astype(BF16), tu[...]))
+    own_labels = column_of(ids[d, seg_rows : seg_rows + 1, :], pairs)
+    grad_final, own_lse, positive = final_grad(*embedded(from_tall(gat[2, lo, hi])), own_labels)
+    grad_hidden = (dot_nt(grad_final.astype(BF16), td[...]) * slope).astype(BF16)
+    ar[4, m] = to_tall(dot_nt(grad_hidden, tu[...]))
     mp_send(ar.at[4], ar_s.at[4], ar_r.at[4])
 
-    tok_third()
-    tok_far_across()
-    positive = jnp.sum(logits * onehot, axis=1, keepdims=True)
-    pair_loss = 0.5 * (row_lse + column_of(col_lse, total)) - positive
-    shape = (total, loss_o.shape[1])
-    spot = lax.broadcasted_iota(jnp.int32, shape, 1)
-    here = lax.broadcasted_iota(jnp.int32, shape, 0) == d * pairs + spot
-    loss_o[...] = jnp.sum(jnp.where(here, pair_loss, 0.0), axis=0, keepdims=True)
-    up_bias = jnp.sum(gh_o[...].astype(F32), axis=0, keepdims=True)
+    token_steps(6)
+    lanes = lax.broadcasted_iota(jnp.int32, (pairs, total), 1)
+    mine_first = lax.broadcasted_iota(jnp.int32, (pairs, total), 0) + d * pairs
+    own_col = jnp.sum(jnp.where(lanes == mine_first, col_lse, 0.0), axis=1, keepdims=True)
+    pair_loss = 0.5 * (own_lse + own_col) - positive
+    shape = (pairs, loss_o.shape[1])
+    diagonal = lax.broadcasted_iota(jnp.int32, shape, 0) == lax.broadcasted_iota(
+        jnp.int32, shape, 1
+    )
+    loss_o[...] = jnp.sum(jnp.where(diagonal, pair_loss, 0.0), axis=0, keepdims=True)
+    small_recv(0, ids)
+    labels = jnp.concatenate(
+        [column_of(ids[i, seg_rows : seg_rows + 1, :], pairs) for i in range(n_dp)], axis=0
+    )
+    fin_o[...] = final_grad(shrink_all, unit_all, logits, labels)[0].astype(BF16)
+    dp_forward(0)
 
     grad_n2 = summed(4)
-    grad_middle = wide_c[own, :] + norm_back(grad_n2, hat_two, factor_two, gain_two)
-    gat[3, d] = to_tall(grad_middle)
+    grad_middle = grad_final + norm_back(grad_n2, hat_two, factor_two, gain_two)
+    gat[3, lo, hi] = to_tall(grad_middle)
     dp_send(3)
     middle_low = grad_middle.astype(BF16)
     grad_context = dot_nt(middle_low, to[...]).astype(BF16)
     grad_folded = dot(head_blocks(grad_context.astype(F32), width).astype(BF16), tw[2])
     fg[m] = padded(grad_folded, no_foot)
-    far_send(fg, f_s.at[1], f_r.at[1])
     grad_probs = dot_nt(grad_folded.astype(BF16), normed)
     grad_scores = probs * (grad_probs - jnp.sum(grad_probs * probs, axis=-1, keepdims=True))
     scaled = grad_scores * scale
     score_rows = head_rows(scaled)
-    drow[d] = score_rows
-    small_send(2, drow)
+    prow[d] = jnp.concatenate([prob_rows[:heads], score_rows[: 8 - heads]], axis=0)
     mixed_back = dot(scaled.astype(BF16), normed).astype(BF16)
     grad_queries = head_pick(dot_nt(mixed_back, tw[1]), width).astype(BF16)
     fd[m] = padded(dot(grad_queries, tw[0]), score_rows)
-    far_send(fd, f_s.at[2], f_r.at[2])
 
     def spread(slots, ref, at):
         parts = []
@@ -916,84 +903,87 @@
     stm[m] = stats_pack(
         [jnp.sum(part * hat_one, axis=0, keepdims=True), jnp.sum(part, axis=0, keepdims=True)]
     )
-    mp_send(stm, f_s.at[3], f_r.at[3])
+    mp_send(stm, st_s.at[0], st_r.at[0])
+    far_send(fg, 1)
+    far_send(fd, 2)
+    small_send(1, prow)
     stats_two = [
         jnp.sum(grad_n2 * hat_two, axis=0, keepdims=True),
         jnp.sum(grad_n2, axis=0, keepdims=True),
     ]
 
-    tok_pass()
+    token_steps(7)
+    dp_recv(0)
+    n2_all = (normalized(gathered(0))[0] * gain_two + shift_two).astype(BF16)
+    n2_o[...] = n2_all
+    act_all, slope_all = gelu_parts(dot(n2_all, tu[...]) + up_shift)
+    act_o[...] = act_all.astype(BF16)
+    gh_o[...] = (dot_nt(fin_o[...], td[...]) * slope_all).astype(BF16)
+    up_bias = jnp.sum(gh_o[...].astype(F32), axis=0, keepdims=True)
+    mp_recv(stm, st_s.at[0], st_r.at[0])
+    one = stm[0]
+    for i in range(1, n_mp):
+        one = one + stm[i]
+    std[d] = stats_pack(stats_unpack(one, 2, features) + stats_two)
+    small_send(2, std)
+    dp_forward(3)
+    far_pass(fg, 1)
+    far_pass(fd, 2)
+    token_steps(8)
+
+    for at, buf in ((0, fq), (1, fg), (2, fd)):
+        far_recv(buf, at)
+    flat = [ref[...].reshape(n_mp * ref.shape[1], features) for ref in (fq, fg, fd)]
+    grad_normed = first_norm_grad(list(range(n_mp)), flat)
+    text_grad = norm_back(grad_normed, hat_one, factor_one, gain_one)
+    tg_o[...] = text_grad + dot_tn(pick, middle_low)
+
     small_recv(1, prow)
     tok_last()
     twice = 2 * pairs
-
-    def pair_of(j, rows_ref):
-        seg = jnp.concatenate([ids[2 * j, 0:1, :], ids[2 * j + 1, 0:1, :]], axis=1)
+    for j in range(half_dp):
+        seg = jnp.concatenate(
+            [ids[i, k : k + 1, :] for i in (2 * j, 2 * j + 1) for k in range(seg_rows)], axis=1
+        )
         here, picks = caption_masks(seg, j * twice, twice)
-        values = jnp.concatenate([rows_ref[2 * j], rows_ref[2 * j + 1]], axis=1)
+        values = jnp.concatenate([prow[2 * j], prow[2 * j + 1]], axis=1)
         parts = [jnp.where(here, values[h : h + 1], 0.0) for h in range(heads)]
+        parts += [jnp.where(here, values[heads + h : heads + h + 1], 0.0) for h in range(heads)]
+        parts = [part.astype(BF16) for part in parts] + [picks]
         low = tok[2 * j : 2 * j + 2].reshape(2 * tokens, features)
-        return jnp.concatenate(parts, axis=0).astype(BF16), picks, low
-
-    for j in range(half_dp):
-        values, picks, low = pair_of(j, prow)
+        mixed = dot(jnp.concatenate(parts, axis=0), low).astype(BF16)
         rows = slice(j * twice, (j + 1) * twice)
-        mixed = dot(values, low).astype(BF16)
         for h in range(heads):
             xv_o[h, rows, :] = mixed[h * twice : (h + 1) * twice]
-        nsel_o[rows, :] = dot(picks, low).astype(BF16)
-
-    far_pass(fg, f_s.at[1], f_r.at[1])
-    far_pass(fd, f_s.at[2], f_r.at[2])
-    dp_forward(3)
-    mp_recv(stm, f_s.at[3], f_r.at[3])
-    own_stats = stm[0]
-    for i in range(1, n_mp):
-        own_stats = own_stats + stm[i]
-    std[d] = stats_pack(stats_unpack(own_stats, 2, features) + stats_two)
-    small_send(3, std)
+            xk_o[h, rows, :] = mixed[(heads + h) * twice : (heads + h + 1) * twice]
+        nsel_o[rows, :] = mixed[2 * heads * twice :]
     q_o[...] = dot_nt(nsel_o[...], tw[0]).astype(BF16)
     ctx_o[...] = head_pick(
         dot_nt(xv_o[...].reshape(heads * total, features), tw[2]), width
     ).astype(BF16)
-
-    small_recv(2, drow)
-    for j in range(half_dp):
-        values, picks, low = pair_of(j, drow)
-        rows = slice(j * twice, (j + 1) * twice)
-        mixed = dot(values, low).astype(BF16)
-        for h in range(heads):
-            xk_o[h, rows, :] = mixed[h * twice : (h + 1) * twice]
     dq_o[...] = head_pick(
         dot_nt(xk_o[...].reshape(heads * total, features), tw[1]), width
     ).astype(BF16)
     dp_recv(3)
-    mid_all = from_tall_all(gat.at[3], n_dp).astype(BF16)
+    mid_all = gathered(3).astype(BF16)
     mid_o[...] = mid_all
     gctx_o[...] = dot_nt(mid_all, to[...]).astype(BF16)
 
-    for at, buf in ((0, fq), (1, fg), (2, fd)):
-        far_recv(buf, f_s.at[at], f_r.at[at])
-    flat = [ref[...].reshape(n_mp * ref.shape[1], features) for ref in (fq, fg, fd)]
-    grad_normed = first_norm_grad(list(range(n_mp)), flat)
-    text_grad = norm_back(grad_normed, hat_one, factor_one, gain_one)
-    tg_o[...] = text_grad + dot_tn(pick, middle_low)
-
-    small_recv(3, std)
+    small_recv(2, std)
     stats = std[0]
     for i in range(1, n_dp):
         stats = stats + std[i]
-    vec_o[...] = jnp.concatenate(
-        stats_unpack(stats, 4, features) + [up_bias, jnp.zeros((3, features), F32)], axis=0
-    )
+    rows = stats_unpack(stats, 4, features)
+    vec_o[...] = jnp.concatenate(rows + [up_bias, jnp.zeros((3, features), F32)], axis=0)
 
     for at in range(ar.shape[0]):
         mp_drain(ar.at[at], ar_s.at[at], ar_r.at[at])
-    for at, buf in enumerate((fq, fg, fd, stm)):
-        mp_drain(buf, f_s.at[at], f_r.at[at])
+    mp_drain(stm, st_s.at[0], st_r.at[0])
+    for at, buf in enumerate((fq, fg, fd)):
+        far_drain(buf, at)
     for at in range(gat.shape[0]):
         dp_drain(at)
-    for at, buf in enumerate((ids, prow, drow, std)):
+    for at, buf in enumerate((ids, prow, std)):
         small_drain(at, buf)
     tok_drain()
 
@@ -1171,33 +1161,35 @@
         + [vmem(array.shape, array.dtype) for array in vectors]
         + [
             vmem((n_dp, tokens, features), BF16),
-            vmem((n_dp, 8, tokens), jnp.int32),
-            vmem((n_dp, 8, tokens), F32),
+            vmem((n_dp, 8, 128), jnp.int32),
             vmem((n_dp, 8, tokens), F32),
             vmem((n_mp, 16, 128), F32),
-            vmem((n_dp, 32, 128), F32),
+            vmem((n_dp, 24, 128), F32),
             vmem((5, n_mp) + tall, BF16),
-            vmem((4, n_dp) + tall, BF16),
+            vmem((4, 2, half_dp) + tall, BF16),
             vmem((n_mp, fold_rows, features), BF16),
             vmem((n_mp, fold_rows, features), BF16),
             vmem((n_mp, pairs + 8, features), BF16),
-            vmem((total, hidden), F32),
-            vmem((total, features), F32),
             sems(22),
             sems(5),
-        ]
-        + [sems(half_dp)] * 4
-        + [sems(n_dp)] * 6
-        + [
-            sems(5, n_mp),
-            sems(5, n_mp),
-            sems(4, n_dp),
-            sems(4, n_dp),
-            sems(4, n_dp),
-            sems(4, n_mp),
-            sems(4, n_mp),
-            sems(4, n_dp),
-            sems(4, n_dp),
+            sems(1),
+            sems(TOKEN_PARTS),
+            sems(TOKEN_PARTS),
+            sems(TOKEN_PARTS, 2),
+            sems(1),
+            sems(5),
+            sems(5),
+            sems(4),
+            sems(4),
+            sems(4),
+            sems(4),
+            sems(3),
+            sems(3),
+            sems(3),
+            sems(1),
+            sems(1),
+            sems(3),
+            sems(3),
         ],
         compiler_params=pltpu.CompilerParams(
             collective_id=0, has_side_effects=True, vmem_limit_bytes=48 * 2**20

time: 62.7 us -> 50.8 us (0.81)
  Pallas kernels: 61.8 us -> 49.7 us
    pallas_call x1, Pallas kernels: 57.7 us -> 45.6 us  [kernel_device(): pl.pallas_call(functools.partial(step_kernel, (n_dp, n_mp, pairs, tokens,...]
where the time goes in v4:
time: 50.8 us; the launch traced here: 50.3 us
  Pallas kernels  49.7 us (98%)
  between operations  0.66 us (1%)
    pallas_call x1, Pallas kernels, kernel_device(): pl.pallas_call(functools.partial(step_kernel, (n_dp, n_mp, pairs, tokens,...  45.6 us
    pallas_call x1, Pallas kernels, kernel_device(): pl.pallas_call(weights_kernel, out_shape=[jax.ShapeDtypeStruct((tokens, f...  4.1 us

profile of v4, /device:TPU:0, one launch (start us, length us, event | category | flops | bytes accessed | tf_op | source)
XLA Modules:
  0.0 50.3 jit_solution(17450962442305499738)
XLA Ops:
  0.7 45.6 %step.1 = (bf16[192,768]{1,0:T(8,128)(2,1)S(1)}, bf16[192,768]{1,0:T(8,128)(2,1)S(1)}, bf16[192,768]{1,0:T(8,128)(2,1)S(1)}, bf16[192,768]{1,0:T(8,128)(2,1)S(1)...) custom-call(bf16[256,768]{1,0:T(8,128)(2,1)} %text_hbm.1, ...), custom_call_target="tpu_custom_call" | custom-call | tf_op jit(solution)/shard_map/step/pallas_call | solution.py:1143
  46.2 4.1 %weights.1 = (f32[256,768]{1,0:T(8,128)}, f32[3,192,768]{2,1,0:T(8,128)}, f32[192,768]{1,0:T(8,128)}, f32[768,768]{1,0:T(8,128)}, f32[768,768]{1,0:T(8,128)}, /*...) custom-call(bf16[192,768]{1,0:T(8,128)(2,1)S(1)} %get-tuple-element.37.a, ...), custom_call_target="tpu_custom_call" | custom-call | tf_op jit(solution)/shard_map/weights/pallas_call | solution.py:1200

commit v5 on v4

--- a/solution.py
+++ b/solution.py
@@ -248,11 +248,12 @@
 
 MESH = pl.DeviceIdType.MESH
 TOKEN_PARTS = 2
+SHIP_PARTS = 4
 STEPS = {
     0: (("start", 0), ("start", 1)),
     3: (("second", 0), ("near", 0)),
     4: (("second", 1), ("near", 1)),
-    5: (("third", 0), ("far", 0), ("pass", 0)),
+    9: (("third", 0), ("far", 0), ("pass", 0)),
     6: (("third", 1), ("far", 1), ("pass", 1)),
     8: (("last", 0), ("last", 1)),
 }
@@ -330,16 +331,12 @@
     tg2_hbm,
     tb2_hbm,
     tub_hbm,
-    act_o,
-    fin_o,
-    n2_o,
-    gh_o,
-    ctx_o,
+    up_o,
+    down_o,
+    tw,
+    to,
     mid_o,
     nsel_o,
-    dq_o,
-    q_o,
-    gctx_o,
     xk_o,
     xv_o,
     tg_o,
@@ -347,13 +344,10 @@
     loss_o,
     xt,
     xi,
-    ni,
     iw,
     io,
     iu,
     idn,
-    tw,
-    to,
     tu,
     td,
     seg_ref,
@@ -427,39 +421,46 @@
         loads[name] = pltpu.make_async_copy(src, dst, load_sem.at[len(loads)])
         loads[name].start()
 
+    for k in range(chunk):
+        image_load(k).start()
+    load("ig1", ig1_hbm, ig1_ref)
+    load("ib1", ib1_hbm, ib1_ref)
+    load("iw", iw_hbm, iw)
+    load("io", io_hbm, io)
+
+    def vector(name, ref):
+        loads[name].wait()
+        return ref[...].reshape(1, ref.shape[0])
+
+    barrier = pltpu.get_barrier_semaphore()
+    for i in range(1, n_mp):
+        pl.semaphore_signal(
+            barrier, inc=1, device_id=(d, lax.rem(m + i, n_mp)), device_id_type=MESH
+        )
+
+    @pl.loop(1, n_dp)
+    def _(i):
+        pl.semaphore_signal(
+            barrier, inc=1, device_id=(lax.rem(d + i, n_dp), m), device_id_type=MESH
+        )
+
     load("text", text_hbm, xt)
     load("tg1", tg1_hbm, tg1_ref)
     load("tb1", tb1_hbm, tb1_ref)
     load("seg", seg_hbm, seg_ref)
     load("lab", lab_hbm, lab_ref)
-    load("ig1", ig1_hbm, ig1_ref)
-    load("ib1", ib1_hbm, ib1_ref)
-    for k in range(chunk):
-        image_load(k).start()
-    load("iw", iw_hbm, iw)
-    load("io", io_hbm, io)
+    load("tw", tw_hbm, tw)
+    load("to", to_hbm, to)
     load("ig2", ig2_hbm, ig2_ref)
     load("ib2", ib2_hbm, ib2_ref)
     load("iub", iub_hbm, iub_ref)
+    load("iu", iu_hbm, iu)
+    load("id", id_hbm, idn)
     load("tg2", tg2_hbm, tg2_ref)
     load("tb2", tb2_hbm, tb2_ref)
     load("tub", tub_hbm, tub_ref)
-
-    def vector(name, ref):
-        loads[name].wait()
-        return ref[...].reshape(1, ref.shape[0])
-
-    barrier = pltpu.get_barrier_semaphore()
-    for i in range(1, n_mp):
-        pl.semaphore_signal(
-            barrier, inc=1, device_id=(d, lax.rem(m + i, n_mp)), device_id_type=MESH
-        )
-
-    @pl.loop(1, n_dp)
-    def _(i):
-        pl.semaphore_signal(
-            barrier, inc=1, device_id=(lax.rem(d + i, n_dp), m), device_id_type=MESH
-        )
+    load("tu", tu_hbm, tu)
+    load("td", td_hbm, td)
 
     def remote(src, dst, send, recv, device):
         return pltpu.make_async_remote_copy(
@@ -702,47 +703,48 @@
         context = head_pick(dot_nt(mixed, weights[2]), width).astype(BF16)
         return folded, probs, context
 
+    for k in range(chunk):
+        image_load(k).wait()
+    gain, shift = vector("ig1", ig1_ref), vector("ib1", ib1_ref)
+    firsts = [i * IMG_LEN for i in range(pairs)]
+    image_first = jnp.concatenate([xi[r : r + 1, :].astype(F32) for r in firsts], axis=0)
+    first_n = (normalized(image_first)[0] * gain + shift).astype(BF16)
+    loads["iw"].wait()
+    image_q = dot_nt(first_n, iw[0])
+    image_fold = dot(head_blocks(image_q, width).astype(BF16), iw[1])
+    group = pairs // chunk
+    shape = (group, chunk_rows)
+    place = lax.broadcasted_iota(jnp.int32, shape, 1)
+    begin = lax.broadcasted_iota(jnp.int32, shape, 0) * IMG_LEN
+    inside = jnp.concatenate([(place >= begin) & (place < begin + IMG_LEN)] * heads, axis=0)
+    image_mixed = []
+    for k in range(chunk):
+        hat = normalized(xi[k * chunk_rows : (k + 1) * chunk_rows, :].astype(F32))[0]
+        low = (hat * gain + shift).astype(BF16)
+        spots = [h * pairs + k * group for h in range(heads)]
+        asked = jnp.concatenate([image_fold[at : at + group] for at in spots], axis=0)
+        scores = dot_nt(asked.astype(BF16), low) * scale
+        image_mixed.append(dot(softmax_rows(scores, inside).astype(BF16), low))
+    image_mixed = jnp.concatenate(
+        [mixed[h * group : (h + 1) * group] for h in range(heads) for mixed in image_mixed], axis=0
+    )
+    image_context = head_pick(dot_nt(image_mixed.astype(BF16), iw[2]), width).astype(BF16)
+    loads["io"].wait()
+    ar[0, m] = to_tall(dot(image_context, io[...]))
+
+    pl.semaphore_wait(barrier, n_mp - 1 + n_dp - 1)
+    mp_send(ar.at[0], ar_s.at[0], ar_r.at[0])
+
     loads["text"].wait()
     gain_one = vector("tg1", tg1_ref)
     hat_one, factor_one = normalized(xt[...].astype(F32))
     tok[d] = (hat_one * gain_one + vector("tb1", tb1_ref)).astype(BF16)
+    token_steps(0)
     seg = vector("seg", seg_ref)
     seg_rows = tokens // 128
     for i in range(seg_rows):
         ids[d, i : i + 1, :] = seg[:, i * 128 : (i + 1) * 128]
     ids[d, seg_rows : seg_rows + 1, 0:pairs] = vector("lab", lab_ref)
-
-    gain, shift = vector("ig1", ig1_ref), vector("ib1", ib1_ref)
-
-    @pl.loop(0, chunk)
-    def _(k):
-        image_load(k).wait()
-        rows = pl.ds(pl.multiple_of(k * chunk_rows, 16), chunk_rows)
-        hat = normalized(xi[rows, :].astype(F32))[0]
-        ni[rows, :] = (hat * gain + shift).astype(BF16)
-
-    load("tw", tw_hbm, tw)
-    load("to", to_hbm, to)
-    load("iu", iu_hbm, iu)
-    load("id", id_hbm, idn)
-    load("tu", tu_hbm, tu)
-    load("td", td_hbm, td)
-    firsts = [i * IMG_LEN for i in range(pairs)]
-    image_first = jnp.concatenate([xi[r : r + 1, :].astype(F32) for r in firsts], axis=0)
-    first_n = (normalized(image_first)[0] * gain + shift).astype(BF16)
-    loads["iw"].wait()
-    image_q = dot_nt(first_n, iw[0]).astype(BF16)
-    shape = (pairs, xi.shape[0])
-    place = lax.broadcasted_iota(jnp.int32, shape, 1)
-    begin = lax.broadcasted_iota(jnp.int32, shape, 0) * IMG_LEN
-    inside = jnp.concatenate([(place >= begin) & (place < begin + IMG_LEN)] * heads, axis=0)
-    image_context = attend_rows(image_q, ni[...], inside, iw)[2]
-    loads["io"].wait()
-    ar[0, m] = to_tall(dot(image_context, io[...]))
-
-    pl.semaphore_wait(barrier, n_mp - 1 + n_dp - 1)
-    mp_send(ar.at[0], ar_s.at[0], ar_r.at[0])
-    token_steps(0)
     small_send(0, ids)
 
     normed = tok[d]
@@ -812,6 +814,7 @@
 
     token_steps(4)
     dp_forward(1)
+    token_steps(9)
     dp_forward(2)
     dp_send(0)
     far_pass(fq, 0)
@@ -860,7 +863,7 @@
     labels = jnp.concatenate(
         [column_of(ids[i, seg_rows : seg_rows + 1, :], pairs) for i in range(n_dp)], axis=0
     )
-    fin_o[...] = final_grad(shrink_all, unit_all, logits, labels)[0].astype(BF16)
+    fin_all = final_grad(shrink_all, unit_all, logits, labels)[0].astype(BF16)
     dp_forward(0)
 
     grad_n2 = summed(4)
@@ -915,11 +918,9 @@
     token_steps(7)
     dp_recv(0)
     n2_all = (normalized(gathered(0))[0] * gain_two + shift_two).astype(BF16)
-    n2_o[...] = n2_all
     act_all, slope_all = gelu_parts(dot(n2_all, tu[...]) + up_shift)
-    act_o[...] = act_all.astype(BF16)
-    gh_o[...] = (dot_nt(fin_o[...], td[...]) * slope_all).astype(BF16)
-    up_bias = jnp.sum(gh_o[...].astype(F32), axis=0, keepdims=True)
+    gh_all = (dot_nt(fin_all, td[...]) * slope_all).astype(BF16)
+    up_bias = jnp.sum(gh_all.astype(F32), axis=0, keepdims=True)
     mp_recv(stm, st_s.at[0], st_r.at[0])
     one = stm[0]
     for i in range(1, n_mp):
@@ -930,6 +931,8 @@
     far_pass(fg, 1)
     far_pass(fd, 2)
     token_steps(8)
+    up_o[...] = dot_tn(n2_all, gh_all)
+    down_o[...] = dot_tn(act_all.astype(BF16), fin_all)
 
     for at, buf in ((0, fq), (1, fg), (2, fd)):
         far_recv(buf, at)
@@ -957,17 +960,8 @@
             xv_o[h, rows, :] = mixed[h * twice : (h + 1) * twice]
             xk_o[h, rows, :] = mixed[(heads + h) * twice : (heads + h + 1) * twice]
         nsel_o[rows, :] = mixed[2 * heads * twice :]
-    q_o[...] = dot_nt(nsel_o[...], tw[0]).astype(BF16)
-    ctx_o[...] = head_pick(
-        dot_nt(xv_o[...].reshape(heads * total, features), tw[2]), width
-    ).astype(BF16)
-    dq_o[...] = head_pick(
-        dot_nt(xk_o[...].reshape(heads * total, features), tw[1]), width
-    ).astype(BF16)
     dp_recv(3)
-    mid_all = gathered(3).astype(BF16)
-    mid_o[...] = mid_all
-    gctx_o[...] = dot_nt(mid_all, to[...]).astype(BF16)
+    mid_o[...] = gathered(3).astype(BF16)
 
     small_recv(2, std)
     stats = std[0]
@@ -989,16 +983,12 @@
 
 
 def weights_kernel(
-    act,
-    fin,
-    n2,
-    gh,
-    ctx,
+    up,
+    down,
+    tw,
+    to,
     mid,
     nsel,
-    dq,
-    q,
-    gctx,
     xk,
     xv,
     tg,
@@ -1017,12 +1007,10 @@
     ub_out,
     qkv_buf,
     out_buf,
-    up_buf,
-    down_buf,
     sem,
 ):
     heads, total, features = xk.shape
-    width = q.shape[1]
+    width = to.shape[0]
     started = []
 
     def ship(src, dst):
@@ -1030,24 +1018,26 @@
         copy.start()
         started.append(copy)
 
+    for src, dst in ((up, up_out), (down, down_out)):
+        step = src.shape[0] // SHIP_PARTS
+        for at in range(0, src.shape[0], step):
+            rows = pl.ds(at, step)
+            ship(src.at[rows], dst.at[rows])
     ship(tg, tg_out)
-    step = 256
-    for left, right, buf, dst in (
-        (act, fin, down_buf, down_out),
-        (n2, gh, up_buf, up_out),
-    ):
-        for at in range(0, features, step):
-            rows = pl.ds(at, step)
-            buf[rows, :] = dot_tn(left[:, at : at + step], right[...])
-            ship(buf.at[rows], dst.at[rows])
-    out_buf[...] = dot_tn(ctx[...], mid[...])
+    flat_k = xk[...].reshape(heads * total, features)
+    flat_v = xv[...].reshape(heads * total, features)
+    queries = dot_nt(nsel[...], tw[0])
+    grad_context = dot_nt(mid[...], to[...])
+    for at, rows, flat in ((1, queries, flat_k), (2, grad_context, flat_v)):
+        stacked = head_blocks(rows.astype(BF16).astype(F32), width).astype(BF16)
+        qkv_buf[at] = dot_tn(stacked, flat)
+        ship(qkv_buf.at[at], qkv_out.at[at])
+    grad_queries = head_pick(dot_nt(flat_k, tw[1]), width).astype(BF16)
+    qkv_buf[0] = dot_tn(grad_queries, nsel[...])
+    ship(qkv_buf.at[0], qkv_out.at[0])
+    context = head_pick(dot_nt(flat_v, tw[2]), width).astype(BF16)
+    out_buf[...] = dot_tn(context, mid[...])
     ship(out_buf, out_out)
-    qkv_buf[0] = dot_tn(dq[...], nsel[...])
-    ship(qkv_buf.at[0], qkv_out.at[0])
-    for at, rows, blocks in ((1, q, xk), (2, gctx, xv)):
-        stacked = head_blocks(rows[...].astype(F32), width).astype(BF16)
-        qkv_buf[at] = dot_tn(stacked, blocks[...].reshape(heads * total, features))
-        ship(qkv_buf.at[at], qkv_out.at[at])
     for at, dst in enumerate((g1_out, b1_out, g2_out, b2_out, ub_out)):
         dst[...] = vec[at, :]
     loss_out[...] = loss[0, 0 : loss_out.shape[0]]
@@ -1096,16 +1086,12 @@
         return pltpu.SemaphoreType.DMA(shape)
 
     outs = [
-        ((total, hidden), BF16),
+        ((features, hidden), F32),
+        ((hidden, features), F32),
+        ((3, width, features), BF16),
+        ((width, features), BF16),
         ((total, features), BF16),
         ((total, features), BF16),
-        ((total, hidden), BF16),
-        ((total, width), BF16),
-        ((total, features), BF16),
-        ((total, features), BF16),
-        ((total, width), BF16),
-        ((total, width), BF16),
-        ((total, width), BF16),
         ((heads, total, features), BF16),
         ((heads, total, features), BF16),
         ((tokens, features), F32),
@@ -1148,13 +1134,10 @@
         scratch_shapes=[
             vmem(text_tokens.shape, BF16),
             vmem(image_tokens.shape, BF16),
-            vmem(image_tokens.shape, BF16),
             vmem((3, width, features), BF16),
             vmem(image_out.shape, BF16),
             vmem(image_up.shape, BF16),
             vmem(image_down.shape, BF16),
-            vmem((3, width, features), BF16),
-            vmem(text_out.shape, BF16),
             vmem(text_up.shape, BF16),
             vmem(text_down.shape, BF16),
         ]
@@ -1171,7 +1154,7 @@
             vmem((n_mp, fold_rows, features), BF16),
             vmem((n_mp, pairs + 8, features), BF16),
             sems(22),
-            sems(5),
+            sems(pairs // 8),
             sems(1),
             sems(TOKEN_PARTS),
             sems(TOKEN_PARTS),
@@ -1217,9 +1200,7 @@
         scratch_shapes=[
             vmem((3, width, features), F32),
             vmem((width, features), F32),
-            vmem((features, hidden), F32),
-            vmem((hidden, features), F32),
-            sems(16),
+            sems(2 * SHIP_PARTS + 5),
         ],
         compiler_params=pltpu.CompilerParams(vmem_limit_bytes=32 * 2**20),
         name="weights",

time: 50.8 us -> 48.5 us (0.955)
  Pallas kernels: 49.7 us -> 47.7 us
    pallas_call x1, Pallas kernels: 45.6 us -> 43.7 us  [kernel_device(): pl.pallas_call(functools.partial(step_kernel, (n_dp, n_mp, pairs, tokens,...]
where the time goes in v5:
time: 48.5 us; the launch traced here: 48.4 us
  Pallas kernels  47.7 us (98%)
  between operations  0.66 us (1%)
    pallas_call x1, Pallas kernels, kernel_device(): pl.pallas_call(functools.partial(step_kernel, (n_dp, n_mp, pairs, tokens,...  43.7 us
    pallas_call x1, Pallas kernels, kernel_device(): pl.pallas_call(weights_kernel, out_shape=[jax.ShapeDtypeStruct((tokens, f...  4.05 us

profile of v5, /device:TPU:0, one launch (start us, length us, event | category | flops | bytes accessed | tf_op | source)
XLA Modules:
  0.0 48.4 jit_solution(2238714243804416085)
XLA Ops:
  0.7 43.7 %step.1 = (f32[768,768]{1,0:T(8,128)S(1)}, f32[768,768]{1,0:T(8,128)S(1)}, bf16[3,192,768]{2,1,0:T(8,128)(2,1)S(1)}, bf16[192,768]{1,0:T(8,128)(2,1)S(1)}, bf16[...) custom-call(bf16[256,768]{1,0:T(8,128)(2,1)} %text_hbm.1, ...), custom_call_target="tpu_custom_call" | custom-call | tf_op jit(solution)/shard_map/step/pallas_call | solution.py:1129
  44.3 4.0 %weights.1 = (f32[256,768]{1,0:T(8,128)}, f32[3,192,768]{2,1,0:T(8,128)}, f32[192,768]{1,0:T(8,128)}, f32[768,768]{1,0:T(8,128)}, f32[768,768]{1,0:T(8,128)}, /*...) custom-call(f32[768,768]{1,0:T(8,128)S(1)} %get-tuple-element.33.up, ...), custom_call_target="tpu_custom_call" | custom-call | tf_op jit(solution)/shard_map/weights/pallas_call | solution.py:1183

commit v6 on v5

--- a/solution.py
+++ b/solution.py
@@ -249,10 +249,11 @@
 MESH = pl.DeviceIdType.MESH
 TOKEN_PARTS = 2
 SHIP_PARTS = 4
+FIRST_FOLDS = 2
 STEPS = {
     0: (("start", 0), ("start", 1)),
-    3: (("second", 0), ("near", 0)),
-    4: (("second", 1), ("near", 1)),
+    3: (("second", 0), ("near", 0), ("own", 0)),
+    4: (("second", 1), ("near", 1), ("own", 1)),
     9: (("third", 0), ("far", 0), ("pass", 0)),
     6: (("third", 1), ("far", 1), ("pass", 1)),
     8: (("last", 0), ("last", 1)),
@@ -290,12 +291,12 @@
     return expo / jnp.sum(expo, axis=-1, keepdims=True)
 
 
-def stats_pack(rows):
+def stats_pack(rows, multiple=8):
     pieces = []
     for row in rows:
         pieces += [row[:, at : at + 128] for at in range(0, row.shape[1], 128)]
-    if len(pieces) % 8:
-        pieces.append(jnp.zeros((-len(pieces) % 8, 128), F32))
+    if len(pieces) % multiple:
+        pieces.append(jnp.zeros((-len(pieces) % multiple, 128), F32))
     return jnp.concatenate(pieces, axis=0)
 
 
@@ -377,6 +378,7 @@
     t_s,
     tz_r,
     ty_r,
+    to_r,
     tx_r,
     tl_r,
     ar_s,
@@ -484,23 +486,35 @@
         slots = buf.at[pl.ds(0, n_mp - 1)]
         remote(slots, slots, send, recv, partner).wait_send()
 
-    def far_send(buf, at):
-        slot = buf.at[m]
+    def far_send(at):
+        buf, first, rows = far[at]
+        slot = buf.at[m, pl.ds(first, rows)]
         remote(slot, slot, f_s.at[at], f_x.at[at], across).start()
         remote(slot, slot, f_s.at[at], f_c.at[at], partner).start()
 
-    def far_pass(buf, at):
-        slot = buf.at[lax.rem(m + 2, 4)]
+    def far_pass(at):
+        buf, first, rows = far[at]
+        slot = buf.at[lax.rem(m + 2, 4), pl.ds(first, rows)]
         remote(slot, slot, f_s.at[at], f_x.at[at], partner).wait_recv()
         remote(slot, slot, f_s.at[at], f_c.at[at], partner).start()
 
-    def far_recv(buf, at):
-        slots = buf.at[pl.ds(0, 2)]
+    def far_recv(at):
+        buf, first, rows = far[at]
+        slots = buf.at[pl.ds(0, 2), pl.ds(first, rows)]
         remote(slots, slots, f_s.at[at], f_c.at[at], partner).wait_recv()
 
-    def far_drain(buf, at):
-        slots = buf.at[pl.ds(0, 3)]
+    def far_drain(at):
+        buf, first, rows = far[at]
+        slots = buf.at[pl.ds(0, 3), pl.ds(first, rows)]
         remote(slots, slots, f_s.at[at], f_c.at[at], partner).wait_send()
+
+    split_row = FIRST_FOLDS * 16
+    far = (
+        (fq, 0, fq.shape[1]),
+        (fg, 0, split_row),
+        (fg, split_row, fg.shape[1] - split_row),
+        (fd, 0, fd.shape[1]),
+    )
 
     def on_core(which):
         return pl.when(core == which)
@@ -590,15 +604,11 @@
     def far_slot(i):
         return lax.rem(hi + half_dp - i, half_dp) * 2 + 1 - lo
 
-    def split_far(mine, body):
-        split_hi(mine, lambda i: body(half_dp + i, far_slot(i)))
-
-        @pl.when(core == (0 if mine else 1))
-        def _():
-            body(half_dp, far_slot(0))
-
-    def split_near(mine, body):
-        split_hi(mine, lambda i: body(i, near_slot(i)))
+    def split_far(body):
+        split_hi(True, lambda i: body(far_slot(i)))
+
+    def split_near(body):
+        split_hi(True, lambda i: body(near_slot(i)))
 
     def rows_of(slot, part, which):
         start = (which * TOKEN_PARTS + part) * part_rows
@@ -617,8 +627,7 @@
                     remote(rows, rows, t_s.at[0], recv, partner).wait_recv()
 
     quarter = half_dp // 2
-    near_counts = (quarter - 1, quarter)
-    far_counts = (quarter, quarter)
+    counts = (quarter - 1, quarter)
 
     def tok_start(part):
         rows = rows_of(d, part, side)
@@ -627,43 +636,47 @@
             tok_push(rows, tz_r.at[part], (lax.rem(hi + i, half_dp) * 2 + lo, m))
 
         split_hi(True, body)
-        on_core(0)(lambda: tok_push(rows, ty_r.at[part], beside))
+
+        @on_core(0)
+        def _():
+            for which in (0, 1):
+                tok_push(rows_of(d, part, which), to_r.at[part], beside)
+
+    def tok_own(part):
+        tok_wait(to_r.at[part], (2, 0))
+
+        @on_core(0)
+        def _():
+            for which in (0, 1):
+                tok_push(rows_of(far_slot(0), part, which), tl_r.at[0], partner)
 
     def tok_second(part):
-        tok_wait(tz_r.at[part], near_counts)
-
-        def body(i, slot):
+        tok_wait(tz_r.at[part], counts)
+
+        def body(slot):
             rows = rows_of(slot, part, side)
             tok_push(rows, ty_r.at[part], beside)
             tok_push(rows, tl_r.at[0], partner)
 
-        split_near(True, body)
+        split_near(body)
 
     def tok_third(part):
-        tok_wait(ty_r.at[part], far_counts)
-        split_far(True, lambda at, slot: tok_push(rows_of(slot, part, side), tl_r.at[0], partner))
+        tok_wait(ty_r.at[part], counts)
+        split_far(lambda slot: tok_push(rows_of(slot, part, side), tl_r.at[0], partner))
 
     def tok_near(part):
-        split_near(
-            True, lambda at, slot: tok_push(rows_of(slot, part, side), tx_r.at[part, 0], across)
-        )
+        split_near(lambda slot: tok_push(rows_of(slot, part, side), tx_r.at[part, 0], across))
 
     def tok_far(part):
-        split_far(
-            True, lambda at, slot: tok_push(rows_of(slot, part, side), tx_r.at[part, 1], across)
-        )
+        split_far(lambda slot: tok_push(rows_of(slot, part, side), tx_r.at[part, 1], across))
 
     def tok_pass_near(part):
-        tok_wait(tx_r.at[part, 0], near_counts)
-        split_near(
-            True, lambda at, slot: tok_push(rows_of(slot, part, 1 - side), tl_r.at[0], partner)
-        )
+        tok_wait(tx_r.at[part, 0], counts)
+        split_near(lambda slot: tok_push(rows_of(slot, part, 1 - side), tl_r.at[0], partner))
 
     def tok_pass_far(part):
-        tok_wait(tx_r.at[part, 1], far_counts)
-        split_far(
-            True, lambda at, slot: tok_push(rows_of(slot, part, 1 - side), tl_r.at[0], partner)
-        )
+        tok_wait(tx_r.at[part, 1], counts)
+        split_far(lambda slot: tok_push(rows_of(slot, part, 1 - side), tl_r.at[0], partner))
 
     def tok_last():
         for which, count in ((0, 2 * quarter), (1, 2 * quarter - 1)):
@@ -684,6 +697,7 @@
     def token_steps(at):
         steps = {
             "start": tok_start,
+            "own": tok_own,
             "second": tok_second,
             "third": tok_third,
             "near": tok_near,
@@ -706,28 +720,37 @@
     for k in range(chunk):
         image_load(k).wait()
     gain, shift = vector("ig1", ig1_ref), vector("ib1", ib1_ref)
+    loads["iw"].wait()
+    hats = [
+        normalized(xi[k * chunk_rows : (k + 1) * chunk_rows, :].astype(F32))[0].astype(BF16)
+        for k in range(chunk)
+    ]
     firsts = [i * IMG_LEN for i in range(pairs)]
     image_first = jnp.concatenate([xi[r : r + 1, :].astype(F32) for r in firsts], axis=0)
     first_n = (normalized(image_first)[0] * gain + shift).astype(BF16)
-    loads["iw"].wait()
-    image_q = dot_nt(first_n, iw[0])
-    image_fold = dot(head_blocks(image_q, width).astype(BF16), iw[1])
+    image_fold = dot(head_blocks(dot_nt(first_n, iw[0]), width).astype(BF16), iw[1])
+    shifted = jnp.sum(image_fold * shift, axis=-1, keepdims=True)
+    image_fold = image_fold * gain
     group = pairs // chunk
     shape = (group, chunk_rows)
     place = lax.broadcasted_iota(jnp.int32, shape, 1)
     begin = lax.broadcasted_iota(jnp.int32, shape, 0) * IMG_LEN
     inside = jnp.concatenate([(place >= begin) & (place < begin + IMG_LEN)] * heads, axis=0)
-    image_mixed = []
-    for k in range(chunk):
-        hat = normalized(xi[k * chunk_rows : (k + 1) * chunk_rows, :].astype(F32))[0]
-        low = (hat * gain + shift).astype(BF16)
+
+    def of_group(rows, k):
         spots = [h * pairs + k * group for h in range(heads)]
-        asked = jnp.concatenate([image_fold[at : at + group] for at in spots], axis=0)
-        scores = dot_nt(asked.astype(BF16), low) * scale
-        image_mixed.append(dot(softmax_rows(scores, inside).astype(BF16), low))
+        return jnp.concatenate([rows[at : at + group] for at in spots], axis=0)
+
+    image_scores = [
+        (dot_nt(of_group(image_fold, k).astype(BF16), hats[k]) + of_group(shifted, k)) * scale
+        for k in range(chunk)
+    ]
+    image_probs = [softmax_rows(scores, inside).astype(BF16) for scores in image_scores]
+    image_mixed = [dot(image_probs[k], hats[k]) for k in range(chunk)]
     image_mixed = jnp.concatenate(
         [mixed[h * group : (h + 1) * group] for h in range(heads) for mixed in image_mixed], axis=0
     )
+    image_mixed = image_mixed * gain + shift
     image_context = head_pick(dot_nt(image_mixed.astype(BF16), iw[2]), width).astype(BF16)
     loads["io"].wait()
     ar[0, m] = to_tall(dot(image_context, io[...]))
@@ -810,19 +833,20 @@
     dp_send(1)
     gat[2, lo, hi] = to_tall(middle + summed(3))
     dp_send(2)
-    far_send(fq, 0)
+    far_send(0)
 
     token_steps(4)
     dp_forward(1)
     token_steps(9)
     dp_forward(2)
     dp_send(0)
-    far_pass(fq, 0)
+    far_pass(0)
     token_steps(5)
     dp_recv(1)
+    image_low = gathered(1).astype(BF16)
+    own_labels = column_of(ids[d, seg_rows : seg_rows + 1, :], pairs)
     dp_recv(2)
 
-    image_low = gathered(1).astype(BF16)
 
     def embedded(rows):
         shrink = lax.rsqrt(jnp.sum(rows * rows, axis=-1, keepdims=True) + 1e-06)
@@ -843,7 +867,6 @@
     shrink_all, unit_all, logits = embedded(gathered(2))
     col_top = jnp.max(logits, axis=0, keepdims=True)
     col_lse = col_top + jnp.log(jnp.sum(jnp.exp(logits - col_top), axis=0, keepdims=True))
-    own_labels = column_of(ids[d, seg_rows : seg_rows + 1, :], pairs)
     grad_final, own_lse, positive = final_grad(*embedded(from_tall(gat[2, lo, hi])), own_labels)
     grad_hidden = (dot_nt(grad_final.astype(BF16), td[...]) * slope).astype(BF16)
     ar[4, m] = to_tall(dot_nt(grad_hidden, tu[...]))
@@ -874,6 +897,7 @@
     grad_context = dot_nt(middle_low, to[...]).astype(BF16)
     grad_folded = dot(head_blocks(grad_context.astype(F32), width).astype(BF16), tw[2])
     fg[m] = padded(grad_folded, no_foot)
+    far_send(1)
     grad_probs = dot_nt(grad_folded.astype(BF16), normed)
     grad_scores = probs * (grad_probs - jnp.sum(grad_probs * probs, axis=-1, keepdims=True))
     scaled = grad_scores * scale
@@ -907,8 +931,8 @@
         [jnp.sum(part * hat_one, axis=0, keepdims=True), jnp.sum(part, axis=0, keepdims=True)]
     )
     mp_send(stm, st_s.at[0], st_r.at[0])
-    far_send(fg, 1)
-    far_send(fd, 2)
+    far_send(2)
+    far_send(3)
     small_send(1, prow)
     stats_two = [
         jnp.sum(grad_n2 * hat_two, axis=0, keepdims=True),
@@ -921,21 +945,22 @@
     act_all, slope_all = gelu_parts(dot(n2_all, tu[...]) + up_shift)
     gh_all = (dot_nt(fin_all, td[...]) * slope_all).astype(BF16)
     up_bias = jnp.sum(gh_all.astype(F32), axis=0, keepdims=True)
+    up_o[...] = dot_tn(n2_all, gh_all)
+    down_o[...] = dot_tn(act_all.astype(BF16), fin_all)
     mp_recv(stm, st_s.at[0], st_r.at[0])
     one = stm[0]
     for i in range(1, n_mp):
         one = one + stm[i]
-    std[d] = stats_pack(stats_unpack(one, 2, features) + stats_two)
+    std[d] = stats_pack(stats_unpack(one, 2, features) + stats_two, 16).astype(BF16)
     small_send(2, std)
+    far_pass(1)
+    far_pass(2)
     dp_forward(3)
-    far_pass(fg, 1)
-    far_pass(fd, 2)
+    far_pass(3)
     token_steps(8)
-    up_o[...] = dot_tn(n2_all, gh_all)
-    down_o[...] = dot_tn(act_all.astype(BF16), fin_all)
-
-    for at, buf in ((0, fq), (1, fg), (2, fd)):
-        far_recv(buf, at)
+
+    for at in range(len(far)):
+        far_recv(at)
     flat = [ref[...].reshape(n_mp * ref.shape[1], features) for ref in (fq, fg, fd)]
     grad_normed = first_norm_grad(list(range(n_mp)), flat)
     text_grad = norm_back(grad_normed, hat_one, factor_one, gain_one)
@@ -964,17 +989,17 @@
     mid_o[...] = gathered(3).astype(BF16)
 
     small_recv(2, std)
-    stats = std[0]
+    stats = std[0].astype(F32)
     for i in range(1, n_dp):
-        stats = stats + std[i]
+        stats = stats + std[i].astype(F32)
     rows = stats_unpack(stats, 4, features)
     vec_o[...] = jnp.concatenate(rows + [up_bias, jnp.zeros((3, features), F32)], axis=0)
 
     for at in range(ar.shape[0]):
         mp_drain(ar.at[at], ar_s.at[at], ar_r.at[at])
     mp_drain(stm, st_s.at[0], st_r.at[0])
-    for at, buf in enumerate((fq, fg, fd)):
-        far_drain(buf, at)
+    for at in range(len(far)):
+        far_drain(at)
     for at in range(gat.shape[0]):
         dp_drain(at)
     for at, buf in enumerate((ids, prow, std)):
@@ -1147,7 +1172,7 @@
             vmem((n_dp, 8, 128), jnp.int32),
             vmem((n_dp, 8, tokens), F32),
             vmem((n_mp, 16, 128), F32),
-            vmem((n_dp, 24, 128), F32),
+            vmem((n_dp, 32, 128), BF16),
             vmem((5, n_mp) + tall, BF16),
             vmem((4, 2, half_dp) + tall, BF16),
             vmem((n_mp, fold_rows, features), BF16),
@@ -1158,6 +1183,7 @@
             sems(1),
             sems(TOKEN_PARTS),
             sems(TOKEN_PARTS),
+            sems(TOKEN_PARTS),
             sems(TOKEN_PARTS, 2),
             sems(1),
             sems(5),
@@ -1166,9 +1192,9 @@
             sems(4),
             sems(4),
             sems(4),
-            sems(3),
-            sems(3),
-            sems(3),
+            sems(4),
+            sems(4),
+            sems(4),
             sems(1),
             sems(1),
             sems(3),

time: 48.5 us -> 46.9 us (0.967)
  Pallas kernels: 47.7 us -> 46.1 us
    pallas_call x1, Pallas kernels: 43.7 us -> 42 us  [kernel_device(): pl.pallas_call(functools.partial(step_kernel, (n_dp, n_mp, pairs, tokens,...]
where the time goes in v6:
time: 46.9 us; the launch traced here: 46.8 us
  Pallas kernels  46.1 us (98%)
  between operations  0.66 us (1%)
    pallas_call x1, Pallas kernels, kernel_device(): pl.pallas_call(functools.partial(step_kernel, (n_dp, n_mp, pairs, tokens,...  42 us
    pallas_call x1, Pallas kernels, kernel_device(): pl.pallas_call(weights_kernel, out_shape=[jax.ShapeDtypeStruct((tokens, f...  4.05 us

profile of v6, /device:TPU:0, one launch (start us, length us, event | category | flops | bytes accessed | tf_op | source)
XLA Modules:
  0.0 46.8 jit_solution(6232683539063888313)
XLA Ops:
  0.7 42.0 %step.1 = (f32[768,768]{1,0:T(8,128)S(1)}, f32[768,768]{1,0:T(8,128)S(1)}, bf16[3,192,768]{2,1,0:T(8,128)(2,1)S(1)}, bf16[192,768]{1,0:T(8,128)(2,1)S(1)}, bf16[...) custom-call(bf16[256,768]{1,0:T(8,128)(2,1)} %text_hbm.1, ...), custom_call_target="tpu_custom_call" | custom-call | tf_op jit(solution)/shard_map/step/pallas_call | solution.py:1154
  42.7 4.1 %weights.1 = (f32[256,768]{1,0:T(8,128)}, f32[3,192,768]{2,1,0:T(8,128)}, f32[192,768]{1,0:T(8,128)}, f32[768,768]{1,0:T(8,128)}, f32[768,768]{1,0:T(8,128)}, /*...) custom-call(f32[768,768]{1,0:T(8,128)S(1)} %get-tuple-element.33.up, ...), custom_call_target="tpu_custom_call" | custom-call | tf_op jit(solution)/shard_map/weights/pallas_call | solution.py:1209

commit v7 on v6

--- a/solution.py
+++ b/solution.py
@@ -366,6 +366,7 @@
     tok,
     ids,
     prow,
+    drow,
     stm,
     std,
     ar,
@@ -768,7 +769,6 @@
     for i in range(seg_rows):
         ids[d, i : i + 1, :] = seg[:, i * 128 : (i + 1) * 128]
     ids[d, seg_rows : seg_rows + 1, 0:pairs] = vector("lab", lab_ref)
-    small_send(0, ids)
 
     normed = tok[d]
     mine, pick = caption_masks(seg, d * pairs, pairs)
@@ -795,6 +795,7 @@
     no_foot = jnp.zeros((8, tokens), F32)
     prob_rows = head_rows(probs)
     fq[m] = padded(folded.astype(F32), prob_rows)
+    prow[d] = stats_pack([prob_rows[h : h + 1] for h in range(heads)])
     token_steps(1)
 
     def summed(at):
@@ -840,6 +841,7 @@
     token_steps(9)
     dp_forward(2)
     dp_send(0)
+    small_send(0, ids)
     far_pass(0)
     token_steps(5)
     dp_recv(1)
@@ -871,6 +873,7 @@
     grad_hidden = (dot_nt(grad_final.astype(BF16), td[...]) * slope).astype(BF16)
     ar[4, m] = to_tall(dot_nt(grad_hidden, tu[...]))
     mp_send(ar.at[4], ar_s.at[4], ar_r.at[4])
+    small_send(1, prow)
 
     token_steps(6)
     lanes = lax.broadcasted_iota(jnp.int32, (pairs, total), 1)
@@ -888,6 +891,22 @@
     )
     fin_all = final_grad(shrink_all, unit_all, logits, labels)[0].astype(BF16)
     dp_forward(0)
+
+    def spread(slots, ref, at):
+        parts = []
+        for i in slots:
+            foot = ref[i, at : at + 8, 0:tokens].astype(F32)
+            for h in range(heads):
+                parts.append(jnp.where(mine, foot[h : h + 1], 0.0))
+            parts.append(jnp.zeros((8, tokens), F32))
+        return jnp.concatenate(parts, axis=0).astype(BF16)
+
+    def placed(count):
+        spots = jnp.concatenate([pick.astype(F32), jnp.zeros((8, tokens), F32)], axis=0)
+        return jnp.concatenate([spots] * count, axis=0).astype(BF16)
+
+    own_probs = spread([m], fq, pairs * heads)
+    own_spots = placed(1)
 
     grad_n2 = summed(4)
     grad_middle = grad_final + norm_back(grad_n2, hat_two, factor_two, gain_two)
@@ -902,42 +921,25 @@
     grad_scores = probs * (grad_probs - jnp.sum(grad_probs * probs, axis=-1, keepdims=True))
     scaled = grad_scores * scale
     score_rows = head_rows(scaled)
-    prow[d] = jnp.concatenate([prob_rows[:heads], score_rows[: 8 - heads]], axis=0)
     mixed_back = dot(scaled.astype(BF16), normed).astype(BF16)
     grad_queries = head_pick(dot_nt(mixed_back, tw[1]), width).astype(BF16)
     fd[m] = padded(dot(grad_queries, tw[0]), score_rows)
 
-    def spread(slots, ref, at):
-        parts = []
-        for i in slots:
-            foot = ref[i, at : at + 8, 0:tokens].astype(F32)
-            for h in range(heads):
-                parts.append(jnp.where(mine, foot[h : h + 1], 0.0))
-            parts.append(jnp.zeros((8, tokens), F32))
-        return jnp.concatenate(parts, axis=0).astype(BF16)
-
-    def first_norm_grad(slots, sources):
-        folds, backs, rests = sources
-        place_low = jnp.concatenate(
-            [jnp.concatenate([pick.astype(F32), jnp.zeros((8, tokens), F32)], axis=0)] * len(slots),
-            axis=0,
-        ).astype(BF16)
-        grads = dot_tn(spread(slots, fd, pairs), folds)
-        grads = grads + dot_tn(spread(slots, fq, pairs * heads), backs)
-        return grads + dot_tn(place_low, rests)
-
-    part = first_norm_grad([m], (fq[m], fg[m], fd[m]))
+    part = dot_tn(spread([m], fd, pairs), fq[m])
+    part = part + dot_tn(own_probs, fg[m])
+    part = part + dot_tn(own_spots, fd[m])
     stm[m] = stats_pack(
         [jnp.sum(part * hat_one, axis=0, keepdims=True), jnp.sum(part, axis=0, keepdims=True)]
     )
     mp_send(stm, st_s.at[0], st_r.at[0])
     far_send(2)
     far_send(3)
-    small_send(1, prow)
     stats_two = [
         jnp.sum(grad_n2 * hat_two, axis=0, keepdims=True),
         jnp.sum(grad_n2, axis=0, keepdims=True),
     ]
+    drow[d] = stats_pack([score_rows[h : h + 1] for h in range(heads)] + stats_two, 16).astype(BF16)
+    small_send(3, drow)
 
     token_steps(7)
     dp_recv(0)
@@ -951,7 +953,7 @@
     one = stm[0]
     for i in range(1, n_mp):
         one = one + stm[i]
-    std[d] = stats_pack(stats_unpack(one, 2, features) + stats_two, 16).astype(BF16)
+    std[d] = stats_pack(stats_unpack(one, 2, features), 16).astype(BF16)
     small_send(2, std)
     far_pass(1)
     far_pass(2)
@@ -959,32 +961,55 @@
     far_pass(3)
     token_steps(8)
 
-    for at in range(len(far)):
+    everyone = list(range(n_mp))
+
+    def flat(ref):
+        return ref[...].reshape(n_mp * ref.shape[1], features)
+
+    for at in range(3):
         far_recv(at)
-    flat = [ref[...].reshape(n_mp * ref.shape[1], features) for ref in (fq, fg, fd)]
-    grad_normed = first_norm_grad(list(range(n_mp)), flat)
+    from_probs = dot_tn(spread(everyone, fq, pairs * heads), flat(fg))
+    far_recv(3)
+    grad_normed = dot_tn(spread(everyone, fd, pairs), flat(fq)) + from_probs
+    grad_normed = grad_normed + dot_tn(placed(n_mp), flat(fd))
     text_grad = norm_back(grad_normed, hat_one, factor_one, gain_one)
     tg_o[...] = text_grad + dot_tn(pick, middle_low)
 
     small_recv(1, prow)
     tok_last()
     twice = 2 * pairs
+    pair_masks = []
     for j in range(half_dp):
         seg = jnp.concatenate(
             [ids[i, k : k + 1, :] for i in (2 * j, 2 * j + 1) for k in range(seg_rows)], axis=1
         )
-        here, picks = caption_masks(seg, j * twice, twice)
-        values = jnp.concatenate([prow[2 * j], prow[2 * j + 1]], axis=1)
-        parts = [jnp.where(here, values[h : h + 1], 0.0) for h in range(heads)]
-        parts += [jnp.where(here, values[heads + h : heads + h + 1], 0.0) for h in range(heads)]
-        parts = [part.astype(BF16) for part in parts] + [picks]
-        low = tok[2 * j : 2 * j + 2].reshape(2 * tokens, features)
-        mixed = dot(jnp.concatenate(parts, axis=0), low).astype(BF16)
-        rows = slice(j * twice, (j + 1) * twice)
+        pair_masks.append(caption_masks(seg, j * twice, twice))
+
+    def pair_at(j):
+        return slice(j * twice, (j + 1) * twice)
+
+    def pair_rows(j):
+        return tok[2 * j : 2 * j + 2].reshape(2 * tokens, features)
+
+    def spread_pair(j, rows, h):
+        values = jnp.concatenate([rows[2 * j][h], rows[2 * j + 1][h]], axis=1)
+        return jnp.where(pair_masks[j][0], values, 0.0).astype(BF16)
+
+    early_rows = [stats_unpack(prow[i], heads, tokens) for i in range(n_dp)]
+    for j in range(half_dp):
+        parts = [spread_pair(j, early_rows, h) for h in range(heads)] + [pair_masks[j][1]]
+        mixed = dot(jnp.concatenate(parts, axis=0), pair_rows(j)).astype(BF16)
         for h in range(heads):
-            xv_o[h, rows, :] = mixed[h * twice : (h + 1) * twice]
-            xk_o[h, rows, :] = mixed[(heads + h) * twice : (heads + h + 1) * twice]
-        nsel_o[rows, :] = mixed[2 * heads * twice :]
+            xv_o[h, pair_at(j), :] = mixed[h * twice : (h + 1) * twice]
+        nsel_o[pair_at(j), :] = mixed[heads * twice :]
+
+    small_recv(3, drow)
+    late_rows = [stats_unpack(drow[i].astype(F32), heads, tokens) for i in range(n_dp)]
+    for j in range(half_dp):
+        parts = [spread_pair(j, late_rows, h) for h in range(heads)]
+        mixed = dot(jnp.concatenate(parts, axis=0), pair_rows(j)).astype(BF16)
+        for h in range(heads):
+            xk_o[h, pair_at(j), :] = mixed[h * twice : (h + 1) * twice]
     dp_recv(3)
     mid_o[...] = gathered(3).astype(BF16)
 
@@ -992,7 +1017,11 @@
     stats = std[0].astype(F32)
     for i in range(1, n_dp):
         stats = stats + std[i].astype(F32)
-    rows = stats_unpack(stats, 4, features)
+    late = drow[0].astype(F32)
+    for i in range(1, n_dp):
+        late = late + drow[i].astype(F32)
+    rows = stats_unpack(stats, 2, features)
+    rows += stats_unpack(late[heads * seg_rows :], 2, features)
     vec_o[...] = jnp.concatenate(rows + [up_bias, jnp.zeros((3, features), F32)], axis=0)
 
     for at in range(ar.shape[0]):
@@ -1002,7 +1031,7 @@
         far_drain(at)
     for at in range(gat.shape[0]):
         dp_drain(at)
-    for at, buf in enumerate((ids, prow, std)):
+    for at, buf in enumerate((ids, prow, std, drow)):
         small_drain(at, buf)
     tok_drain()
 
@@ -1033,6 +1062,7 @@
     qkv_buf,
     out_buf,
     sem,
+    *vec_bufs,
 ):
     heads, total, features = xk.shape
     width = to.shape[0]
@@ -1049,6 +1079,11 @@
             rows = pl.ds(at, step)
             ship(src.at[rows], dst.at[rows])
     ship(tg, tg_out)
+    for at, dst in enumerate((g1_out, b1_out, g2_out, b2_out, ub_out)):
+        vec_bufs[at][...] = vec[at, :]
+        ship(vec_bufs[at], dst)
+    vec_bufs[5][...] = loss[0, 0 : loss_out.shape[0]]
+    ship(vec_bufs[5], loss_out)
     flat_k = xk[...].reshape(heads * total, features)
     flat_v = xv[...].reshape(heads * total, features)
     queries = dot_nt(nsel[...], tw[0])
@@ -1063,9 +1098,6 @@
     context = head_pick(dot_nt(flat_v, tw[2]), width).astype(BF16)
     out_buf[...] = dot_tn(context, mid[...])
     ship(out_buf, out_out)
-    for at, dst in enumerate((g1_out, b1_out, g2_out, b2_out, ub_out)):
-        dst[...] = vec[at, :]
-    loss_out[...] = loss[0, 0 : loss_out.shape[0]]
     for copy in started:
         copy.wait()
 
@@ -1170,9 +1202,10 @@
         + [
             vmem((n_dp, tokens, features), BF16),
             vmem((n_dp, 8, 128), jnp.int32),
-            vmem((n_dp, 8, tokens), F32),
+            vmem((n_dp, 8, 128), F32),
+            vmem((n_dp, 32, 128), BF16),
             vmem((n_mp, 16, 128), F32),
-            vmem((n_dp, 32, 128), BF16),
+            vmem((n_dp, 16, 128), BF16),
             vmem((5, n_mp) + tall, BF16),
             vmem((4, 2, half_dp) + tall, BF16),
             vmem((n_mp, fold_rows, features), BF16),
@@ -1197,8 +1230,8 @@
             sems(4),
             sems(1),
             sems(1),
-            sems(3),
-            sems(3),
+            sems(4),
+            sems(4),
         ],
         compiler_params=pltpu.CompilerParams(
             collective_id=0, has_side_effects=True, vmem_limit_bytes=48 * 2**20
@@ -1222,12 +1255,14 @@
             jax.ShapeDtypeStruct((hidden,), F32),
         ],
         in_specs=[whole] * len(outs),
-        out_specs=[anywhere] * 5 + [whole] * 6,
+        out_specs=[anywhere] * 11,
         scratch_shapes=[
             vmem((3, width, features), F32),
             vmem((width, features), F32),
-            sems(2 * SHIP_PARTS + 5),
-        ],
+            sems(2 * SHIP_PARTS + 11),
+        ]
+        + [vmem((features,), F32)] * 4
+        + [vmem((hidden,), F32), vmem((pairs,), F32)],
         compiler_params=pltpu.CompilerParams(vmem_limit_bytes=32 * 2**20),
         name="weights",
     )(*[pltpu.with_memory_space_constraint(factor, pltpu.VMEM) for factor in factors])

time: 46.9 us -> 46 us (0.981)
  Pallas kernels: 46.1 us -> 45.2 us
    pallas_call x1, Pallas kernels: 4.05 us -> 3.45 us  [kernel_device(): pl.pallas_call(weights_kernel, out_shape=[jax.ShapeDtypeStruct((tokens, f...]
where the time goes in v7:
time: 46 us; the launch traced here: 45.8 us
  Pallas kernels  45.2 us (98%)
  between operations  0.66 us (1%)
    pallas_call x1, Pallas kernels, kernel_device(): pl.pallas_call(functools.partial(step_kernel, (n_dp, n_mp, pairs, tokens,...  41.7 us
    pallas_call x1, Pallas kernels, kernel_device(): pl.pallas_call(weights_kernel, out_shape=[jax.ShapeDtypeStruct((tokens, f...  3.45 us

profile of v7, /device:TPU:0, one launch (start us, length us, event | category | flops | bytes accessed | tf_op | source)
XLA Modules:
  0.0 45.8 jit_solution(14264546935286319846)
XLA Ops:
  0.7 41.7 %step.1 = (f32[768,768]{1,0:T(8,128)S(1)}, f32[768,768]{1,0:T(8,128)S(1)}, bf16[3,192,768]{2,1,0:T(8,128)(2,1)S(1)}, bf16[192,768]{1,0:T(8,128)(2,1)S(1)}, bf16[...) custom-call(bf16[256,768]{1,0:T(8,128)(2,1)} %text_hbm.1, ...), custom_call_target="tpu_custom_call" | custom-call | tf_op jit(solution)/shard_map/step/pallas_call | solution.py:1186
  42.4 3.4 %weights.1 = (f32[256,768]{1,0:T(8,128)}, f32[3,192,768]{2,1,0:T(8,128)}, f32[192,768]{1,0:T(8,128)}, f32[768,768]{1,0:T(8,128)}, f32[768,768]{1,0:T(8,128)}, /*...) custom-call(f32[768,768]{1,0:T(8,128)S(1)} %get-tuple-element.33.up, ...), custom_call_target="tpu_custom_call" | custom-call | tf_op jit(solution)/shard_map/weights/pallas_call | solution.py:1242

commit v8 on v7

--- a/solution.py
+++ b/solution.py
@@ -248,15 +248,16 @@
 
 MESH = pl.DeviceIdType.MESH
 TOKEN_PARTS = 2
-SHIP_PARTS = 4
+SHIP_PARTS = 1
 FIRST_FOLDS = 2
 STEPS = {
     0: (("start", 0), ("start", 1)),
     3: (("second", 0), ("near", 0), ("own", 0)),
     4: (("second", 1), ("near", 1), ("own", 1)),
-    9: (("third", 0), ("far", 0), ("pass", 0)),
-    6: (("third", 1), ("far", 1), ("pass", 1)),
-    8: (("last", 0), ("last", 1)),
+    9: (("pass", 0),),
+    6: (("pass", 1),),
+    7: (("third", 0), ("third", 1)),
+    8: (("fourth", 0), ("fourth", 1)),
 }
 
 
@@ -381,6 +382,7 @@
     ty_r,
     to_r,
     tx_r,
+    tw_r,
     tl_r,
     ar_s,
     ar_r,
@@ -666,17 +668,20 @@
         split_far(lambda slot: tok_push(rows_of(slot, part, side), tl_r.at[0], partner))
 
     def tok_near(part):
-        split_near(lambda slot: tok_push(rows_of(slot, part, side), tx_r.at[part, 0], across))
-
-    def tok_far(part):
-        split_far(lambda slot: tok_push(rows_of(slot, part, side), tx_r.at[part, 1], across))
-
-    def tok_pass_near(part):
-        tok_wait(tx_r.at[part, 0], counts)
-        split_near(lambda slot: tok_push(rows_of(slot, part, 1 - side), tl_r.at[0], partner))
-
-    def tok_pass_far(part):
-        tok_wait(tx_r.at[part, 1], counts)
+        split_near(lambda slot: tok_push(rows_of(slot, part, side), tx_r.at[part], across))
+
+    def tok_pass(part):
+        tok_wait(tx_r.at[part], counts)
+
+        def body(slot):
+            rows = rows_of(slot, part, 1 - side)
+            tok_push(rows, tw_r.at[part], beside)
+            tok_push(rows, tl_r.at[0], partner)
+
+        split_near(body)
+
+    def tok_fourth(part):
+        tok_wait(tw_r.at[part], counts)
         split_far(lambda slot: tok_push(rows_of(slot, part, 1 - side), tl_r.at[0], partner))
 
     def tok_last():
@@ -702,9 +707,8 @@
             "second": tok_second,
             "third": tok_third,
             "near": tok_near,
-            "far": tok_far,
-            "pass": tok_pass_near,
-            "last": tok_pass_far,
+            "pass": tok_pass,
+            "fourth": tok_fourth,
         }
         for name, part in STEPS.get(at, ()):
             steps[name](part)
@@ -840,8 +844,6 @@
     dp_forward(1)
     token_steps(9)
     dp_forward(2)
-    dp_send(0)
-    small_send(0, ids)
     far_pass(0)
     token_steps(5)
     dp_recv(1)
@@ -873,6 +875,8 @@
     grad_hidden = (dot_nt(grad_final.astype(BF16), td[...]) * slope).astype(BF16)
     ar[4, m] = to_tall(dot_nt(grad_hidden, tu[...]))
     mp_send(ar.at[4], ar_s.at[4], ar_r.at[4])
+    small_send(0, ids)
+    dp_send(0)
     small_send(1, prow)
 
     token_steps(6)
@@ -885,12 +889,6 @@
         jnp.int32, shape, 1
     )
     loss_o[...] = jnp.sum(jnp.where(diagonal, pair_loss, 0.0), axis=0, keepdims=True)
-    small_recv(0, ids)
-    labels = jnp.concatenate(
-        [column_of(ids[i, seg_rows : seg_rows + 1, :], pairs) for i in range(n_dp)], axis=0
-    )
-    fin_all = final_grad(shrink_all, unit_all, logits, labels)[0].astype(BF16)
-    dp_forward(0)
 
     def spread(slots, ref, at):
         parts = []
@@ -942,6 +940,12 @@
     small_send(3, drow)
 
     token_steps(7)
+    small_recv(0, ids)
+    labels = jnp.concatenate(
+        [column_of(ids[i, seg_rows : seg_rows + 1, :], pairs) for i in range(n_dp)], axis=0
+    )
+    fin_all = final_grad(shrink_all, unit_all, logits, labels)[0].astype(BF16)
+    dp_forward(0)
     dp_recv(0)
     n2_all = (normalized(gathered(0))[0] * gain_two + shift_two).astype(BF16)
     act_all, slope_all = gelu_parts(dot(n2_all, tu[...]) + up_shift)
@@ -1217,7 +1221,8 @@
             sems(TOKEN_PARTS),
             sems(TOKEN_PARTS),
             sems(TOKEN_PARTS),
-            sems(TOKEN_PARTS, 2),
+            sems(TOKEN_PARTS),
+            sems(TOKEN_PARTS),
             sems(1),
             sems(5),
             sems(5),

time: 46 us -> 44.8 us (0.974)
  Pallas kernels: 45.2 us -> 43.9 us
    pallas_call x1, Pallas kernels: 41.7 us -> 40.5 us  [kernel_device(): pl.pallas_call(functools.partial(step_kernel, (n_dp, n_mp, pairs, tokens,...]
where the time goes in v8:
time: 44.8 us; the launch traced here: 44.6 us
  Pallas kernels  43.9 us (98%)
  between operations  0.66 us (1%)
    pallas_call x1, Pallas kernels, kernel_device(): pl.pallas_call(functools.partial(step_kernel, (n_dp, n_mp, pairs, tokens,...  40.5 us
    pallas_call x1, Pallas kernels, kernel_device(): pl.pallas_call(weights_kernel, out_shape=[jax.ShapeDtypeStruct((tokens, f...  3.39 us

profile of v8, /device:TPU:0, one launch (start us, length us, event | category | flops | bytes accessed | tf_op | source)
XLA Modules:
  0.0 44.6 jit_solution(9140191167166011658)
XLA Ops:
  0.7 40.5 %step.1 = (f32[768,768]{1,0:T(8,128)S(1)}, f32[768,768]{1,0:T(8,128)S(1)}, bf16[3,192,768]{2,1,0:T(8,128)(2,1)S(1)}, bf16[192,768]{1,0:T(8,128)(2,1)S(1)}, bf16[...) custom-call(bf16[256,768]{1,0:T(8,128)(2,1)} %text_hbm.1, ...), custom_call_target="tpu_custom_call" | custom-call | tf_op jit(solution)/shard_map/step/pallas_call | solution.py:1190
  41.2 3.4 %weights.1 = (f32[256,768]{1,0:T(8,128)}, f32[3,192,768]{2,1,0:T(8,128)}, f32[192,768]{1,0:T(8,128)}, f32[768,768]{1,0:T(8,128)}, f32[768,768]{1,0:T(8,128)}, /*...) custom-call(f32[768,768]{1,0:T(8,128)S(1)} %get-tuple-element.33.up, ...), custom_call_target="tpu_custom_call" | custom-call | tf_op jit(solution)/shard_map/weights/pallas_call | solution.py:1247

commit v9 on v8

--- a/solution.py
+++ b/solution.py
@@ -760,13 +760,13 @@
     loads["io"].wait()
     ar[0, m] = to_tall(dot(image_context, io[...]))
 
-    pl.semaphore_wait(barrier, n_mp - 1 + n_dp - 1)
-    mp_send(ar.at[0], ar_s.at[0], ar_r.at[0])
-
     loads["text"].wait()
     gain_one = vector("tg1", tg1_ref)
     hat_one, factor_one = normalized(xt[...].astype(F32))
     tok[d] = (hat_one * gain_one + vector("tb1", tb1_ref)).astype(BF16)
+    pl.semaphore_wait(barrier, n_mp - 1 + n_dp - 1)
+    mp_send(ar.at[0], ar_s.at[0], ar_r.at[0])
+
     token_steps(0)
     seg = vector("seg", seg_ref)
     seg_rows = tokens // 128

time: 44.8 us -> 44.8 us (level)
  no operation moved by 1% of the time
where the time goes in v9:
time: 44.8 us; the launch traced here: 44.7 us
  Pallas kernels  44 us (98%)
  between operations  0.66 us (1%)
    pallas_call x1, Pallas kernels, kernel_device(): pl.pallas_call(functools.partial(step_kernel, (n_dp, n_mp, pairs, tokens,...  40.6 us
    pallas_call x1, Pallas kernels, kernel_device(): pl.pallas_call(weights_kernel, out_shape=[jax.ShapeDtypeStruct((tokens, f...  3.39 us

profile of v9, /device:TPU:0, one launch (start us, length us, event | category | flops | bytes accessed | tf_op | source)
XLA Modules:
  0.0 44.7 jit_solution(16847207846539591610)
XLA Ops:
  0.7 40.6 %step.1 = (f32[768,768]{1,0:T(8,128)S(1)}, f32[768,768]{1,0:T(8,128)S(1)}, bf16[3,192,768]{2,1,0:T(8,128)(2,1)S(1)}, bf16[192,768]{1,0:T(8,128)(2,1)S(1)}, bf16[...) custom-call(bf16[256,768]{1,0:T(8,128)(2,1)} %text_hbm.1, ...), custom_call_target="tpu_custom_call" | custom-call | tf_op jit(solution)/shard_map/step/pallas_call | solution.py:1190
  41.3 3.4 %weights.1 = (f32[256,768]{1,0:T(8,128)}, f32[3,192,768]{2,1,0:T(8,128)}, f32[192,768]{1,0:T(8,128)}, f32[768,768]{1,0:T(8,128)}, f32[768,768]{1,0:T(8,128)}, /*...) custom-call(f32[768,768]{1,0:T(8,128)S(1)} %get-tuple-element.33.up, ...), custom_call_target="tpu_custom_call" | custom-call | tf_op jit(solution)/shard_map/weights/pallas_call | solution.py:1247
